TPU v7x, 32 devices: a whole 2x2x4 slice. The times are simulated.
32 devices in a mesh: dp: 8 (over z, y), own: 4 (over x, core).
Axes of the slice: x: 2, y: 2, z: 4, core: 2. Of those that a mesh axis runs over, the one named last changes fastest.
Arguments:
- tokens: bfloat16 [1024, 6144], P('dp', 'own'), may hold values from -6 to 6
- expert_ids: int32 [1024, 2], P('dp'), may hold values from 0 to 7, all different within a row; in each aligned block of 128 rows (0 to 127, 128 to 255, ...) at most 40 rows name the same one
- combine_weights: float32 [1024, 2], P('dp'), may hold values from 0.2 to 1
- gate_weight: bfloat16 [2, 6144, 8192], P(None, 'own', 'dp'), may hold values from -0.078125 to 0.078125
- up_weight: bfloat16 [2, 6144, 8192], P(None, 'own', 'dp'), may hold values from -0.078125 to 0.078125
- down_weight: bfloat16 [2, 8192, 6144], P(None, 'dp', 'own'), may hold values from -0.0625 to 0.0625
- out_grad: bfloat16 [1024, 6144], P('dp', 'own'), may hold values from -6 to 6
Outputs:
- mixed: bfloat16 [1024, 6144], P('dp', 'own')
- token_grad: bfloat16 [1024, 6144], P('dp', 'own')
- gate_grad_weight: float32 [2, 6144, 8192], P(None, 'own', 'dp')
- up_grad_weight: float32 [2, 6144, 8192], P(None, 'own', 'dp')
- down_grad_weight: float32 [2, 8192, 6144], P(None, 'dp', 'own')
Inputs may be any that keep to these rules, and one draw needn't show every extreme that they name: `expert_ids`: each row names 2 different experts. The 128 rows of one index of dp name each expert at most 40 times, and in every draw some expert is named exactly 40 times by the rows of one index of dp.
All inputs are finite; a program needn't handle non-finite values.
Results may differ from a plain program's by a relative error of at most 0.024.
Values may be sent and summed in bfloat16 or wider, within the bound.
No kernel may reach another device: no remote copies, remote signals or barrier semaphores. Data moves between devices by JAX's collectives and lax.ppermute only.
A program may use at most 192 MiB of HBM per device.

v0:
```python
import jax
import jax.numpy as jnp
from jax import lax
from jax.sharding import PartitionSpec as P

CAP = 40


def slot_order(shard_ids, expert):
    chosen = shard_ids == expert
    routed = jnp.any(chosen, axis=-1)
    position = jnp.cumsum(routed.astype(jnp.int32)) - 1
    slot_ids = jnp.arange(CAP, dtype=jnp.int32)
    matches = routed[None, :] & (position[None, :] == slot_ids[:, None])
    token_ids = jnp.arange(shard_ids.shape[0], dtype=jnp.int32)
    source = jnp.sum(jnp.where(matches, token_ids[None, :], 0), axis=1)
    filled = jnp.any(matches, axis=1)
    target = jnp.where(routed, position, 0)
    return (chosen, routed, source, filled, target)


def local(tokens, expert_ids, combine_weights, gate_weight, up_weight, down_weight, out_grad):
    experts = gate_weight.shape[0]
    shard_tokens = tokens.shape[0]
    tables = [slot_order(expert_ids, expert) for expert in range(experts)]
    weights = [
        jnp.sum(jnp.where(tables[expert][0], combine_weights, 0.0), axis=-1)
        for expert in range(experts)
    ]
    all_tokens = lax.all_gather(tokens, "dp", axis=0, tiled=True)
    all_ids = lax.all_gather(expert_ids, "dp", axis=0, tiled=True)
    shards = all_ids.reshape(-1, shard_tokens, expert_ids.shape[1])
    shard_base = jnp.arange(shards.shape[0], dtype=jnp.int32)[:, None] * shard_tokens
    columns = []
    for expert in range(experts):

        def one_shard(shard_ids):
            return slot_order(shard_ids, expert)

        unused_a, unused_b, source_all, filled_all, unused_c = jax.vmap(one_shard)(shards)
        source_flat = (source_all + shard_base).reshape(-1)
        filled_flat = filled_all.reshape(-1)
        columns.append(jnp.where(filled_flat[:, None], all_tokens[source_flat], 0))
    dispatched = jnp.stack(columns, axis=1)
    gate_part = jnp.einsum(
        "red,edf->ref", dispatched, gate_weight, preferred_element_type=jnp.float32
    )
    up_part = jnp.einsum("red,edf->ref", dispatched, up_weight, preferred_element_type=jnp.float32)
    gate_sum, up_sum = (
        lax.psum(gate_part.astype(jnp.bfloat16), "own").astype(jnp.float32),
        lax.psum(up_part.astype(jnp.bfloat16), "own").astype(jnp.float32),
    )
    sigma = jax.nn.sigmoid(gate_sum)
    swish = gate_sum * sigma
    hidden = (swish * up_sum).astype(jnp.bfloat16)
    expert_out = lax.psum_scatter(
        jnp.einsum("ref,efd->red", hidden, down_weight, preferred_element_type=jnp.float32).astype(
            jnp.bfloat16
        ),
        "dp",
        scatter_dimension=0,
        tiled=True,
    ).astype(jnp.float32)
    mixed = jnp.zeros(tokens.shape, jnp.float32)
    scaled_rows = []
    for expert in range(experts):
        chosen, routed, source, filled, target = tables[expert]
        token_weight = jnp.where(routed, weights[expert], 0.0)
        mixed = mixed + token_weight[:, None] * expert_out[target, expert]
        slot_weight = jnp.where(filled, weights[expert][source], 0.0)
        scaled_rows.append(
            (slot_weight[:, None] * out_grad[source].astype(jnp.float32)).astype(jnp.bfloat16)
        )
    scaled = jnp.stack(scaled_rows, axis=1)
    scaled_all = lax.all_gather(scaled, "dp", axis=0, tiled=True)
    hidden_part = jnp.einsum(
        "red,efd->ref", scaled_all, down_weight, preferred_element_type=jnp.float32
    )
    hidden_grad = lax.psum(hidden_part.astype(jnp.bfloat16), "own").astype(jnp.float32)
    gate_grad = (hidden_grad * up_sum * sigma * (1.0 + gate_sum * (1.0 - sigma))).astype(
        jnp.bfloat16
    )
    up_grad = (hidden_grad * swish).astype(jnp.bfloat16)
    first_term = jnp.einsum(
        "ref,edf->red", gate_grad, gate_weight, preferred_element_type=jnp.float32
    )
    second_term = jnp.einsum("ref,edf->red", up_grad, up_weight, preferred_element_type=jnp.float32)
    row_grad = lax.psum_scatter(
        (first_term + second_term).astype(jnp.bfloat16), "dp", scatter_dimension=0, tiled=True
    ).astype(jnp.float32)
    token_grad = jnp.zeros(tokens.shape, jnp.float32)
    for expert in range(experts):
        chosen, routed, source, filled, target = tables[expert]
        token_grad = token_grad + jnp.where(routed[:, None], row_grad[target, expert], 0.0)
    gate_grad_weight = jnp.einsum(
        "red,ref->edf", dispatched, gate_grad, preferred_element_type=jnp.float32
    )
    up_grad_weight = jnp.einsum(
        "red,ref->edf", dispatched, up_grad, preferred_element_type=jnp.float32
    )
    down_grad_weight = jnp.einsum(
        "ref,red->efd", hidden, scaled_all, preferred_element_type=jnp.float32
    )
    return (
        mixed.astype(jnp.bfloat16),
        token_grad.astype(jnp.bfloat16),
        gate_grad_weight,
        up_grad_weight,
        down_grad_weight,
    )


def solution(mesh):
    in_specs = (
        P("dp", "own"),
        P("dp", None),
        P("dp", None),
        P(None, "own", "dp"),
        P(None, "own", "dp"),
        P(None, "dp", "own"),
        P("dp", "own"),
    )
    out_specs = (
        P("dp", "own"),
        P("dp", "own"),
        P(None, "own", "dp"),
        P(None, "own", "dp"),
        P(None, "dp", "own"),
    )
    return jax.shard_map(local, mesh=mesh, in_specs=in_specs, out_specs=out_specs, check_vma=False)
```

profile of v0, /device:TPU:0, one launch (start us, length us, event | category | flops | bytes accessed | tf_op | source)
XLA Modules:
  0.0 388.9 jit_solution(4101486923503015238)
XLA Ops:
  7.2 0.7 fusion.35
  10.1 0.8 gather_fusion.4
  12.2 0.8 gather_fusion.6
  14.7 22.3 %all_gather.9 = s32[1024,2]{0,1:T(2,128)S(1)} all-gather(s32[128,2]{0,1:T(2,128)S(1)} %copy-done.8), channel_id=1, replica_groups=mesh['dp'=8,'own'=4] {'dp'}, dimensions={0}, use_global_device_ids=true | all-gather | bytes 9216 | tf_op jit(solution)/shard_map/all_gather | solution.py:31
  39.1 25.2 %all-gather.5.cloned.1.call-done = bf16[320,2,1536]{2,0,1:T(8,128)(2,1)} async-done(((bf16[40,2,1536]{2,0,1:T(8,128)(2,1)}), bf16[320,2,1536]{2,0,1:T(8,128)(2,1)}) %all-gather.5.cloned.1.call-update) | async-done | bytes 1966096 | tf_op jit(solution)/shard_map/all_gather | solution.py:75
  64.3 6.7 %fusion.13 = bf16[320,2,1024]{2,0,1:T(8,128)(2,1)} fusion(bf16[320,2,1536]{2,0,1:T(8,128)(2,1)} %all-gather.5.cloned.1.call-done, bf16[2,1024,1536]{2,1,0:T(8,128)(2,1)} %param.12), kind=kOutput, calls=%fused_computation.35 | convolution fusion | flops 2013921280 | bytes 9568256 | tf_op jit(solution)/shard_map/red,efd->ref/dot_general | solution.py:76
  70.9 55.1 %all-gather.3.cloned.1.call-done = bf16[1024,1536]{1,0:T(8,128)(2,1)} async-done(((bf16[128,1536]{1,0:T(8,128)(2,1)}), bf16[1024,1536]{1,0:T(8,128)(2,1)}) %all-gather.3.cloned.1.call-update) | async-done | bytes 3145744 | tf_op jit(solution)/shard_map/all_gather | solution.py:30
  126.0 6.6 %gather_fusion.1 = bf16[320,1536]{1,0:T(8,128)(2,1)} fusion(bf16[1024,1536]{1,0:T(8,128)(2,1)} %all-gather.3.cloned.1.call-done, s32[1024]{0:T(1024)S(1)} %pad_clamp_fusion.2), kind=kCustom, calls=%fused_computation.1 | custom fusion | bytes 1967360 | tf_op jit(solution)/shard_map/gather | solution.py:43
  132.7 2.3 bitcast_select_fusion
  134.9 2.7 gather_fusion
  137.7 1.5 bitcast_select_fusion.1
  139.2 6.5 %fusion.12 = bf16[320,2,1024]{2,0,1:T(8,128)(2,1)} fusion(bf16[2,1536,1024]{2,1,0:T(8,128)(2,1)} %param.11, bf16[320,1,1536]{2,0,1:T(8,128)(2,1)} %bitcast_select_fusion, bf16[320,1,1536]{2,0,1:T(8,128)(2,1)S(1)} %bitcast_select_fusion.1), kind=kOutput, calls=%fused_computation.34 | convolution fusion | flops 2014904320 | bytes 9568256 | tf_op jit(solution)/shard_map/red,edf->ref/dot_general | solution.py:48
  145.7 3.3 fusion.11
  149.2 80.2 %all-reduce.5.cloned.1.call-done = (bf16[320,2,1024]{2,0,1:T(8,128)(2,1)}, bf16[320,2,1024]{2,0,1:T(8,128)(2,1)}, bf16[320,2,1024]{2,0,1:T(8,128)(2,1)}) async-done(((bf16[320,2,1024]{2,0,1:T(8,128)(2,1)}, bf16[320,2,1024]{2,0,1:T(8,128)(2,1)}, bf16[320,2,1024]{2,0,1:T(8,128)(2,1)}), (bf16[320,2,1024]{2,0,1:T(8,128)(2,1)}, bf16[320,2,1024]{2,0,1:T(8,128)(2,1)}, ...) | async-done | bytes 3932176 | tf_op jit(solution)/shard_map/psum | solution.py:51
  229.4 5.9 %fusion = bf16[2,40,8,1536]{3,2,1,0:T(8,128)(2,1)S(1)} fusion(bf16[2,1024,1536]{2,1,0:T(8,128)(2,1)} %param.12, bf16[320,2,1024]{2,0,1:T(8,128)(2,1)} %get-tuple-element.15, bf16[320,2,1024]{2,0,1:T(8,128)(2,1)} %get-tuple-element.16), kind=kOutput, calls=%fused_computation.18 | convolution fusion | flops 2019491840 | bytes 10878976 | tf_op jit(solution)/shard_map/ref,efd->red/dot_general | solution.py:57
  235.3 1.5 copy.44
  236.9 6.9 %fusion.45 = f32[2,320,1536]{2,1,0:T(8,128)S(1)} fusion(bf16[2,1536,1024]{2,1,0:T(8,128)(2,1)} %param.10, bf16[320,2,1024]{2,0,1:T(8,128)(2,1)} %get-tuple-element.15, bf16[320,2,1024]{2,0,1:T(8,128)(2,1)} %get-tuple-element.17, bf16[320,2,1024]{2,0,1:T(8,128)(2,1)} %get-tuple-element.16), kind=kOutput, calls=%fused_computation.108 | convolution fusion | flops 2021785600 | bytes 14155776 | tf_op jit(solution)/shard_map/ref,edf->red/dot_general | solution.py:84
  243.8 5.4 %fusion.1 = bf16[2,40,8,1536]{3,2,1,0:T(8,128)(2,1)S(1)} fusion(f32[2,320,1536]{2,1,0:T(8,128)S(1)} %fusion.45, bf16[2,1536,1024]{2,1,0:T(8,128)(2,1)} %param.11, bf16[320,2,1024]{2,0,1:T(8,128)(2,1)S(1)} %copy-done.12, bf16[320,2,1024]{2,0,1:T(8,128)(2,1)S(1)} %copy-done.10), kind=kOutput, calls=%fused_computation.19 | convolution fusion | flops 2020474880 | bytes 14811136 | tf_op jit(solution)/shard_map/ref,edf->red/dot_general | solution.py:87
  249.2 1.6 copy.45
  250.8 10.9 %fusion.41 = f32[2,1024,1536]{2,1,0:T(8,128)} fusion(bf16[320,2,1536]{2,0,1:T(8,128)(2,1)} %all-gather.5.cloned.1.call-done, bf16[320,2,1024]{2,0,1:T(8,128)(2,1)} %get-tuple-element.15, bf16[320,2,1024]{2,0,1:T(8,128)(2,1)} %get-tuple-element.16), kind=kOutput, calls=%fused_computation.107 | convolution fusion | flops 2018508800 | bytes 17170432 | tf_op jit(solution)/shard_map/ref,red->efd/dot_general | solution.py:101
  261.8 7.3 %fusion.37 = f32[2,1536,1024]{2,1,0:T(8,128)} fusion(bf16[320,1,1536]{2,0,1:T(8,128)(2,1)S(1)} %copy-done.3, bf16[320,1,1536]{2,0,1:T(8,128)(2,1)S(1)} %bitcast_select_fusion.1, bf16[320,2,1024]{2,0,1:T(8,128)(2,1)S(1)} %copy-done.13, bf16[320,2,1024]{2,0,1:T(8,128)(2,1)S(1)} %copy-done.11), kind=kOutput, calls=%fused_computation.105 | convolution fusion | flops 2019491840 | bytes 17170432 | tf_op jit(solution)/shard_map/red,ref->edf/dot_general | solution.py:98
  269.1 7.3 %fusion.38 = f32[2,1536,1024]{2,1,0:T(8,128)} fusion(bf16[320,1,1536]{2,0,1:T(8,128)(2,1)S(1)} %copy-done.3, bf16[320,1,1536]{2,0,1:T(8,128)(2,1)S(1)} %bitcast_select_fusion.1, bf16[320,2,1024]{2,0,1:T(8,128)(2,1)S(1)} %copy-done.9, bf16[320,2,1024]{2,0,1:T(8,128)(2,1)S(1)} %copy-done.13, bf16[320,2,1024]{2,0,1:T(8,128)(2,1)S(1)} %copy-done.11), kind=kOutput, calls=%fused_computation.106 | convolution fusion | flops 2022768640 | bytes 18481152 | tf_op jit(solution)/shard_map/red,ref->edf/dot_general | solution.py:95
  276.4 27.5 %reduce-scatter.7.cloned.1.call-done = bf16[40,3072]{1,0:T(8,128)(2,1)} async-done(((bf16[320,3072]{1,0:T(8,128)(2,1)}), bf16[40,3072]{1,0:T(8,128)(2,1)}) %reduce-scatter.7.cloned.1.call-update) | async-done | bytes 245776
  303.9 1.1 reshape.443
  305.2 2.0 gather_fusion.3
  307.2 2.0 gather_fusion.2
  309.1 64.3 %reduce-scatter.9.cloned.1.call-done = bf16[40,3072]{1,0:T(8,128)(2,1)} async-done(((bf16[320,3072]{1,0:T(8,128)(2,1)}), bf16[40,3072]{1,0:T(8,128)(2,1)}) %reduce-scatter.9.cloned.1.call-update) | async-done | bytes 245776
  373.4 1.1 reshape.445
  374.7 2.0 gather_fusion.9
  376.7 2.8 gather_fusion.8
  379.5 2.0 add_convert_fusion.1
  381.5 0.9 add_convert_fusion.2
  (90 shorter events, 7.8 us)
Async XLA Ops:
  7.2 3.7 copy-start
  7.2 57.1 %all-gather.5.cloned.1.call-start = ((), (), s32[]{:S(2)}) async-start(), calls=%async_computation.3 | async-start | bytes 2211840 | tf_op jit(solution)/shard_map/all_gather | solution.py:75
  8.0 1.3 copy-start.4
  8.0 1.3 copy-start.6
  8.7 6.1 %copy-start.8 = (s32[128,2]{0,1:T(2,128)S(1)}, s32[128,2]{0,1:T(2,128)}, u32[]{:S(2)}) copy-start(s32[128,2]{0,1:T(2,128)} %param.8) | copy-start | bytes 3076
  13.9 112.1 %all-gather.3.cloned.1.call-start = ((), (), s32[]{:S(2)}) async-start(), calls=%async_computation.2 | async-start | bytes 3538944 | tf_op jit(solution)/shard_map/all_gather | solution.py:30
  14.7 214.7 %all-reduce.5.cloned.1.call-start = ((), (), s32[]{:S(2)}) async-start(), calls=%async_computation.6 | async-start | bytes 7864320 | tf_op jit(solution)/shard_map/psum | solution.py:51
  126.0 8.9 %copy-start.2 = (bf16[1024,1536]{1,0:T(8,128)(2,1)S(1)}, bf16[1024,1536]{1,0:T(8,128)(2,1)}, u32[]{:S(2)}) copy-start(bf16[1024,1536]{1,0:T(8,128)(2,1)} %all-gather.3.cloned.1.call-done) | copy-start | bytes 9437188
  137.7 8.0 %slice-start = ((s8[6291456]{0:T(1024)(128)(4,1)}), s8[4194304]{0:T(1024)(128)(4,1)S(1)}, s32[]{:S(2)}) async-start(s8[6291456]{0:T(1024)(128)(4,1)} %bitcast.58), calls=%async_computation.7 | async-start | bytes 8388608
  139.2 6.5 %copy-start.3 = (bf16[320,1,1536]{2,0,1:T(8,128)(2,1)S(1)}, bf16[320,1,1536]{2,0,1:T(8,128)(2,1)}, u32[]{:S(2)}) copy-start(bf16[320,1,1536]{2,0,1:T(8,128)(2,1)} %bitcast_select_fusion) | copy-start | bytes 2949124
  139.2 6.5 %slice-start.1 = ((s8[6291456]{0:T(1024)(128)(4,1)}), s8[2097152]{0:T(1024)(128)(4,1)S(1)}, s32[]{:S(2)}) async-start(s8[6291456]{0:T(1024)(128)(4,1)} %bitcast.58), calls=%async_computation.8 | async-start | bytes 4194304
  149.0 154.9 %reduce-scatter.7.cloned.1.call-start = ((), (), s32[]{:S(2)}) async-start(), calls=%async_computation.4 | async-start | bytes 2211840
  236.8 136.6 %reduce-scatter.9.cloned.1.call-start = ((), (), s32[]{:S(2)}) async-start(), calls=%async_computation.5 | async-start | bytes 2211840
  236.8 6.9 %copy-start.10 = (bf16[320,2,1024]{2,0,1:T(8,128)(2,1)S(1)}, bf16[320,2,1024]{2,0,1:T(8,128)(2,1)}, u32[]{:S(2)}) copy-start(bf16[320,2,1024]{2,0,1:T(8,128)(2,1)} %get-tuple-element.16) | copy-start | bytes 3932164
  236.9 6.9 %copy-start.12 = (bf16[320,2,1024]{2,0,1:T(8,128)(2,1)S(1)}, bf16[320,2,1024]{2,0,1:T(8,128)(2,1)}, u32[]{:S(2)}) copy-start(bf16[320,2,1024]{2,0,1:T(8,128)(2,1)} %get-tuple-element.17) | copy-start | bytes 3932164
  249.2 1.6 copy-start.5
  249.2 1.6 copy-start.7
  250.8 10.9 %copy-start.11 = (bf16[320,2,1024]{2,0,1:T(8,128)(2,1)S(1)}, bf16[320,2,1024]{2,0,1:T(8,128)(2,1)}, u32[]{:S(2)}) copy-start(bf16[320,2,1024]{2,0,1:T(8,128)(2,1)} %get-tuple-element.16) | copy-start | bytes 3932164
  250.8 10.9 %copy-start.13 = (bf16[320,2,1024]{2,0,1:T(8,128)(2,1)S(1)}, bf16[320,2,1024]{2,0,1:T(8,128)(2,1)}, u32[]{:S(2)}) copy-start(bf16[320,2,1024]{2,0,1:T(8,128)(2,1)} %get-tuple-element.17) | copy-start | bytes 3932164
  261.8 7.3 %copy-start.9 = (bf16[320,2,1024]{2,0,1:T(8,128)(2,1)S(1)}, bf16[320,2,1024]{2,0,1:T(8,128)(2,1)}, u32[]{:S(2)}) copy-start(bf16[320,2,1024]{2,0,1:T(8,128)(2,1)} %get-tuple-element.15) | copy-start | bytes 3932164
  376.7 5.7 %copy-start.1 = (bf16[128,1536]{1,0:T(8,128)(2,1)S(1)}, bf16[128,1536]{1,0:T(8,128)(2,1)}, u32[]{:S(2)}) copy-start(bf16[128,1536]{1,0:T(8,128)(2,1)} %param.13) | copy-start | bytes 1179652
Sparse Core Ops, SparseCore 0:
  14.1 50.1 all-gather.4
  66.4 59.5 all-gather.2
  149.1 80.2 all-reduce.4
  236.9 66.9 reduce-scatter.6
  307.6 65.7 reduce-scatter.8
where the time goes:
time: 389 us
  waiting for transfers between devices  253 us (65%)
  matrix products  60.2 us (15%)
  local copies, waits for them, and re-layouts  27.1 us (7%)
  blocking collectives  22.3 us (6%)
  between operations  14.1 us (4%)
  other arithmetic  11.9 us (3%)
    unnamed x7, waiting for transfers between devices  92.5 us
    psum x1, waiting for transfers between devices, local(): lax.psum(up_part.astype(jnp.bfloat16), 'own').astype(jnp.float32)  80.2 us
    all_gather x1, waiting for transfers between devices, local(): all_tokens = lax.all_gather(tokens, 'dp', axis=0, tiled=True)  55.1 us
    all_gather x1, waiting for transfers between devices, local(): scaled_all = lax.all_gather(scaled, 'dp', axis=0, tiled=True)  25.2 us
    all_gather x1, blocking collectives, local(): all_ids = lax.all_gather(expert_ids, 'dp', axis=0, tiled=True)  22.3 us
    dot_general x1, matrix products, local(): jnp.einsum('ref,red->efd', hidden, scaled_all, preferred_element_type=jnp...  10.9 us
    gather x2, local copies, waits for them, and re-layouts, local(): columns.append(jnp.where(filled_flat[:, None], all_tokens[source_flat], 0))  9.37 us
  transfers between devices with their start and end apart: 5, of which 5 were waited for; matrix products, arithmetic and copies ran while one was open for 14% of the time, Pallas kernels for 0%

commit v1 on v0

v1 whole, which is shorter than its diff:
```python
import functools
import jax
import jax.numpy as jnp
from jax import lax
from jax.experimental import pallas as pl
from jax.experimental.pallas import tpu as pltpu
from jax.sharding import PartitionSpec as P

CAP = 40
BF = jnp.bfloat16
F32 = jnp.float32
MIB = 1024 * 1024
ROWS = (((0,), (0,)), ((), ()))
LAST = (((1,), (1,)), ((), ()))


def shape(dims, dtype=BF):
    return jax.ShapeDtypeStruct(dims, dtype)


def whole(dims):
    return pl.BlockSpec(dims, lambda *a: (0,) * len(dims))


def cost(flops, size):
    return pl.CostEstimate(flops=int(flops), bytes_accessed=int(size), transcendentals=0)


def mm(a, b):
    return jnp.dot(a, b, preferred_element_type=F32)


def dispatch_kernel(experts, ids, cw, tokens, grad, *outs):
    rows, scaled, pick, weight = outs[:experts], outs[experts : 2 * experts], outs[-2], outs[-1]
    n = ids.shape[0]
    tri = (
        lax.broadcasted_iota(jnp.int32, (n, n), 0) >= lax.broadcasted_iota(jnp.int32, (n, n), 1)
    ).astype(BF)
    slots = lax.broadcasted_iota(jnp.int32, (n, CAP), 1)
    token = tokens[...]
    cot = grad[...].astype(F32)
    for e in range(experts):
        chosen = ids[...] == e
        routed = jnp.sum(chosen.astype(F32), axis=1, keepdims=True)
        w = jnp.sum(jnp.where(chosen, cw[...], 0.0), axis=1, keepdims=True)
        position = mm(tri, jnp.broadcast_to(routed, (n, 128)).astype(BF))[:, :CAP]
        match = (position.astype(jnp.int32) - 1 == slots) & (routed > 0.0)
        match = jnp.where(match, 1.0, 0.0).astype(BF)
        pick[e] = match
        weight[e] = jnp.broadcast_to(w, (n, 128))
        rows[e][...] = lax.dot_general(match, token, ROWS, preferred_element_type=F32).astype(BF)
        scaled[e][...] = lax.dot_general(
            match, (w * cot).astype(BF), ROWS, preferred_element_type=F32
        ).astype(BF)


def dispatch(ids, cw, tokens, grad, experts):
    n, d = tokens.shape
    outs = [shape((CAP, d))] * (2 * experts) + [
        shape((experts, n, CAP)),
        shape((experts, n, 128), F32),
    ]
    res = pl.pallas_call(
        functools.partial(dispatch_kernel, experts),
        out_shape=outs,
        compiler_params=pltpu.CompilerParams(vmem_limit_bytes=16 * MIB),
        cost_estimate=cost(4 * experts * CAP * n * d, 8 * n * d),
        name="dispatch",
    )(ids, cw, tokens, grad)
    return res[:experts], res[experts : 2 * experts], res[-2], res[-1]


def project_kernel(parts, transposed, core, first, second, *refs):
    weights, keep, send = refs[:parts], refs[parts], refs[parts + 1]
    j, half = pl.program_id(0), pl.num_programs(0) // 2
    h = first.shape[0]

    def store(out):
        for p in range(parts):
            w = weights[p][0]
            for i, ref in enumerate((first, second)):
                if transposed:
                    val = lax.dot_general(ref[...], w, LAST, preferred_element_type=F32)
                else:
                    val = mm(ref[...], w)
                out[p, i * h : (i + 1) * h, :] = val.astype(BF)

    @pl.when(j < half)
    def _():
        store(keep)

    @pl.when(j >= half)
    def _():
        store(send)


def project(core, first, second, weights, expert, transposed):
    h, d = first.shape
    f = weights[0].shape[1] if transposed else weights[0].shape[2]
    fb = min(256, f // 2)
    n = f // fb
    parts = len(weights)

    def block(j, c):
        return (j + c[0] * (n // 2)) % n

    if transposed:
        wspec = pl.BlockSpec((1, fb, d), lambda j, c: (expert, block(j, c), 0))
    else:
        wspec = pl.BlockSpec((1, d, fb), lambda j, c: (expert, 0, block(j, c)))
    grid_spec = pltpu.PrefetchScalarGridSpec(
        num_scalar_prefetch=1,
        grid=(n,),
        in_specs=[whole((h, d)), whole((h, d))] + [wspec] * parts,
        out_specs=[
            pl.BlockSpec((parts, 2 * h, fb), lambda j, c: (0, 0, jnp.minimum(j, n // 2 - 1))),
            pl.BlockSpec((parts, 2 * h, fb), lambda j, c: (0, 0, jnp.maximum(j - n // 2, 0))),
        ],
    )
    return pl.pallas_call(
        functools.partial(project_kernel, parts, transposed),
        grid_spec=grid_spec,
        out_shape=[shape((parts, 2 * h, f // 2))] * 2,
        compiler_params=pltpu.CompilerParams(vmem_limit_bytes=24 * MIB),
        cost_estimate=cost(4 * h * d * f * parts, 2 * d * f * parts + 4 * h * d),
        name="hidden_grad_part" if transposed else "gate_up_part",
    )(core, first, second, *weights)


def back_kernel(parts, transposed, core, *refs):
    acts, weights, keep, send = (
        refs[: 2 * parts],
        refs[2 * parts : 4 * parts],
        refs[4 * parts],
        refs[4 * parts + 1],
    )
    total = None
    for a, w in zip(acts, weights):
        if transposed:
            val = lax.dot_general(a[...], w[0], LAST, preferred_element_type=F32)
        else:
            val = mm(a[...], w[0])
        total = val if total is None else total + val
    h = keep.shape[0]
    keep[...] = total[:h].astype(BF)
    send[...] = total[h:].astype(BF)


def back(core, acts, weights, expert, transposed):
    r, half = acts[0].shape
    d = weights[0].shape[1] if transposed else weights[0].shape[2]
    db = 256 if d % 256 == 0 else 128
    parts = len(weights)
    wspecs, warrs = [], []
    for p in range(parts):
        for b in range(2):
            if transposed:
                wspecs.append(
                    pl.BlockSpec((1, db, half), lambda j, c, b=b: (expert, j, (c[0] + b) % 2))
                )
            else:
                wspecs.append(
                    pl.BlockSpec((1, half, db), lambda j, c, b=b: (expert, (c[0] + b) % 2, j))
                )
            warrs.append(weights[p])
    grid_spec = pltpu.PrefetchScalarGridSpec(
        num_scalar_prefetch=1,
        grid=(d // db,),
        in_specs=[whole((r, half))] * (2 * parts) + wspecs,
        out_specs=[pl.BlockSpec((r // 2, db), lambda j, c: (0, j))] * 2,
    )
    return pl.pallas_call(
        functools.partial(back_kernel, parts, transposed),
        grid_spec=grid_spec,
        out_shape=[shape((r // 2, d))] * 2,
        compiler_params=pltpu.CompilerParams(vmem_limit_bytes=24 * MIB),
        cost_estimate=cost(4 * r * d * half * parts, 4 * d * half * parts + 2 * r * d),
        name="row_grad_part" if transposed else "expert_part",
    )(core, *acts, *warrs)


def add_kernel(keep, got, out):
    out[...] = (keep[...].astype(F32) + got[...].astype(F32)).astype(BF)


def add(keep, got):
    return pl.pallas_call(
        add_kernel,
        out_shape=shape(keep.shape),
        compiler_params=pltpu.CompilerParams(vmem_limit_bytes=16 * MIB),
        cost_estimate=cost(keep.size, 6 * keep.size),
        name="add",
    )(keep, got)


def halve_kernel(keep, got, out_keep, out_send):
    h = out_keep.shape[0]
    total = (keep[...].astype(F32) + got[...].astype(F32)).astype(BF)
    out_keep[...] = total[:h]
    out_send[...] = total[h:]


def halve(keep, got):
    r, d = keep.shape
    return pl.pallas_call(
        halve_kernel,
        out_shape=[shape((r // 2, d))] * 2,
        compiler_params=pltpu.CompilerParams(vmem_limit_bytes=16 * MIB),
        cost_estimate=cost(keep.size, 6 * keep.size),
        name="halve",
    )(keep, got)


def join_kernel(a, b, out):
    n = a.shape[0]
    out[:n] = a[...]
    out[n:] = b[...]


def join(a, b):
    return jnp.concatenate([a, b], axis=0)


def hidden_kernel(n, keep, got, *refs):
    others, sums, hidden = refs[:n], refs[n], refs[n + 1]
    total = keep[...].astype(F32) + got[...].astype(F32)
    for ref in others:
        total = total + ref[...].astype(F32)
    sums[...] = total
    gate, up = total[0], total[1]
    hidden[...] = (gate * jax.nn.sigmoid(gate) * up).astype(BF)


def hidden_of(keep, got, others):
    _, r, half = keep.shape
    blk = min(r, 320)
    spec = pl.BlockSpec((2, blk, half), lambda i: (0, i, 0))
    return pl.pallas_call(
        functools.partial(hidden_kernel, len(others)),
        grid=(r // blk,),
        in_specs=[spec] * (2 + len(others)),
        out_specs=[spec, pl.BlockSpec((blk, half), lambda i: (i, 0))],
        out_shape=[shape((2, r, half), F32), shape((r, half))],
        compiler_params=pltpu.CompilerParams(vmem_limit_bytes=24 * MIB),
        cost_estimate=cost(20 * r * half, 20 * r * half),
        name="hidden",
    )(keep, got, *others)


def grads_kernel(n, sums, keep, got, *refs):
    others, out = refs[:n], refs[n]
    total = keep[0].astype(F32) + got[0].astype(F32)
    for ref in others:
        total = total + ref[0].astype(F32)
    gate, up = sums[0], sums[1]
    sig = jax.nn.sigmoid(gate)
    out[0] = (total * up * sig * (1.0 + gate * (1.0 - sig))).astype(BF)
    out[1] = (total * gate * sig).astype(BF)


def grads_of(sums, keep, got, others):
    _, r, half = sums.shape
    blk = min(r, 320)
    one = pl.BlockSpec((1, blk, half), lambda i: (0, i, 0))
    two = pl.BlockSpec((2, blk, half), lambda i: (0, i, 0))
    return pl.pallas_call(
        functools.partial(grads_kernel, len(others)),
        grid=(r // blk,),
        in_specs=[two] + [one] * (2 + len(others)),
        out_specs=two,
        out_shape=shape((2, r, half)),
        compiler_params=pltpu.CompilerParams(vmem_limit_bytes=24 * MIB),
        cost_estimate=cost(20 * r * half, 20 * r * half),
        name="gate_up_grads",
    )(sums, keep, got, *others)


def weight_kernel(pairs, has_prev, by_columns, core, *refs):
    refs = list(refs)
    first, second = refs[0], refs[1]
    acts = refs[2 : 2 + 2 * pairs]
    outs = refs[len(refs) - pairs :]
    b = pl.program_id(0)
    h = first.shape[0]
    for p in range(pairs):
        for i in range(2):

            @pl.when(b == i)
            def _():
                act = acts[2 * p + i]
                if by_columns:
                    val = lax.dot_general(first[...], act[:h], ROWS, preferred_element_type=F32)
                    val += lax.dot_general(second[...], act[h:], ROWS, preferred_element_type=F32)
                else:
                    val = lax.dot_general(act[:h], first[...], ROWS, preferred_element_type=F32)
                    val += lax.dot_general(act[h:], second[...], ROWS, preferred_element_type=F32)
                outs[p][0] = val


def weight_grads(core, first, second, acts, expert, experts, prev, by_columns):
    h, d = first.shape
    r, half = acts[0].shape
    pairs = len(acts) // 2
    db = 512 if d % 512 == 0 else 128
    n = d // db
    if by_columns:
        out = shape((experts, d, 2 * half), F32)
        ospec = pl.BlockSpec((1, db, half), lambda b, j, c: (expert, j, (c[0] + b) % 2))
    else:
        out = shape((experts, 2 * half, d), F32)
        ospec = pl.BlockSpec((1, half, db), lambda b, j, c: (expert, (c[0] + b) % 2, j))
    rspec = pl.BlockSpec((h, db), lambda b, j, c: (0, j))
    aspecs = [whole((r, half))] * (2 * pairs)
    extra = [] if prev is None else list(prev)
    grid_spec = pltpu.PrefetchScalarGridSpec(
        num_scalar_prefetch=1,
        grid=(2, n),
        in_specs=[rspec, rspec] + aspecs + [pl.BlockSpec(memory_space=pl.ANY)] * len(extra),
        out_specs=[ospec] * pairs,
    )
    aliases = {3 + 2 * pairs + p: p for p in range(len(extra))}
    return pl.pallas_call(
        functools.partial(weight_kernel, pairs, bool(extra), by_columns),
        grid_spec=grid_spec,
        out_shape=[out] * pairs,
        input_output_aliases=aliases,
        compiler_params=pltpu.CompilerParams(vmem_limit_bytes=24 * MIB),
        cost_estimate=cost(4 * r * d * half * pairs, 8 * d * half * pairs),
        name="gate_up_weight_grad" if by_columns else "down_weight_grad",
    )(core, first, second, *acts, *extra)


def combine_kernel(experts, weighted, pick, weight, *refs):
    keeps, gots, out = refs[:experts], refs[experts : 2 * experts], refs[-1]
    total = 0.0
    for e in range(experts):
        val = (keeps[e][...].astype(F32) + gots[e][...].astype(F32)).astype(BF)
        val = mm(pick[e], val)
        if weighted:
            val = weight[e][:, :1] * val
        total = total + val
    out[...] = total.astype(BF)


def combine(pick, weight, keeps, gots, weighted):
    experts, n, _ = pick.shape
    d = keeps[0].shape[1]
    return pl.pallas_call(
        functools.partial(combine_kernel, experts, weighted),
        out_shape=shape((n, d)),
        compiler_params=pltpu.CompilerParams(vmem_limit_bytes=16 * MIB),
        cost_estimate=cost(4 * n * CAP * d, 4 * n * d),
        name="combine",
    )(pick, weight, *keeps, *gots)


def build(n_dp, n_own):
    bits = n_dp.bit_length() - 1
    far_first = list(range(bits - 1, -1, -1))

    def swap(x, bit):
        return lax.ppermute(x, "dp", [(i, i ^ (1 << bit)) for i in range(n_dp)])

    def swap_core(x):
        return lax.ppermute(x, "own", [(i, i ^ 1) for i in range(n_own)])

    def shift_x(x):
        return [
            lax.ppermute(x, "own", [(i, (i + 2 * k) % n_own) for i in range(n_own)])
            for k in range(1, n_own // 2)
        ]

    def gather(x):
        for bit in far_first[:-1]:
            x = join(x, swap(x, bit))
        return x, swap(x, far_first[-1])

    def scatter(keep, send):
        for bit in far_first[:0:-1]:
            keep, send = halve(keep, swap(send, bit))
        return keep, swap(send, far_first[0])

    def local(tokens, expert_ids, combine_weights, gate_weight, up_weight, down_weight, out_grad):
        experts = gate_weight.shape[0]
        core = (lax.axis_index("own") % 2).astype(jnp.int32).reshape(1)
        rows, scaled, pick, weight = dispatch(
            expert_ids, combine_weights, tokens, out_grad, experts
        )
        rows = [gather(x) for x in rows]
        scaled = [gather(x) for x in scaled]
        sums, hiddens, outs = [], [], []
        for e in range(experts):
            keep, send = project(core, *rows[e], [gate_weight, up_weight], e, False)
            got = swap_core(send)
            total, mine = hidden_of(keep, got, shift_x(add(keep, got)))
            sums.append(total)
            hiddens.append((mine, swap_core(mine)))
            outs.append(scatter(*back(core, hiddens[e], [down_weight], e, False)))
        down_grad = None
        gate_up = None
        row_outs = []
        for e in range(experts):
            keep, send = project(core, *scaled[e], [down_weight], e, True)
            got = swap_core(send)
            mine = grads_of(sums[e], keep, got, shift_x(add(keep, got)))
            other = swap_core(mine)
            acts = (mine[0], other[0], mine[1], other[1])
            row_outs.append(scatter(*back(core, acts, [gate_weight, up_weight], e, True)))
            down_grad = weight_grads(
                core, *scaled[e], hiddens[e], e, experts, down_grad, False
            )
            gate_up = weight_grads(core, *rows[e], acts, e, experts, gate_up, True)
        mixed = combine(pick, weight, [o[0] for o in outs], [o[1] for o in outs], True)
        token_grad = combine(
            pick, weight, [o[0] for o in row_outs], [o[1] for o in row_outs], False
        )
        return mixed, token_grad, gate_up[0], gate_up[1], down_grad[0]

    return local


def solution(mesh):
    local = build(mesh.shape["dp"], mesh.shape["own"])
    in_specs = (
        P("dp", "own"),
        P("dp", None),
        P("dp", None),
        P(None, "own", "dp"),
        P(None, "own", "dp"),
        P(None, "dp", "own"),
        P("dp", "own"),
    )
    out_specs = (
        P("dp", "own"),
        P("dp", "own"),
        P(None, "own", "dp"),
        P(None, "own", "dp"),
        P(None, "dp", "own"),
    )
    return jax.shard_map(local, mesh=mesh, in_specs=in_specs, out_specs=out_specs, check_vma=False)
```

time: 389 us -> 204 us (0.52)
  waiting for transfers between devices: 253 us -> 86.9 us
  matrix products: 60.2 us -> 0 us
  Pallas kernels: 0 us -> 58.8 us
  starting transfers between devices: 0.38 us -> 36.1 us
  blocking collectives: 22.3 us -> 0 us
  between operations: 14.1 us -> 1.04 us
  local copies, waits for them, and re-layouts: 27.1 us -> 17 us
  other arithmetic: 11.9 us -> 3.8 us
    unnamed x7 -> x0, waiting for transfers between devices: 92.5 us -> none
    ppermute x0 -> x36, waiting for transfers between devices: none -> 86.9 us  [the longest x24 61.7 us: swap(): return lax.ppermute(x, 'dp', [(i, i ^ 1 << bit) for i in range(n_dp)])]
    all_gather x2 -> x0, waiting for transfers between devices: 80.3 us -> none  [the longest x1 55.1 us: local(): all_tokens = lax.all_gather(tokens, 'dp', axis=0, tiled=True)]
    psum x1 -> x0, waiting for transfers between devices: 80.2 us -> none  [local(): lax.psum(up_part.astype(jnp.bfloat16), 'own').astype(jnp.float32)]
    dot_general x9 -> x0, matrix products: 60.2 us -> none  [the longest x1 10.9 us: local(): jnp.einsum('ref,red->efd', hidden, scaled_all, preferred_element_type=jnp...]
    pallas_call x0 -> x31, Pallas kernels: none -> 58.8 us  [the longest x4 25.9 us: weight_grads(): pl.pallas_call(functools.partial(weight_kernel, pairs, bool(extra), by_co...]
    ppermute x0 -> x36, starting transfers between devices: none -> 36.1 us  [the longest x24 29.5 us: swap(): return lax.ppermute(x, 'dp', [(i, i ^ 1 << bit) for i in range(n_dp)])]
    all_gather x1 -> x0, blocking collectives: 22.3 us -> none  [local(): all_ids = lax.all_gather(expert_ids, 'dp', axis=0, tiled=True)]
  transfers between devices with their start and end apart: 5 -> 36, of which waited for: 5 -> 19; matrix products, arithmetic and copies ran while one was open for 14% -> 4% of each run, Pallas kernels for 0% -> 28%
where the time goes in v1:
time: 204 us
  waiting for transfers between devices  86.9 us (43%)
  Pallas kernels  58.8 us (29%)
  starting transfers between devices  36.1 us (18%)
  local copies, waits for them, and re-layouts  17 us (8%)
  other arithmetic  3.8 us (2%)
    ppermute x24, waiting for transfers between devices, swap(): return lax.ppermute(x, 'dp', [(i, i ^ 1 << bit) for i in range(n_dp)])  61.7 us
    ppermute x24, starting transfers between devices, swap(): return lax.ppermute(x, 'dp', [(i, i ^ 1 << bit) for i in range(n_dp)])  29.5 us
    pallas_call x4, Pallas kernels, weight_grads(): pl.pallas_call(functools.partial(weight_kernel, pairs, bool(extra), by_co...  25.9 us
    ppermute x4, waiting for transfers between devices, shift_x(): lax.ppermute(x, 'own', [(i, (i + 2 * k) % n_own) for i in range(n_own)])  25.1 us
    unnamed x30, local copies, waits for them, and re-layouts  16.7 us
    pallas_call x4, Pallas kernels, project(): pl.pallas_call(functools.partial(project_kernel, parts, transposed), grid...  13.4 us
    pallas_call x4, Pallas kernels, back(): pl.pallas_call(functools.partial(back_kernel, parts, transposed), grid_sp...  13.3 us
    ppermute x4, starting transfers between devices, shift_x(): lax.ppermute(x, 'own', [(i, (i + 2 * k) % n_own) for i in range(n_own)])  5.58 us
  transfers between devices with their start and end apart: 36, of which 19 were waited for; matrix products, arithmetic and copies ran while one was open for 4% of the time, Pallas kernels for 28%

profile of v1, /device:TPU:0, one launch (start us, length us, event | category | flops | bytes accessed | tf_op | source)
XLA Modules:
  0.0 203.6 jit_solution(2023817376178470277)
XLA Ops:
  5.8 4.0 %collective-permute-start = (bf16[40,1536]{1,0:T(8,128)(2,1)}, bf16[40,1536]{1,0:T(8,128)(2,1)}, u32[]{:S(2)}, u32[]{:S(2)}) collective-permute-start(bf16[40,1536]{1,0:T(8,128)(2,1)} %get-tuple-element.53), channel_id=1, source_target_pairs={{0,16},{4,20},{8,24},{12,28},{16,0},{20,4},{24,8},{28,12},{1,17},{... | collective-permute-start | bytes 368648 | tf_op jit(solution)/shard_map/ppermute | solution.py:362
  9.8 2.9 %collective-permute-start.18 = (bf16[40,1536]{1,0:T(8,128)(2,1)S(1)}, bf16[40,1536]{1,0:T(8,128)(2,1)}, u32[]{:S(2)}, u32[]{:S(2)}) collective-permute-start(bf16[40,1536]{1,0:T(8,128)(2,1)S(1)} %get-tuple-element.74), channel_id=1, source_target_pairs={{0,16},{4,20},{8,24},{12,28},{16,0},{20,4},{24,8},{28,12},{1,17},{... | collective-permute-start | bytes 368648 | tf_op jit(solution)/shard_map/ppermute | solution.py:362
  13.8 11.0 %collective-permute-done = bf16[40,1536]{1,0:T(8,128)(2,1)} collective-permute-done((bf16[40,1536]{1,0:T(8,128)(2,1)}, bf16[40,1536]{1,0:T(8,128)(2,1)}, u32[]{:S(2)}, u32[]{:S(2)}) %collective-permute-start) | collective-permute-done | bytes 122912 | tf_op jit(solution)/shard_map/ppermute | solution.py:362
  38.9 3.5 %collective-permute-done.9 = bf16[80,1536]{1,0:T(8,128)(2,1)S(1)} collective-permute-done((bf16[80,1536]{1,0:T(8,128)(2,1)S(1)}, bf16[80,1536]{1,0:T(8,128)(2,1)S(1)}, u32[]{:S(2)}, u32[]{:S(2)}) %collective-permute-start.9) | collective-permute-done | bytes 245792 | tf_op jit(solution)/shard_map/ppermute | solution.py:362
  45.0 2.7 %collective-permute-done.19 = bf16[80,1536]{1,0:T(8,128)(2,1)S(1)} collective-permute-done((bf16[80,1536]{1,0:T(8,128)(2,1)S(1)}, bf16[80,1536]{1,0:T(8,128)(2,1)S(1)}, u32[]{:S(2)}, u32[]{:S(2)}) %collective-permute-start.19) | collective-permute-done | bytes 245792 | tf_op jit(solution)/shard_map/ppermute | solution.py:362
  49.3 2.0 collective-permute-done.2.second.refs_1_
  51.3 2.8 %copy-done = bf16[2,1536,1024]{2,1,0:T(8,128)(2,1)S(1)} copy-done((bf16[2,1536,1024]{2,1,0:T(8,128)(2,1)S(1)}, bf16[2,1536,1024]{2,1,0:T(8,128)(2,1)}, u32[]{:S(2)}) %copy-start) | copy-done | bytes 6291480
  54.1 2.8 %copy-done.1 = bf16[2,1536,1024]{2,1,0:T(8,128)(2,1)S(1)} copy-done((bf16[2,1536,1024]{2,1,0:T(8,128)(2,1)S(1)}, bf16[2,1536,1024]{2,1,0:T(8,128)(2,1)}, u32[]{:S(2)}) %copy-start.1) | copy-done | bytes 6291480
  56.9 3.9 %gate_up_part.2 = (bf16[2,320,512]{2,1,0:T(8,128)(2,1)S(1)}, bf16[2,320,512]{2,1,0:T(8,128)(2,1)S(1)}) custom-call(s32[1]{0:T(128)} %bitcast.core, bf16[160,1536]{1,0:T(8,128)(2,1)S(1)} %constant_dynamic-update-slice_fusion.first.refs_0_, bf16[160,1536]{1,0:T(8,128)(2,1)S(1)} %collective-permute-done.2.second.refs_1_, bf16[2,1536,1024]{2,1,0:T(8,128)(2,1)S(1)} %copy-done, ...), custom_call_target="tpu_custom_call" | custom-call | flops 2013265920 | bytes 7274496 | tf_op jit(solution)/shard_map/gate_up_part/pallas_call | solution.py:120
  61.8 2.8 %copy-done.2 = bf16[2,1536,1024]{2,1,0:T(8,128)(2,1)S(1)} copy-done((bf16[2,1536,1024]{2,1,0:T(8,128)(2,1)S(1)}, bf16[2,1536,1024]{2,1,0:T(8,128)(2,1)}, u32[]{:S(2)}) %copy-start.2) | copy-done | bytes 6291480
  64.6 3.9 %gate_up_part.3 = (bf16[2,320,512]{2,1,0:T(8,128)(2,1)S(1)}, bf16[2,320,512]{2,1,0:T(8,128)(2,1)S(1)}) custom-call(s32[1]{0:T(128)} %bitcast.core, bf16[160,1536]{1,0:T(8,128)(2,1)S(1)} %constant_dynamic-update-slice_fusion.3.first.refs_0_, bf16[160,1536]{1,0:T(8,128)(2,1)S(1)} %collective-permute-done.10.second.refs_1_, ...), custom_call_target="tpu_custom_call" | custom-call | flops 2013265920 | bytes 7274496 | tf_op jit(solution)/shard_map/gate_up_part/pallas_call | solution.py:120
  72.1 2.8 %hidden_grad_part.2 = (bf16[1,320,512]{2,1,0:T(8,128)(2,1)S(1)}, bf16[1,320,512]{2,1,0:T(8,128)(2,1)S(1)}) custom-call(s32[1]{0:T(128)} %bitcast.core, bf16[160,1536]{1,0:T(8,128)(2,1)S(1)} %constant_dynamic-update-slice_fusion.6.first.refs_0_, bf16[160,1536]{1,0:T(8,128)(2,1)S(1)} %collective-permute-done.20.second.refs_1_, bf16[2,1024,1536]{2,1,0:T(8,128)(2,1)S(1)} %bitcast.18), custom_call_target="tpu_custom_call" | custom-call | flops 1006632960 | bytes 4128768 | tf_op jit(solution)/shard_map/hidden_grad_part/pallas_call | solution.py:120
  76.0 6.3 %collective-permute-done.28.second.refs_1_ = bf16[160,1536]{1,0:T(8,128)(2,1)S(1)} collective-permute-done((bf16[160,1536]{1,0:T(8,128)(2,1)S(1)}, bf16[160,1536]{1,0:T(8,128)(2,1)S(1)}, u32[]{:S(2)}, u32[]{:S(2)}) %collective-permute-start.28) | collective-permute-done | bytes 491552 | tf_op jit(solution)/shard_map/ppermute | solution.py:362
  82.3 2.8 %hidden_grad_part.3 = (bf16[1,320,512]{2,1,0:T(8,128)(2,1)S(1)}, bf16[1,320,512]{2,1,0:T(8,128)(2,1)S(1)}) custom-call(s32[1]{0:T(128)} %bitcast.core, bf16[160,1536]{1,0:T(8,128)(2,1)S(1)} %constant_dynamic-update-slice_fusion.9.first.refs_0_, bf16[160,1536]{1,0:T(8,128)(2,1)S(1)} %collective-permute-done.28.second.refs_1_, bf16[2,1024,1536]{2,1,0:T(8,128)(2,1)S(1)} %bitcast.18), custom_call_target="tpu_custom_call" | custom-call | flops 1006632960 | bytes 4128768 | tf_op jit(solution)/shard_map/hidden_grad_part/pallas_call | solution.py:120
  89.0 20.2 %collective-permute-done.22.refs_0_ = bf16[1,320,512]{2,1,0:T(8,128)(2,1)S(1)} collective-permute-done((bf16[1,320,512]{2,1,0:T(8,128)(2,1)S(1)}, bf16[1,320,512]{2,1,0:T(8,128)(2,1)S(1)}, u32[]{:S(2)}, u32[]{:S(2)}) %collective-permute-start.22) | collective-permute-done | bytes 327712 | tf_op jit(solution)/shard_map/ppermute | solution.py:369
  110.6 4.9 %collective-permute-done.30.refs_0_ = bf16[1,320,512]{2,1,0:T(8,128)(2,1)S(1)} collective-permute-done((bf16[1,320,512]{2,1,0:T(8,128)(2,1)S(1)}, bf16[1,320,512]{2,1,0:T(8,128)(2,1)S(1)}, u32[]{:S(2)}, u32[]{:S(2)}) %collective-permute-start.30) | collective-permute-done | bytes 327712 | tf_op jit(solution)/shard_map/ppermute | solution.py:369
  116.1 2.5 %expert_part.2 = (bf16[160,1536]{1,0:T(8,128)(2,1)S(1)}, bf16[160,1536]{1,0:T(8,128)(2,1)S(1)}) custom-call(s32[1]{0:T(128)} %bitcast.core, bf16[320,512]{1,0:T(8,128)(2,1)S(1)} %get-tuple-element.56.refs_0_.refs_2_, bf16[320,512]{1,0:T(8,128)(2,1)S(1)} %collective-permute-done.5.refs_1_.refs_3_, bf16[2,1024,1536]{2,1,0:T(8,128)(2,1)S(1)} %bitcast.18, ...), custom_call_target="tpu_custom_call" | custom-call | flops 1006632960 | bytes 4128768 | tf_op jit(solution)/shard_map/expert_part/pallas_call | solution.py:172
  119.0 2.5 %expert_part.3 = (bf16[160,1536]{1,0:T(8,128)(2,1)S(1)}, bf16[160,1536]{1,0:T(8,128)(2,1)S(1)}) custom-call(s32[1]{0:T(128)} %bitcast.core, bf16[320,512]{1,0:T(8,128)(2,1)S(1)} %get-tuple-element.65.refs_0_.refs_2_, bf16[320,512]{1,0:T(8,128)(2,1)S(1)} %collective-permute-done.13.refs_1_.refs_3_, bf16[2,1024,1536]{2,1,0:T(8,128)(2,1)S(1)} %bitcast.18, ...), custom_call_target="tpu_custom_call" | custom-call | flops 1006632960 | bytes 4128768 | tf_op jit(solution)/shard_map/expert_part/pallas_call | solution.py:172
  123.4 4.1 %row_grad_part.2 = (bf16[160,1536]{1,0:T(8,128)(2,1)S(1)}, bf16[160,1536]{1,0:T(8,128)(2,1)S(1)}) custom-call(s32[1]{0:T(128)} %bitcast.core, bf16[320,512]{1,0:T(8,128)(2,1)S(1)} %get-tuple-element.104.refs_0_.refs_2_, bf16[320,512]{1,0:T(8,128)(2,1)S(1)} %get-tuple-element.102.refs_1_.refs_3_, bf16[320,512]{1,0:T(8,128)(2,1)S(1)} %get-tuple-element.103.refs_2_.refs_4_, ...), custom_call_target="tpu_custom_call" | custom-call | flops 2013265920 | bytes 7274496 | tf_op jit(solution)/shard_map/row_grad_part/pallas_call | solution.py:172
  128.0 4.1 %row_grad_part.3 = (bf16[160,1536]{1,0:T(8,128)(2,1)S(1)}, bf16[160,1536]{1,0:T(8,128)(2,1)S(1)}) custom-call(s32[1]{0:T(128)} %bitcast.core, bf16[320,512]{1,0:T(8,128)(2,1)S(1)} %get-tuple-element.100.refs_0_.refs_2_, bf16[320,512]{1,0:T(8,128)(2,1)S(1)} %get-tuple-element.98.refs_1_.refs_3_, bf16[320,512]{1,0:T(8,128)(2,1)S(1)} %get-tuple-element.99.refs_2_.refs_4_, ...), custom_call_target="tpu_custom_call" | custom-call | flops 2013265920 | bytes 7274496 | tf_op jit(solution)/shard_map/row_grad_part/pallas_call | solution.py:172
  133.8 5.0 %down_weight_grad.2.refs_4_ = f32[2,1024,1536]{2,1,0:T(8,128)} custom-call(s32[1]{0:T(128)} %bitcast.core, bf16[160,1536]{1,0:T(8,128)(2,1)S(1)} %constant_dynamic-update-slice_fusion.6.first.refs_0_, bf16[160,1536]{1,0:T(8,128)(2,1)S(1)} %collective-permute-done.20.second.refs_1_, bf16[320,512]{1,0:T(8,128)(2,1)S(1)} %get-tuple-element.56.refs_0_.refs_2_, ...), custom_call_target="tpu_custom_call" | custom-call | flops 1006632960 | bytes 6291456 | tf_op jit(solution)/shard_map/down_weight_grad/pallas_call | solution.py:322
  139.6 3.6 %collective-permute-done.14.got = bf16[160,1536]{1,0:T(8,128)(2,1)S(1)} collective-permute-done((bf16[160,1536]{1,0:T(8,128)(2,1)S(1)}, bf16[160,1536]{1,0:T(8,128)(2,1)S(1)}, u32[]{:S(2)}, u32[]{:S(2)}) %collective-permute-start.14) | collective-permute-done | bytes 491552 | tf_op jit(solution)/shard_map/ppermute | solution.py:362
  144.0 9.8 %collective-permute-done.24.got = bf16[160,1536]{1,0:T(8,128)(2,1)S(1)} collective-permute-done((bf16[160,1536]{1,0:T(8,128)(2,1)S(1)}, bf16[160,1536]{1,0:T(8,128)(2,1)S(1)}, u32[]{:S(2)}, u32[]{:S(2)}) %collective-permute-start.24) | collective-permute-done | bytes 491552 | tf_op jit(solution)/shard_map/ppermute | solution.py:362
  154.5 9.4 %collective-permute-done.32.got = bf16[160,1536]{1,0:T(8,128)(2,1)S(1)} collective-permute-done((bf16[160,1536]{1,0:T(8,128)(2,1)S(1)}, bf16[160,1536]{1,0:T(8,128)(2,1)S(1)}, u32[]{:S(2)}, u32[]{:S(2)}) %collective-permute-start.32) | collective-permute-done | bytes 491552 | tf_op jit(solution)/shard_map/ppermute | solution.py:362
  164.7 5.0 %down_weight_grad.3 = f32[2,1024,1536]{2,1,0:T(8,128)} custom-call(s32[1]{0:T(128)} %bitcast.core, bf16[160,1536]{1,0:T(8,128)(2,1)S(1)} %constant_dynamic-update-slice_fusion.9.first.refs_0_, bf16[160,1536]{1,0:T(8,128)(2,1)S(1)} %collective-permute-done.28.second.refs_1_, ...), custom_call_target="tpu_custom_call", output_to_operand_aliasing={{}: (5, {})} | custom-call | flops 1006632960 | bytes 6291456 | tf_op jit(solution)/shard_map/down_weight_grad/pallas_call | solution.py:322
  169.7 7.9 %gate_up_weight_grad.2 = (f32[2,1536,1024]{2,1,0:T(8,128)}, f32[2,1536,1024]{2,1,0:T(8,128)}) custom-call(s32[1]{0:T(128)} %bitcast.core, bf16[160,1536]{1,0:T(8,128)(2,1)S(1)} %constant_dynamic-update-slice_fusion.first.refs_0_, bf16[160,1536]{1,0:T(8,128)(2,1)S(1)} %collective-permute-done.2.second.refs_1_, ...), custom_call_target="tpu_custom_call" | custom-call | flops 2013265920 | bytes 12582912 | tf_op jit(solution)/shard_map/gate_up_weight_grad/pallas_call | solution.py:322
  177.7 3.4 %collective-permute-start.16 = (bf16[40,1536]{1,0:T(8,128)(2,1)S(1)}, bf16[40,1536]{1,0:T(8,128)(2,1)S(1)}, u32[]{:S(2)}, u32[]{:S(2)}) collective-permute-start(bf16[40,1536]{1,0:T(8,128)(2,1)S(1)} %get-tuple-element.71), channel_id=1, source_target_pairs={{0,16},{4,20},{8,24},{12,28},{16,0},{20,4},{24,8},{28,12},{1,17},{... | collective-permute-start | bytes 368648 | tf_op jit(solution)/shard_map/ppermute | solution.py:362
  181.3 3.0 %collective-permute-start.34 = (bf16[40,1536]{1,0:T(8,128)(2,1)S(1)}, bf16[40,1536]{1,0:T(8,128)(2,1)S(1)}, u32[]{:S(2)}, u32[]{:S(2)}) collective-permute-start(bf16[40,1536]{1,0:T(8,128)(2,1)S(1)} %get-tuple-element.91), channel_id=1, source_target_pairs={{0,16},{4,20},{8,24},{12,28},{16,0},{20,4},{24,8},{28,12},{1,17},{... | collective-permute-start | bytes 368648 | tf_op jit(solution)/shard_map/ppermute | solution.py:362
  184.4 7.9 %gate_up_weight_grad.3 = (f32[2,1536,1024]{2,1,0:T(8,128)}, f32[2,1536,1024]{2,1,0:T(8,128)}) custom-call(s32[1]{0:T(128)} %bitcast.core, bf16[160,1536]{1,0:T(8,128)(2,1)S(1)} %constant_dynamic-update-slice_fusion.3.first.refs_0_, bf16[160,1536]{1,0:T(8,128)(2,1)S(1)} %collective-permute-done.10.second.refs_1_, ...), custom_call_target="tpu_custom_call", output_to_operand_aliasing={{0}: (7, {}), {1}: (8, {})} | custom-call | flops 2013265920 | bytes 12582912 | tf_op jit(solution)/shard_map/gate_up_weight_grad/pallas_call | solution.py:322
  192.4 2.4 %collective-permute-done.16.refs_2_ = bf16[40,1536]{1,0:T(8,128)(2,1)S(1)} collective-permute-done((bf16[40,1536]{1,0:T(8,128)(2,1)S(1)}, bf16[40,1536]{1,0:T(8,128)(2,1)S(1)}, u32[]{:S(2)}, u32[]{:S(2)}) %collective-permute-start.16) | collective-permute-done | bytes 122912 | tf_op jit(solution)/shard_map/ppermute | solution.py:362
  194.8 2.6 %collective-permute-done.17.refs_3_ = bf16[40,1536]{1,0:T(8,128)(2,1)S(1)} collective-permute-done((bf16[40,1536]{1,0:T(8,128)(2,1)S(1)}, bf16[40,1536]{1,0:T(8,128)(2,1)S(1)}, u32[]{:S(2)}, u32[]{:S(2)}) %collective-permute-start.17) | collective-permute-done | bytes 122912 | tf_op jit(solution)/shard_map/ppermute | solution.py:362
  200.1 2.4 %collective-permute-done.35.refs_3_ = bf16[40,1536]{1,0:T(8,128)(2,1)S(1)} collective-permute-done((bf16[40,1536]{1,0:T(8,128)(2,1)S(1)}, bf16[40,1536]{1,0:T(8,128)(2,1)S(1)}, u32[]{:S(2)}, u32[]{:S(2)}) %collective-permute-start.35) | collective-permute-done | bytes 122912 | tf_op jit(solution)/shard_map/ppermute | solution.py:362
  (116 shorter events, 47.4 us)
Async XLA Ops:
  5.8 19.0 %collective-permute-start = (bf16[40,1536]{1,0:T(8,128)(2,1)}, bf16[40,1536]{1,0:T(8,128)(2,1)}, u32[]{:S(2)}, u32[]{:S(2)}) collective-permute-start(bf16[40,1536]{1,0:T(8,128)(2,1)} %get-tuple-element.53), channel_id=1, source_target_pairs={{0,16},{4,20},{8,24},{12,28},{16,0},{20,4},{24,8},{28,12},{1,17},{... | collective-permute-start | bytes 368648 | tf_op jit(solution)/shard_map/ppermute | solution.py:362
  9.8 17.7 %collective-permute-start.8 = (bf16[40,1536]{1,0:T(8,128)(2,1)}, bf16[40,1536]{1,0:T(8,128)(2,1)}, u32[]{:S(2)}, u32[]{:S(2)}) collective-permute-start(bf16[40,1536]{1,0:T(8,128)(2,1)} %get-tuple-element.62), channel_id=1, source_target_pairs={{0,16},{4,20},{8,24},{12,28},{16,0},{20,4},{24,8},{28,12},{1,17},{... | collective-permute-start | bytes 368648 | tf_op jit(solution)/shard_map/ppermute | solution.py:362
  9.8 20.3 %collective-permute-start.18 = (bf16[40,1536]{1,0:T(8,128)(2,1)S(1)}, bf16[40,1536]{1,0:T(8,128)(2,1)}, u32[]{:S(2)}, u32[]{:S(2)}) collective-permute-start(bf16[40,1536]{1,0:T(8,128)(2,1)S(1)} %get-tuple-element.74), channel_id=1, source_target_pairs={{0,16},{4,20},{8,24},{12,28},{16,0},{20,4},{24,8},{28,12},{1,17},{... | collective-permute-start | bytes 368648 | tf_op jit(solution)/shard_map/ppermute | solution.py:362
  12.7 19.2 %collective-permute-start.26 = (bf16[40,1536]{1,0:T(8,128)(2,1)S(1)}, bf16[40,1536]{1,0:T(8,128)(2,1)}, u32[]{:S(2)}, u32[]{:S(2)}) collective-permute-start(bf16[40,1536]{1,0:T(8,128)(2,1)S(1)} %get-tuple-element.83), channel_id=1, source_target_pairs={{0,16},{4,20},{8,24},{12,28},{16,0},{20,4},{24,8},{28,12},{1,17},{... | collective-permute-start | bytes 368648 | tf_op jit(solution)/shard_map/ppermute | solution.py:362
  25.8 11.3 %collective-permute-start.1 = (bf16[80,1536]{1,0:T(8,128)(2,1)S(1)}, bf16[80,1536]{1,0:T(8,128)(2,1)S(1)}, u32[]{:S(2)}, u32[]{:S(2)}) collective-permute-start(bf16[80,1536]{1,0:T(8,128)(2,1)S(1)} %pad_maximum_fusion), channel_id=1, source_target_pairs={{0,8},{4,12},{8,0},{12,4},{16,24},{20,28},{24,16},{28,20},{1,9},{5... | collective-permute-start | bytes 737288 | tf_op jit(solution)/shard_map/ppermute | solution.py:362
  28.5 13.9 %collective-permute-start.9 = (bf16[80,1536]{1,0:T(8,128)(2,1)S(1)}, bf16[80,1536]{1,0:T(8,128)(2,1)S(1)}, u32[]{:S(2)}, u32[]{:S(2)}) collective-permute-start(bf16[80,1536]{1,0:T(8,128)(2,1)S(1)} %pad_maximum_fusion.1), channel_id=1, source_target_pairs={{0,8},{4,12},{8,0},{12,4},{16,24},{20,28},{24,16},{28,20},{1,9},{5... | collective-permute-start | bytes 737288 | tf_op jit(solution)/shard_map/ppermute | solution.py:362
  31.1 16.6 %collective-permute-start.19 = (bf16[80,1536]{1,0:T(8,128)(2,1)S(1)}, bf16[80,1536]{1,0:T(8,128)(2,1)S(1)}, u32[]{:S(2)}, u32[]{:S(2)}) collective-permute-start(bf16[80,1536]{1,0:T(8,128)(2,1)S(1)} %pad_maximum_fusion.2), channel_id=1, source_target_pairs={{0,8},{4,12},{8,0},{12,4},{16,24},{20,28},{24,16},{28,20},{1,9},{5... | collective-permute-start | bytes 737288 | tf_op jit(solution)/shard_map/ppermute | solution.py:362
  32.9 35.7 %collective-permute-start.27 = (bf16[80,1536]{1,0:T(8,128)(2,1)S(1)}, bf16[80,1536]{1,0:T(8,128)(2,1)S(1)}, u32[]{:S(2)}, u32[]{:S(2)}) collective-permute-start(bf16[80,1536]{1,0:T(8,128)(2,1)S(1)} %pad_maximum_fusion.3), channel_id=1, source_target_pairs={{0,8},{4,12},{8,0},{12,4},{16,24},{20,28},{24,16},{28,20},{1,9},{5... | collective-permute-start | bytes 737288 | tf_op jit(solution)/shard_map/ppermute | solution.py:362
  37.1 14.2 %collective-permute-start.2 = (bf16[160,1536]{1,0:T(8,128)(2,1)S(1)}, bf16[160,1536]{1,0:T(8,128)(2,1)S(1)}, u32[]{:S(2)}, u32[]{:S(2)}) collective-permute-start(bf16[160,1536]{1,0:T(8,128)(2,1)S(1)} %constant_dynamic-update-slice_fusion.first.refs_0_), channel_id=1, source_target_pairs={{0,4},{4,0},{8,12},{12,8},{16,20},{20,16},{24,28},{28,24},{1,5},{5... | collective-permute-start | bytes 1474568 | tf_op jit(solution)/shard_map/ppermute | solution.py:362
  42.4 19.4 %collective-permute-start.10 = (bf16[160,1536]{1,0:T(8,128)(2,1)S(1)}, bf16[160,1536]{1,0:T(8,128)(2,1)S(1)}, u32[]{:S(2)}, u32[]{:S(2)}) collective-permute-start(bf16[160,1536]{1,0:T(8,128)(2,1)S(1)} %constant_dynamic-update-slice_fusion.3.first.refs_0_), channel_id=1, source_target_pairs={{0,4},{4,0},{8,12},{12,8},{16,20},{20,16},{24,28},{28,24},{1,5},{5... | collective-permute-start | bytes 1474568 | tf_op jit(solution)/shard_map/ppermute | solution.py:362
  47.7 24.4 %collective-permute-start.20 = (bf16[160,1536]{1,0:T(8,128)(2,1)S(1)}, bf16[160,1536]{1,0:T(8,128)(2,1)S(1)}, u32[]{:S(2)}, u32[]{:S(2)}) collective-permute-start(bf16[160,1536]{1,0:T(8,128)(2,1)S(1)} %constant_dynamic-update-slice_fusion.6.first.refs_0_), channel_id=1, source_target_pairs={{0,4},{4,0},{8,12},{12,8},{16,20},{20,16},{24,28},{28,24},{1,5},{5... | collective-permute-start | bytes 1474568 | tf_op jit(solution)/shard_map/ppermute | solution.py:362
  68.6 13.7 %collective-permute-start.28 = (bf16[160,1536]{1,0:T(8,128)(2,1)S(1)}, bf16[160,1536]{1,0:T(8,128)(2,1)S(1)}, u32[]{:S(2)}, u32[]{:S(2)}) collective-permute-start(bf16[160,1536]{1,0:T(8,128)(2,1)S(1)} %constant_dynamic-update-slice_fusion.9.first.refs_0_), channel_id=1, source_target_pairs={{0,4},{4,0},{8,12},{12,8},{16,20},{20,16},{24,28},{28,24},{1,5},{5... | collective-permute-start | bytes 1474568 | tf_op jit(solution)/shard_map/ppermute | solution.py:362
  70.5 18.1 %collective-permute-start.4 = (bf16[2,320,512]{2,1,0:T(8,128)(2,1)S(1)}, bf16[2,320,512]{2,1,0:T(8,128)(2,1)S(1)}, u32[]{:S(2)}, u32[]{:S(2)}) collective-permute-start(bf16[2,320,512]{2,1,0:T(8,128)(2,1)S(1)} %add.9), channel_id=1, source_target_pairs={{0,2},{1,3},{2,0},{3,1},{4,6},{5,7},{6,4},{7,5},{8,10},{9,11},{10,... | collective-permute-start | bytes 1966088 | tf_op jit(solution)/shard_map/ppermute | solution.py:369
  75.0 10.3 %collective-permute-start.21 = (bf16[1,320,512]{2,1,0:T(8,128)(2,1)S(1)}, bf16[1,320,512]{2,1,0:T(8,128)(2,1)S(1)}, u32[]{:S(2)}, u32[]{:S(2)}) collective-permute-start(bf16[1,320,512]{2,1,0:T(8,128)(2,1)S(1)} %get-tuple-element.76), channel_id=1, source_target_pairs={{0,1},{1,0},{2,3},{3,2},{4,5},{5,4},{6,7},{7,6},{8,9},{9,8},{10,11... | collective-permute-start | bytes 983048 | tf_op jit(solution)/shard_map/ppermute | solution.py:365
  75.2 34.5 %collective-permute-start.12 = (bf16[2,320,512]{2,1,0:T(8,128)(2,1)S(1)}, bf16[2,320,512]{2,1,0:T(8,128)(2,1)S(1)}, u32[]{:S(2)}, u32[]{:S(2)}) collective-permute-start(bf16[2,320,512]{2,1,0:T(8,128)(2,1)S(1)} %add.10), channel_id=1, source_target_pairs={{0,2},{1,3},{2,0},{3,1},{4,6},{5,7},{6,4},{7,5},{8,10},{9,11},{10,... | collective-permute-start | bytes 1966088 | tf_op jit(solution)/shard_map/ppermute | solution.py:369
  85.3 23.9 %collective-permute-start.22 = (bf16[1,320,512]{2,1,0:T(8,128)(2,1)S(1)}, bf16[1,320,512]{2,1,0:T(8,128)(2,1)S(1)}, u32[]{:S(2)}, u32[]{:S(2)}) collective-permute-start(bf16[1,320,512]{2,1,0:T(8,128)(2,1)S(1)} %add.11), channel_id=1, source_target_pairs={{0,2},{1,3},{2,0},{3,1},{4,6},{5,7},{6,4},{7,5},{8,10},{9,11},{10,... | collective-permute-start | bytes 983048 | tf_op jit(solution)/shard_map/ppermute | solution.py:369
  87.1 28.4 %collective-permute-start.30 = (bf16[1,320,512]{2,1,0:T(8,128)(2,1)S(1)}, bf16[1,320,512]{2,1,0:T(8,128)(2,1)S(1)}, u32[]{:S(2)}, u32[]{:S(2)}) collective-permute-start(bf16[1,320,512]{2,1,0:T(8,128)(2,1)S(1)} %add.12), channel_id=1, source_target_pairs={{0,2},{1,3},{2,0},{3,1},{4,6},{5,7},{6,4},{7,5},{8,10},{9,11},{10,... | collective-permute-start | bytes 983048 | tf_op jit(solution)/shard_map/ppermute | solution.py:369
  88.9 27.1 %collective-permute-start.5 = (bf16[320,512]{1,0:T(8,128)(2,1)S(1)}, bf16[320,512]{1,0:T(8,128)(2,1)S(1)}, u32[]{:S(2)}, u32[]{:S(2)}) collective-permute-start(bf16[320,512]{1,0:T(8,128)(2,1)S(1)} %get-tuple-element.56.refs_0_.refs_2_), channel_id=1, source_target_pairs={{0,1},{1,0},{2,3},{3,2},{4,5},{5,4},{6,7},{7,6},{8,9},{9,8},{10,11... | collective-permute-start | bytes 983048 | tf_op jit(solution)/shard_map/ppermute | solution.py:365
  109.6 13.7 %collective-permute-start.23 = (bf16[2,320,512]{2,1,0:T(8,128)(2,1)S(1)}, bf16[2,320,512]{2,1,0:T(8,128)(2,1)S(1)}, u32[]{:S(2)}, u32[]{:S(2)}) collective-permute-start(bf16[2,320,512]{2,1,0:T(8,128)(2,1)S(1)} %gate_up_grads.2), channel_id=1, source_target_pairs={{0,1},{1,0},{2,3},{3,2},{4,5},{5,4},{6,7},{7,6},{8,9},{9,8},{10,11... | collective-permute-start | bytes 1966088 | tf_op jit(solution)/shard_map/ppermute | solution.py:365
  115.9 12.0 %collective-permute-start.31 = (bf16[2,320,512]{2,1,0:T(8,128)(2,1)S(1)}, bf16[2,320,512]{2,1,0:T(8,128)(2,1)S(1)}, u32[]{:S(2)}, u32[]{:S(2)}) collective-permute-start(bf16[2,320,512]{2,1,0:T(8,128)(2,1)S(1)} %gate_up_grads.3), channel_id=1, source_target_pairs={{0,1},{1,0},{2,3},{3,2},{4,5},{5,4},{6,7},{7,6},{8,9},{9,8},{10,11... | collective-permute-start | bytes 1966088 | tf_op jit(solution)/shard_map/ppermute | solution.py:365
  118.6 20.2 %collective-permute-start.6 = (bf16[160,1536]{1,0:T(8,128)(2,1)S(1)}, bf16[160,1536]{1,0:T(8,128)(2,1)S(1)}, u32[]{:S(2)}, u32[]{:S(2)}) collective-permute-start(bf16[160,1536]{1,0:T(8,128)(2,1)S(1)} %get-tuple-element.58), channel_id=1, source_target_pairs={{0,4},{4,0},{8,12},{12,8},{16,20},{20,16},{24,28},{28,24},{1,5},{5... | collective-permute-start | bytes 1474568 | tf_op jit(solution)/shard_map/ppermute | solution.py:362
  121.6 21.7 %collective-permute-start.14 = (bf16[160,1536]{1,0:T(8,128)(2,1)S(1)}, bf16[160,1536]{1,0:T(8,128)(2,1)S(1)}, u32[]{:S(2)}, u32[]{:S(2)}) collective-permute-start(bf16[160,1536]{1,0:T(8,128)(2,1)S(1)} %get-tuple-element.67), channel_id=1, source_target_pairs={{0,4},{4,0},{8,12},{12,8},{16,20},{20,16},{24,28},{28,24},{1,5},{5... | collective-permute-start | bytes 1474568 | tf_op jit(solution)/shard_map/ppermute | solution.py:362
  127.5 26.3 %collective-permute-start.24 = (bf16[160,1536]{1,0:T(8,128)(2,1)S(1)}, bf16[160,1536]{1,0:T(8,128)(2,1)S(1)}, u32[]{:S(2)}, u32[]{:S(2)}) collective-permute-start(bf16[160,1536]{1,0:T(8,128)(2,1)S(1)} %get-tuple-element.78), channel_id=1, source_target_pairs={{0,4},{4,0},{8,12},{12,8},{16,20},{20,16},{24,28},{28,24},{1,5},{5... | collective-permute-start | bytes 1474568 | tf_op jit(solution)/shard_map/ppermute | solution.py:362
  132.1 31.8 %collective-permute-start.32 = (bf16[160,1536]{1,0:T(8,128)(2,1)S(1)}, bf16[160,1536]{1,0:T(8,128)(2,1)S(1)}, u32[]{:S(2)}, u32[]{:S(2)}) collective-permute-start(bf16[160,1536]{1,0:T(8,128)(2,1)S(1)} %get-tuple-element.87), channel_id=1, source_target_pairs={{0,4},{4,0},{8,12},{12,8},{16,20},{20,16},{24,28},{28,24},{1,5},{5... | collective-permute-start | bytes 1474568 | tf_op jit(solution)/shard_map/ppermute | solution.py:362
  139.0 38.6 %collective-permute-start.7 = (bf16[80,1536]{1,0:T(8,128)(2,1)S(1)}, bf16[80,1536]{1,0:T(8,128)(2,1)S(1)}, u32[]{:S(2)}, u32[]{:S(2)}) collective-permute-start(bf16[80,1536]{1,0:T(8,128)(2,1)S(1)} %get-tuple-element.60), channel_id=1, source_target_pairs={{0,8},{4,12},{8,0},{12,4},{16,24},{20,28},{24,16},{28,20},{1,9},{5... | collective-permute-start | bytes 737288 | tf_op jit(solution)/shard_map/ppermute | solution.py:362
  143.3 37.8 %collective-permute-start.15 = (bf16[80,1536]{1,0:T(8,128)(2,1)S(1)}, bf16[80,1536]{1,0:T(8,128)(2,1)S(1)}, u32[]{:S(2)}, u32[]{:S(2)}) collective-permute-start(bf16[80,1536]{1,0:T(8,128)(2,1)S(1)} %get-tuple-element.69), channel_id=1, source_target_pairs={{0,8},{4,12},{8,0},{12,4},{16,24},{20,28},{24,16},{28,20},{1,9},{5... | collective-permute-start | bytes 737288 | tf_op jit(solution)/shard_map/ppermute | solution.py:362
  153.9 27.4 %collective-permute-start.25 = (bf16[80,1536]{1,0:T(8,128)(2,1)S(1)}, bf16[80,1536]{1,0:T(8,128)(2,1)S(1)}, u32[]{:S(2)}, u32[]{:S(2)}) collective-permute-start(bf16[80,1536]{1,0:T(8,128)(2,1)S(1)} %get-tuple-element.80), channel_id=1, source_target_pairs={{0,8},{4,12},{8,0},{12,4},{16,24},{20,28},{24,16},{28,20},{1,9},{5... | collective-permute-start | bytes 737288 | tf_op jit(solution)/shard_map/ppermute | solution.py:362
  164.0 20.3 %collective-permute-start.33 = (bf16[80,1536]{1,0:T(8,128)(2,1)S(1)}, bf16[80,1536]{1,0:T(8,128)(2,1)S(1)}, u32[]{:S(2)}, u32[]{:S(2)}) collective-permute-start(bf16[80,1536]{1,0:T(8,128)(2,1)S(1)} %get-tuple-element.89), channel_id=1, source_target_pairs={{0,8},{4,12},{8,0},{12,4},{16,24},{20,28},{24,16},{28,20},{1,9},{5... | collective-permute-start | bytes 737288 | tf_op jit(solution)/shard_map/ppermute | solution.py:362
  177.7 17.1 %collective-permute-start.16 = (bf16[40,1536]{1,0:T(8,128)(2,1)S(1)}, bf16[40,1536]{1,0:T(8,128)(2,1)S(1)}, u32[]{:S(2)}, u32[]{:S(2)}) collective-permute-start(bf16[40,1536]{1,0:T(8,128)(2,1)S(1)} %get-tuple-element.71), channel_id=1, source_target_pairs={{0,16},{4,20},{8,24},{12,28},{16,0},{20,4},{24,8},{28,12},{1,17},{... | collective-permute-start | bytes 368648 | tf_op jit(solution)/shard_map/ppermute | solution.py:362
  181.2 16.3 %collective-permute-start.17 = (bf16[40,1536]{1,0:T(8,128)(2,1)S(1)}, bf16[40,1536]{1,0:T(8,128)(2,1)S(1)}, u32[]{:S(2)}, u32[]{:S(2)}) collective-permute-start(bf16[40,1536]{1,0:T(8,128)(2,1)S(1)} %get-tuple-element.72), channel_id=1, source_target_pairs={{0,16},{4,20},{8,24},{12,28},{16,0},{20,4},{24,8},{28,12},{1,17},{... | collective-permute-start | bytes 368648 | tf_op jit(solution)/shard_map/ppermute | solution.py:362
  181.3 18.8 %collective-permute-start.34 = (bf16[40,1536]{1,0:T(8,128)(2,1)S(1)}, bf16[40,1536]{1,0:T(8,128)(2,1)S(1)}, u32[]{:S(2)}, u32[]{:S(2)}) collective-permute-start(bf16[40,1536]{1,0:T(8,128)(2,1)S(1)} %get-tuple-element.91), channel_id=1, source_target_pairs={{0,16},{4,20},{8,24},{12,28},{16,0},{20,4},{24,8},{28,12},{1,17},{... | collective-permute-start | bytes 368648 | tf_op jit(solution)/shard_map/ppermute | solution.py:362
  184.4 18.1 %collective-permute-start.35 = (bf16[40,1536]{1,0:T(8,128)(2,1)S(1)}, bf16[40,1536]{1,0:T(8,128)(2,1)S(1)}, u32[]{:S(2)}, u32[]{:S(2)}) collective-permute-start(bf16[40,1536]{1,0:T(8,128)(2,1)S(1)} %get-tuple-element.92), channel_id=1, source_target_pairs={{0,16},{4,20},{8,24},{12,28},{16,0},{20,4},{24,8},{28,12},{1,17},{... | collective-permute-start | bytes 368648 | tf_op jit(solution)/shard_map/ppermute | solution.py:362
  (15 other events, 142.0 us)

commit v2 on v0

v2 whole, which is shorter than its diff:
```python
import functools
import jax
import jax.numpy as jnp
from jax import lax
from jax.experimental import pallas as pl
from jax.experimental.pallas import tpu as pltpu
from jax.sharding import PartitionSpec as P

CAP = 40
BF = jnp.bfloat16
F32 = jnp.float32
MIB = 1024 * 1024
LIMIT = 16
VM = pl.BlockSpec(memory_space=pltpu.VMEM)
SM = pl.BlockSpec(memory_space=pltpu.SMEM)
AN = pl.BlockSpec(memory_space=pl.ANY)
ROWS = (((0,), (0,)), ((), ()))
LAST = (((1,), (1,)), ((), ()))


def shape(dims, dtype=BF):
    return jax.ShapeDtypeStruct(dims, dtype)


def mm(a, b):
    return jnp.dot(a, b, preferred_element_type=F32)


class Sequence:
    def __init__(self):
        self.last = None

    def __call__(self, kernel, *args, out_shape, name, in_specs=None, out_specs=None, scratch=(), aliases=None):
        n_in = len(args)
        in_specs = list(in_specs or [VM] * n_in)
        args = list(args)
        extra = 0
        if self.last is not None:
            args.append(self.last)
            in_specs.append(AN)
            extra = 1

        def body(*refs):
            kernel(*refs[:n_in], *refs[n_in + extra :])

        if out_specs is None:
            out_specs = jax.tree.map(lambda o: VM, out_shape)
        out = pl.pallas_call(
            body,
            in_specs=in_specs,
            out_specs=out_specs,
            out_shape=out_shape,
            scratch_shapes=list(scratch),
            input_output_aliases=aliases or {},
            compiler_params=pltpu.CompilerParams(vmem_limit_bytes=LIMIT * MIB),
            cost_estimate=pl.CostEstimate(flops=10**10, bytes_accessed=10**8, transcendentals=0),
            name=name,
        )(*args)
        self.last = min(jax.tree.leaves(out), key=lambda o: o.size)
        return out


def match_of(ids, expert):
    n = ids.shape[1]
    chosen = ids[...] == expert
    routed = jnp.sum(chosen.astype(F32), axis=0, keepdims=True)
    tri = (
        lax.broadcasted_iota(jnp.int32, (n, n), 0) <= lax.broadcasted_iota(jnp.int32, (n, n), 1)
    ).astype(BF)
    position = mm(jnp.broadcast_to(routed, (16, n)).astype(BF), tri)[:1].astype(jnp.int32) - 1
    slots = lax.broadcasted_iota(jnp.int32, (CAP, n), 0)
    match = (position == slots) & (routed > 0.0)
    return chosen, jnp.where(match, 1.0, 0.0)


def rows_kernel(experts, ids, tokens, *outs):
    for e in range(experts):
        _, match = match_of(ids, e)
        outs[e][...] = mm(match.astype(BF), tokens[...]).astype(BF)


def rows_of(run, ids, tokens, experts):
    n, d = tokens.shape
    return run(
        functools.partial(rows_kernel, experts),
        ids,
        tokens,
        out_shape=[shape((CAP, d))] * experts,
        name="rows",
    )


def scaled_kernel(expert, ids, cw, grad, scaled, pick, weight):
    chosen, match = match_of(ids, expert)
    w = jnp.sum(jnp.where(chosen, cw[...], 0.0), axis=0, keepdims=True)
    slot = jnp.sum(match * w, axis=1, keepdims=True)
    scaled[...] = (slot * mm(match.astype(BF), grad[...])).astype(BF)
    pick[...] = match.astype(BF)
    weight[...] = jnp.broadcast_to(slot, weight.shape)


def scaled_of(run, ids, cw, grad, expert):
    n, d = grad.shape
    return run(
        functools.partial(scaled_kernel, expert),
        ids,
        cw,
        grad,
        out_shape=[shape((CAP, d)), shape((CAP, n)), shape((CAP, 128), F32)],
        name="scaled",
    )


def swapped(q):
    n = q.shape[0] // 4
    return jnp.concatenate([q[:n], q[2 * n : 3 * n], q[n : 2 * n], q[3 * n :]], axis=0)


def project_kernel(count, parts, expert, transposed, swap, core, *refs):
    acts, weights = refs[:count], refs[count : count + parts]
    outs = refs[count + parts :]
    act = acts[0][...] if count == 1 else jnp.concatenate([a[...] for a in acts], axis=0)
    if swap:
        act = swapped(act)
    half = outs[0].shape[2]
    fb = min(256, half)
    mine = core[0] * half
    for out, base in zip(outs, (mine, half - mine)):
        for p in range(parts):
            for j in range(half // fb):
                part = pl.ds(pl.multiple_of(base + j * fb, fb), fb)
                if transposed:
                    val = lax.dot_general(
                        act, weights[p][expert, part, :], LAST, preferred_element_type=F32
                    )
                else:
                    val = mm(act, weights[p][expert, :, part])
                out[p, :, j * fb : (j + 1) * fb] = val.astype(BF)


def project(run, core, acts, weights, expert, transposed, swap=False):
    h, d = acts[0].shape
    r = h * len(acts)
    f = weights[0].shape[1] if transposed else weights[0].shape[2]
    parts = len(weights)
    return run(
        functools.partial(project_kernel, len(acts), parts, expert, transposed, swap),
        core,
        *acts,
        *weights,
        in_specs=[SM] + [VM] * (len(acts) + parts),
        out_shape=[shape((parts, r, f // 2))] * 2,
        name="hidden_grad_part" if transposed else "gate_up_part",
    )


def back_kernel(parts, expert, transposed, swap, core, mine, other, *refs):
    weights, keep, send = refs[:parts], refs[parts], refs[parts + 1]
    h, d = keep.shape
    half = mine.shape[2]
    db = 256 if d % 256 == 0 else 128
    first = core[0] * half
    bases = [pl.ds(pl.multiple_of(b, half), half) for b in (first, half - first)]
    for j in range(d // db):
        cols = slice(j * db, (j + 1) * db)
        total = None
        for p in range(parts):
            for act, base in zip((mine, other), bases):
                if transposed:
                    val = lax.dot_general(
                        act[p], weights[p][expert, cols, base], LAST, preferred_element_type=F32
                    )
                else:
                    val = mm(act[p], weights[p][expert, base, cols])
                total = val if total is None else total + val
        total = total.astype(BF)
        if swap:
            total = swapped(total)
        keep[:, cols] = total[:h]
        send[:, cols] = total[h:]


def back(run, core, mine, other, weights, expert, transposed, swap=False):
    parts, r, _ = mine.shape
    d = weights[0].shape[1] if transposed else weights[0].shape[2]
    return run(
        functools.partial(back_kernel, parts, expert, transposed, swap),
        core,
        mine,
        other,
        *weights,
        in_specs=[SM] + [VM] * (2 + parts),
        out_shape=[shape((r // 2, d))] * 2,
        name="row_grad_part" if transposed else "expert_part",
    )


def add_kernel(keep, got, out):
    out[...] = (keep[...].astype(F32) + got[...].astype(F32)).astype(BF)


def add(run, keep, got):
    return run(
        add_kernel,
        keep,
        got,
        out_shape=shape(keep.shape),
        name="add",
    )


def halve_kernel(keep, got, out_keep, out_send):
    h = out_keep.shape[0]
    total = (keep[...].astype(F32) + got[...].astype(F32)).astype(BF)
    out_keep[...] = total[:h]
    out_send[...] = total[h:]


def halve(run, keep, got):
    r, d = keep.shape
    return run(
        halve_kernel,
        keep,
        got,
        out_shape=[shape((r // 2, d))] * 2,
        name="halve",
    )


def join_kernel(a, b, out):
    n = a.shape[0]
    out[:n] = a[...]
    out[n:] = b[...]


def join(run, a, b):
    return run(
        join_kernel,
        a,
        b,
        out_shape=shape((2 * a.shape[0], a.shape[1])),
        name="join",
    )


def total_of(terms):
    total = 0.0
    for ref in terms:
        total = total + ref[...].astype(F32)
    return total


def sum_kernel(*refs):
    refs[-1][...] = total_of(refs[:-1])


def sum_of(run, terms):
    return run(sum_kernel, *terms, out_shape=shape(terms[0].shape, F32), name="sum")


def hidden_kernel(counts, *refs):
    sums, hidden = refs[-2:]
    h = sums.shape[1] // len(counts)
    at = 0
    for i, n in enumerate(counts):
        total = total_of(refs[at : at + n])
        at += n
        sums[:, i * h : (i + 1) * h, :] = total
        gate, up = total[0], total[1]
        hidden[0, i * h : (i + 1) * h, :] = (gate * jax.nn.sigmoid(gate) * up).astype(BF)


def hidden_of(run, groups):
    flat = [t for group in groups for t in group]
    _, h, half = flat[0].shape
    r = h * len(groups)
    return run(
        functools.partial(hidden_kernel, [len(g) for g in groups]),
        *flat,
        out_shape=[shape((2, r, half), F32), shape((1, r, half))],
        name="hidden",
    )


def grads_kernel(sums, *refs):
    terms, out = refs[:-1], refs[-1]
    total = 0.0
    for ref in terms:
        total = total + ref[0].astype(F32)
    gate, up = sums[0], sums[1]
    sig = jax.nn.sigmoid(gate)
    out[0] = (total * up * sig * (1.0 + gate * (1.0 - sig))).astype(BF)
    out[1] = (total * gate * sig).astype(BF)


def grads_of(run, sums, terms):
    _, r, half = sums.shape
    return run(
        grads_kernel,
        sums,
        *terms,
        out_shape=shape((2, r, half)),
        name="gate_up_grads",
    )


SLOTS = 4


def weight_kernel(which, expert, by_columns, swap, core, first, second, mine, other, *refs):
    token, slots, sem = refs[-3:]
    out = refs[-4]
    d = first.shape[1]
    half = mine.shape[2]
    db = slots.shape[1] if by_columns else slots.shape[2]
    token[...] = jnp.zeros(token.shape, F32)
    act = jnp.concatenate([first[...], second[...]], axis=0)
    if swap:
        act = swapped(act)
    base = core[0] * half
    bases = [pl.ds(pl.multiple_of(b, half), half) for b in (base, half - base)]
    pending = []

    def put(val, dst):
        i = len(pending)
        if i >= SLOTS:
            pending[i - SLOTS].wait()
        slots[i % SLOTS] = val
        copy = pltpu.make_async_copy(slots.at[i % SLOTS], dst, sem.at[i % SLOTS])
        copy.start()
        pending.append(copy)

    if by_columns:
        for j in range(d // db):
            cols = slice(j * db, (j + 1) * db)
            turned = act[:, cols].T
            for grads, part in zip((mine, other), bases):
                put(mm(turned, grads[which]), out.at[expert, pl.ds(j * db, db), part])
    else:
        for grads, part in zip((mine, other), bases):
            turned = grads[which].T
            for j in range(d // db):
                cols = slice(j * db, (j + 1) * db)
                put(mm(turned, act[:, cols]), out.at[expert, part, pl.ds(j * db, db)])
    for copy in pending[-SLOTS:]:
        copy.wait()


def weight_grads(run, core, first, second, mine, other, which, expert, experts, prev, by_columns, swap=False):
    h, d = first.shape
    _, r, half = mine.shape
    db = 512 if d % 512 == 0 else 128
    if by_columns:
        out = shape((experts, d, 2 * half), F32)
        slot = (SLOTS, db, half)
    else:
        out = shape((experts, 2 * half, d), F32)
        slot = (SLOTS, half, db)
    extra = [] if prev is None else [prev]
    return run(
        functools.partial(weight_kernel, which, expert, by_columns, swap),
        core,
        first,
        second,
        mine,
        other,
        *extra,
        in_specs=[SM] + [VM] * 4 + [AN] * len(extra),
        out_specs=[AN, VM],
        out_shape=[out, shape((8, 128), F32)],
        scratch=[pltpu.VMEM(slot, F32), pltpu.SemaphoreType.DMA((SLOTS,))],
        aliases={5: 0} if extra else {},
        name="weight_grad",
    )[0]


def combine_kernel(experts, weighted, *refs):
    picks, weights = refs[:experts], refs[experts : 2 * experts]
    keeps, gots = refs[2 * experts : 3 * experts], refs[3 * experts : 4 * experts]
    out = refs[-1]
    total = 0.0
    for e in range(experts):
        val = keeps[e][...].astype(F32) + gots[e][...].astype(F32)
        if weighted:
            val = weights[e][:, :1] * val
        total = total + lax.dot_general(
            picks[e][...], val.astype(BF), ROWS, preferred_element_type=F32
        )
    out[...] = total.astype(BF)


def combine(run, picks, weights, pairs, weighted):
    experts, (_, n) = len(picks), picks[0].shape
    d = pairs[0][0].shape[1]
    args = [*picks, *weights, *[p[0] for p in pairs], *[p[1] for p in pairs]]
    return run(
        functools.partial(combine_kernel, experts, weighted),
        *args,
        out_shape=shape((n, d)),
        name="combine",
    )


def build(n_dp, n_own):
    bits = n_dp.bit_length() - 1
    plain = list(range(bits - 1, -1, -1))
    mixed_order = plain[:-2] + [0, 1]

    def swap(x, bit):
        return lax.ppermute(x, "dp", [(i, i ^ (1 << bit)) for i in range(n_dp)])

    def swap_core(x):
        return lax.ppermute(x, "own", [(i, i ^ 1) for i in range(n_own)])

    def shift_x(x):
        return [
            lax.ppermute(x, "own", [(i, (i + 2 * k) % n_own) for i in range(n_own)])
            for k in range(1, n_own // 2)
        ]

    def gather(run, x, order):
        for bit in order[:-1]:
            got = swap(x, bit)
            yield None
            x = join(run, x, got)
        yield x, swap(x, order[-1])

    def scatter(run, keep, send, order):
        for bit in order[:0:-1]:
            got = swap(send, bit)
            yield None
            keep, send = halve(run, keep, got)
        yield keep, swap(send, order[0])

    def local(tokens, expert_ids, combine_weights, gate_weight, up_weight, down_weight, out_grad):
        run = Sequence()
        experts = gate_weight.shape[0]
        core = (lax.axis_index("own") % 2).astype(jnp.int32).reshape(1)
        ids, cw = expert_ids.T, combine_weights.T
        near = len(plain) - 1

        def steps(gen, n):
            for _ in range(n):
                res = next(gen)
            return res

        def up_gate_part(rows, e):
            keep, send = project(run, core, rows, [gate_weight, up_weight], e, False)
            return keep, swap_core(send)

        def across(part):
            return (*part, *shift_x(add(run, *part)))

        r0, r1 = rows_of(run, ids, tokens, experts)
        a0, a1 = gather(run, r0, plain), gather(run, r1, mixed_order)
        next(a0)
        next(a1)
        steps(a0, near - 1)
        steps(a1, near - 1)
        s0, pick0, weight0 = scaled_of(run, ids, cw, out_grad, 0)
        g0 = gather(run, s0, plain)
        next(g0)
        rows0 = next(a0)
        p0a = up_gate_part(rows0[:1], 0)
        rows1 = next(a1)
        u0a = across(p0a)
        p1a = up_gate_part(rows1[:1], 1)
        steps(g0, near - 1)
        u1a = across(p1a)
        p0b = up_gate_part(rows0[1:], 0)
        scaled0 = next(g0)
        u0b = across(p0b)
        p1b = up_gate_part(rows1[1:], 1)
        u0a = (sum_of(run, u0a),)
        s1, pick1, weight1 = scaled_of(run, ids, cw, out_grad, 1)
        g1 = gather(run, s1, plain)
        next(g1)
        u1b = across(p1b)
        steps(g1, near - 1)
        u1a = (sum_of(run, u1a),)
        scaled1 = next(g1)
        sums0, hidden0 = hidden_of(run, (u0a, u0b))
        hidden0 = (hidden0, swap_core(hidden0))
        hp0 = project(run, core, scaled0, [down_weight], 0, True)
        hp0 = (hp0[0], swap_core(hp0[1]))
        o0 = scatter(run, *back(run, core, *hidden0, [down_weight], 0, False), plain)
        next(o0)
        h0 = across(hp0)
        sums1, hidden1 = hidden_of(run, (u1a, u1b))
        hidden1 = (hidden1, swap_core(hidden1))
        hp1 = project(run, core, scaled1, [down_weight], 1, True, True)
        hp1 = (hp1[0], swap_core(hp1[1]))
        o1 = scatter(run, *back(run, core, *hidden1, [down_weight], 1, False, True), plain)
        next(o1)
        h1 = across(hp1)
        d0 = grads_of(run, sums0, h0)
        d0 = (d0, swap_core(d0))
        down = weight_grads(run, core, *scaled0, *hidden0, 0, 0, experts, None, False)
        q0 = scatter(run, *back(run, core, *d0, [gate_weight, up_weight], 0, True), plain)
        next(q0)
        next(o0)
        d1 = grads_of(run, sums1, h1)
        d1 = (d1, swap_core(d1))
        down = weight_grads(run, core, *scaled1, *hidden1, 0, 1, experts, down, False, True)
        q1 = scatter(run, *back(run, core, *d1, [gate_weight, up_weight], 1, True), mixed_order)
        next(q1)
        out0 = steps(o0, near - 1)
        next(o1)
        gate = weight_grads(run, core, *rows0, *d0, 0, 0, experts, None, True)
        next(q1)
        next(q0)
        up = weight_grads(run, core, *rows0, *d0, 1, 0, experts, None, True)
        out1 = steps(o1, near - 1)
        row1 = steps(q1, near - 1)
        gate = weight_grads(run, core, *rows1, *d1, 0, 1, experts, gate, True)
        row0 = steps(q0, near - 1)
        up = weight_grads(run, core, *rows1, *d1, 1, 1, experts, up, True)
        picks, weights = (pick0, pick1), (weight0, weight1)
        mixed = combine(run, picks, weights, (out0, out1), True)
        token_grad = combine(run, picks, weights, (row0, row1), False)
        return mixed, token_grad, gate, up, down

    return local


def solution(mesh):
    local = build(mesh.shape["dp"], mesh.shape["own"])
    in_specs = (
        P("dp", "own"),
        P("dp", None),
        P("dp", None),
        P(None, "own", "dp"),
        P(None, "own", "dp"),
        P(None, "dp", "own"),
        P("dp", "own"),
    )
    out_specs = (
        P("dp", "own"),
        P("dp", "own"),
        P(None, "own", "dp"),
        P(None, "own", "dp"),
        P(None, "dp", "own"),
    )
    return jax.shard_map(local, mesh=mesh, in_specs=in_specs, out_specs=out_specs, check_vma=False)
```

time: 389 us -> 155 us (0.40)
  waiting for transfers between devices: 253 us -> 70.3 us
  matrix products: 60.2 us -> 0 us
  Pallas kernels: 0 us -> 40.5 us
  starting transfers between devices: 0.38 us -> 35.6 us
  blocking collectives: 22.3 us -> 0 us
  local copies, waits for them, and re-layouts: 27.1 us -> 6.94 us
  between operations: 14.1 us -> 1.34 us
  other arithmetic: 11.9 us -> 0.01 us
    unnamed x7 -> x0, waiting for transfers between devices: 92.5 us -> none
    all_gather x2 -> x0, waiting for transfers between devices: 80.3 us -> none  [the longest x1 55.1 us: local(): all_tokens = lax.all_gather(tokens, 'dp', axis=0, tiled=True)]
    psum x1 -> x0, waiting for transfers between devices: 80.2 us -> none  [local(): lax.psum(up_part.astype(jnp.bfloat16), 'own').astype(jnp.float32)]
    ppermute x0 -> x40, waiting for transfers between devices: none -> 70.3 us  [the longest x24 67.4 us: swap(): return lax.ppermute(x, 'dp', [(i, i ^ 1 << bit) for i in range(n_dp)])]
    dot_general x9 -> x0, matrix products: 60.2 us -> none  [the longest x1 10.9 us: local(): jnp.einsum('ref,red->efd', hidden, scaled_all, preferred_element_type=jnp...]
    pallas_call x0 -> x49, Pallas kernels: none -> 40.5 us  [__call__(): pl.pallas_call(body, in_specs=in_specs, out_specs=out_specs, out_shape=ou...]
    ppermute x0 -> x40, starting transfers between devices: none -> 35.6 us  [the longest x24 29.6 us: swap(): return lax.ppermute(x, 'dp', [(i, i ^ 1 << bit) for i in range(n_dp)])]
    all_gather x1 -> x0, blocking collectives: 22.3 us -> none  [local(): all_ids = lax.all_gather(expert_ids, 'dp', axis=0, tiled=True)]
  transfers between devices with their start and end apart: 5 -> 40, of which waited for: 5 -> 16; matrix products, arithmetic and copies ran while one was open for 14% -> 0% of each run, Pallas kernels for 0% -> 25%
where the time goes in v2:
time: 155 us
  waiting for transfers between devices  70.3 us (45%)
  Pallas kernels  40.5 us (26%)
  starting transfers between devices  35.6 us (23%)
  local copies, waits for them, and re-layouts  6.94 us (4%)
    ppermute x24, waiting for transfers between devices, swap(): return lax.ppermute(x, 'dp', [(i, i ^ 1 << bit) for i in range(n_dp)])  67.4 us
    pallas_call x49, Pallas kernels, __call__(): pl.pallas_call(body, in_specs=in_specs, out_specs=out_specs, out_shape=ou...  40.5 us
    ppermute x24, starting transfers between devices, swap(): return lax.ppermute(x, 'dp', [(i, i ^ 1 << bit) for i in range(n_dp)])  29.6 us
    unnamed x56, local copies, waits for them, and re-layouts  6.94 us
    ppermute x6, starting transfers between devices, shift_x(): lax.ppermute(x, 'own', [(i, (i + 2 * k) % n_own) for i in range(n_own)])  5.22 us
  transfers between devices with their start and end apart: 40, of which 16 were waited for; matrix products, arithmetic and copies ran while one was open for 0% of the time, Pallas kernels for 25%

profile of v2, /device:TPU:0, one launch (start us, length us, event | category | flops | bytes accessed | tf_op | source)
XLA Modules:
  0.0 154.7 jit_solution(8616826837006184834)
XLA Ops:
  2.8 4.1 %collective-permute-start.1 = (bf16[40,1536]{1,0:T(8,128)(2,1)S(1)}, bf16[40,1536]{1,0:T(8,128)(2,1)S(1)}, u32[]{:S(2)}, u32[]{:S(2)}) collective-permute-start(bf16[40,1536]{1,0:T(8,128)(2,1)S(1)} %get-tuple-element.66.refs_0_.refs_2_), channel_id=1, source_target_pairs={{0,16},{4,20},{8,24},{12,28},{16,0},{20,4},{24,8},{28,12},{1,17},{... | collective-permute-start | bytes 368648 | tf_op jit(solution)/shard_map/ppermute | solution.py:410
  7.0 9.3 %collective-permute-done.1.refs_1_ = bf16[40,1536]{1,0:T(8,128)(2,1)S(1)} collective-permute-done((bf16[40,1536]{1,0:T(8,128)(2,1)S(1)}, bf16[40,1536]{1,0:T(8,128)(2,1)S(1)}, u32[]{:S(2)}, u32[]{:S(2)}) %collective-permute-start.1) | collective-permute-done | bytes 122912 | tf_op jit(solution)/shard_map/ppermute | solution.py:410
  16.5 1.7 %collective-permute-done.refs_1_ = bf16[40,1536]{1,0:T(8,128)(2,1)S(1)} collective-permute-done((bf16[40,1536]{1,0:T(8,128)(2,1)S(1)}, bf16[40,1536]{1,0:T(8,128)(2,1)S(1)}, u32[]{:S(2)}, u32[]{:S(2)}) %collective-permute-start) | collective-permute-done | bytes 122912 | tf_op jit(solution)/shard_map/ppermute | solution.py:410
  18.2 1.7 %collective-permute-start.4 = (bf16[80,1536]{1,0:T(8,128)(2,1)S(1)}, bf16[80,1536]{1,0:T(8,128)(2,1)S(1)}, u32[]{:S(2)}, u32[]{:S(2)}) collective-permute-start(bf16[80,1536]{1,0:T(8,128)(2,1)S(1)} %join.9.refs_3_.refs_0_), channel_id=1, source_target_pairs={{0,4},{4,0},{8,12},{12,8},{16,20},{20,16},{24,28},{28,24},{1,5},{5... | collective-permute-start | bytes 737288 | tf_op jit(solution)/shard_map/ppermute | solution.py:410
  20.3 1.6 %collective-permute-start.9 = (bf16[40,1536]{1,0:T(8,128)(2,1)S(1)}, bf16[40,1536]{1,0:T(8,128)(2,1)S(1)}, u32[]{:S(2)}, u32[]{:S(2)}) collective-permute-start(bf16[40,1536]{1,0:T(8,128)(2,1)S(1)} %get-tuple-element.72.refs_0_), channel_id=1, source_target_pairs={{0,16},{4,20},{8,24},{12,28},{16,0},{20,4},{24,8},{28,12},{1,17},{... | collective-permute-start | bytes 368648 | tf_op jit(solution)/shard_map/ppermute | solution.py:410
  21.9 2.8 %collective-permute-done.2.refs_1_ = bf16[80,1536]{1,0:T(8,128)(2,1)S(1)} collective-permute-done((bf16[80,1536]{1,0:T(8,128)(2,1)S(1)}, bf16[80,1536]{1,0:T(8,128)(2,1)S(1)}, u32[]{:S(2)}, u32[]{:S(2)}) %collective-permute-start.2) | collective-permute-done | bytes 245792 | tf_op jit(solution)/shard_map/ppermute | solution.py:410
  24.8 3.0 %collective-permute-start.7 = (bf16[160,1536]{1,0:T(8,128)(2,1)S(1)}, bf16[160,1536]{1,0:T(8,128)(2,1)S(1)}, u32[]{:S(2)}, u32[]{:S(2)}) collective-permute-start(bf16[160,1536]{1,0:T(8,128)(2,1)S(1)} %join.10.refs_1_.refs_4_), channel_id=1, source_target_pairs={{0,4},{4,0},{8,12},{12,8},{16,20},{20,16},{24,28},{28,24},{1,5},{5... | collective-permute-start | bytes 1474568 | tf_op jit(solution)/shard_map/ppermute | solution.py:410
  29.2 1.5 collective-permute-done.3.refs_1_
  30.8 1.6 %collective-permute-start.5 = (bf16[2,160,512]{2,1,0:T(8,128)(2,1)S(1)}, bf16[2,160,512]{2,1,0:T(8,128)(2,1)S(1)}, u32[]{:S(2)}, u32[]{:S(2)}) collective-permute-start(bf16[2,160,512]{2,1,0:T(8,128)(2,1)S(1)} %add.11.refs_4_), channel_id=1, source_target_pairs={{0,2},{1,3},{2,0},{3,1},{4,6},{5,7},{6,4},{7,5},{8,10},{9,11},{10,... | collective-permute-start | bytes 983048 | tf_op jit(solution)/shard_map/ppermute | solution.py:417
  37.3 10.8 %collective-permute-done.11.refs_1_ = bf16[80,1536]{1,0:T(8,128)(2,1)S(1)} collective-permute-done((bf16[80,1536]{1,0:T(8,128)(2,1)S(1)}, bf16[80,1536]{1,0:T(8,128)(2,1)S(1)}, u32[]{:S(2)}, u32[]{:S(2)}) %collective-permute-start.11) | collective-permute-done | bytes 245792 | tf_op jit(solution)/shard_map/ppermute | solution.py:410
  48.3 1.6 %collective-permute-start.12 = (bf16[2,160,512]{2,1,0:T(8,128)(2,1)S(1)}, bf16[2,160,512]{2,1,0:T(8,128)(2,1)S(1)}, u32[]{:S(2)}, u32[]{:S(2)}) collective-permute-start(bf16[2,160,512]{2,1,0:T(8,128)(2,1)S(1)} %add.13.refs_4_), channel_id=1, source_target_pairs={{0,2},{1,3},{2,0},{3,1},{4,6},{5,7},{6,4},{7,5},{8,10},{9,11},{10,... | collective-permute-start | bytes 983048 | tf_op jit(solution)/shard_map/ppermute | solution.py:417
  53.5 7.2 %collective-permute-done.13.refs_1_ = bf16[40,1536]{1,0:T(8,128)(2,1)S(1)} collective-permute-done((bf16[40,1536]{1,0:T(8,128)(2,1)S(1)}, bf16[40,1536]{1,0:T(8,128)(2,1)S(1)}, u32[]{:S(2)}, u32[]{:S(2)}) %collective-permute-start.13) | collective-permute-done | bytes 122912 | tf_op jit(solution)/shard_map/ppermute | solution.py:410
  60.9 7.8 %collective-permute-done.15.refs_1_ = bf16[80,1536]{1,0:T(8,128)(2,1)S(1)} collective-permute-done((bf16[80,1536]{1,0:T(8,128)(2,1)S(1)}, bf16[80,1536]{1,0:T(8,128)(2,1)S(1)}, u32[]{:S(2)}, u32[]{:S(2)}) %collective-permute-start.15) | collective-permute-done | bytes 245792 | tf_op jit(solution)/shard_map/ppermute | solution.py:410
  68.8 2.1 %collective-permute-start.22 = (bf16[160,1536]{1,0:T(8,128)(2,1)S(1)}, bf16[160,1536]{1,0:T(8,128)(2,1)S(1)}, u32[]{:S(2)}, u32[]{:S(2)}) collective-permute-start(bf16[160,1536]{1,0:T(8,128)(2,1)S(1)} %join.15.refs_4_.refs_1_), channel_id=1, source_target_pairs={{0,4},{4,0},{8,12},{12,8},{16,20},{20,16},{24,28},{28,24},{1,5},{5... | collective-permute-start | bytes 1474568 | tf_op jit(solution)/shard_map/ppermute | solution.py:410
  75.5 2.0 %collective-permute-start.19 = (bf16[160,1536]{1,0:T(8,128)(2,1)S(1)}, bf16[160,1536]{1,0:T(8,128)(2,1)S(1)}, u32[]{:S(2)}, u32[]{:S(2)}) collective-permute-start(bf16[160,1536]{1,0:T(8,128)(2,1)S(1)} %get-tuple-element.84), channel_id=1, source_target_pairs={{0,4},{4,0},{8,12},{12,8},{16,20},{20,16},{24,28},{28,24},{1,5},{5... | collective-permute-start | bytes 1474568 | tf_op jit(solution)/shard_map/ppermute | solution.py:410
  77.6 5.4 %collective-permute-done.22.refs_2_ = bf16[160,1536]{1,0:T(8,128)(2,1)S(1)} collective-permute-done((bf16[160,1536]{1,0:T(8,128)(2,1)S(1)}, bf16[160,1536]{1,0:T(8,128)(2,1)S(1)}, u32[]{:S(2)}, u32[]{:S(2)}) %collective-permute-start.22) | collective-permute-done | bytes 491552 | tf_op jit(solution)/shard_map/ppermute | solution.py:410
  85.5 2.1 %collective-permute-start.30 = (bf16[160,1536]{1,0:T(8,128)(2,1)S(1)}, bf16[160,1536]{1,0:T(8,128)(2,1)S(1)}, u32[]{:S(2)}, u32[]{:S(2)}) collective-permute-start(bf16[160,1536]{1,0:T(8,128)(2,1)S(1)} %get-tuple-element.100), channel_id=1, source_target_pairs={{0,4},{4,0},{8,12},{12,8},{16,20},{20,16},{24,28},{28,24},{1,5},{5... | collective-permute-start | bytes 1474568 | tf_op jit(solution)/shard_map/ppermute | solution.py:410
  88.7 3.6 %weight_grad.6 = (f32[2,1024,1536]{2,1,0:T(8,128)}, f32[8,128]{1,0:T(8,128)S(1)}) custom-call(s32[1]{0:T(128)} %bitcast.2.refs_0_, bf16[160,1536]{1,0:T(8,128)(2,1)S(1)} %join.13.refs_2_.refs_1_, bf16[160,1536]{1,0:T(8,128)(2,1)S(1)} %collective-permute-done.18.refs_2_, bf16[1,320,512]{2,1,0:T(8,128)(2,1)S(1)} %get-tuple-element.81.refs_4_.refs_1_.refs_3_, ...), custom_call_target="tpu_custom_call" | custom-call | flops 10000000000 | bytes 100000000 | tf_op jit(solution)/shard_map/weight_grad/pallas_call | solution.py:48
  95.0 2.2 %row_grad_part.2 = (bf16[160,1536]{1,0:T(8,128)(2,1)S(1)}, bf16[160,1536]{1,0:T(8,128)(2,1)S(1)}) custom-call(s32[1]{0:T(128)} %bitcast.2.refs_0_, bf16[2,320,512]{2,1,0:T(8,128)(2,1)S(1)} %gate_up_grads.2.refs_5_.refs_1_.refs_3_, bf16[2,320,512]{2,1,0:T(8,128)(2,1)S(1)} %collective-permute-done.26.refs_2_.refs_4_, bf16[2,1536,1024]{2,1,0:T(8,128)(2,1)S(1)} %bitcast.8, ...), custom_call_target="tpu_custom_call" | custom-call | flops 10000000000 | bytes 100000000 | tf_op jit(solution)/shard_map/row_grad_part/pallas_call | solution.py:48
  98.8 3.2 %weight_grad.7 = (f32[2,1024,1536]{2,1,0:T(8,128)}, f32[8,128]{1,0:T(8,128)S(1)}) custom-call(s32[1]{0:T(128)} %bitcast.2.refs_0_, bf16[160,1536]{1,0:T(8,128)(2,1)S(1)} %join.15.refs_4_.refs_1_, bf16[160,1536]{1,0:T(8,128)(2,1)S(1)} %collective-permute-done.22.refs_2_, ...), custom_call_target="tpu_custom_call", output_to_operand_aliasing={{0}: (5, {})} | custom-call | flops 10000000000 | bytes 100000000 | tf_op jit(solution)/shard_map/weight_grad/pallas_call | solution.py:48
  102.0 2.2 %row_grad_part.3 = (bf16[160,1536]{1,0:T(8,128)(2,1)S(1)}, bf16[160,1536]{1,0:T(8,128)(2,1)S(1)}) custom-call(s32[1]{0:T(128)} %bitcast.2.refs_0_, bf16[2,320,512]{2,1,0:T(8,128)(2,1)S(1)} %gate_up_grads.3.refs_6_.refs_1_.refs_3_, bf16[2,320,512]{2,1,0:T(8,128)(2,1)S(1)} %collective-permute-done.29.refs_2_.refs_4_, bf16[2,1536,1024]{2,1,0:T(8,128)(2,1)S(1)} %bitcast.8, ...), custom_call_target="tpu_custom_call" | custom-call | flops 10000000000 | bytes 100000000 | tf_op jit(solution)/shard_map/row_grad_part/pallas_call | solution.py:48
  106.3 1.6 %collective-permute-start.31 = (bf16[80,1536]{1,0:T(8,128)(2,1)S(1)}, bf16[80,1536]{1,0:T(8,128)(2,1)S(1)}, u32[]{:S(2)}, u32[]{:S(2)}) collective-permute-start(bf16[80,1536]{1,0:T(8,128)(2,1)S(1)} %get-tuple-element.102), channel_id=1, source_target_pairs={{0,8},{4,12},{8,0},{12,4},{16,24},{20,28},{24,16},{28,20},{1,9},{5... | collective-permute-start | bytes 737288 | tf_op jit(solution)/shard_map/ppermute | solution.py:410
  108.4 3.2 %weight_grad.8 = (f32[2,1536,1024]{2,1,0:T(8,128)}, f32[8,128]{1,0:T(8,128)S(1)}) custom-call(s32[1]{0:T(128)} %bitcast.2.refs_0_, bf16[160,1536]{1,0:T(8,128)(2,1)S(1)} %copy-done.5, bf16[160,1536]{1,0:T(8,128)(2,1)S(1)} %copy-done.7, bf16[2,320,512]{2,1,0:T(8,128)(2,1)S(1)} %gate_up_grads.2.refs_5_.refs_1_.refs_3_, ...), custom_call_target="tpu_custom_call" | custom-call | flops 10000000000 | bytes 100000000 | tf_op jit(solution)/shard_map/weight_grad/pallas_call | solution.py:48
  111.6 15.3 %collective-permute-done.33.refs_1_ = bf16[160,1536]{1,0:T(8,128)(2,1)S(1)} collective-permute-done((bf16[160,1536]{1,0:T(8,128)(2,1)S(1)}, bf16[160,1536]{1,0:T(8,128)(2,1)S(1)}, u32[]{:S(2)}, u32[]{:S(2)}) %collective-permute-start.33) | collective-permute-done | bytes 491552 | tf_op jit(solution)/shard_map/ppermute | solution.py:410
  128.0 1.7 %collective-permute-start.37 = (bf16[80,1536]{1,0:T(8,128)(2,1)S(1)}, bf16[80,1536]{1,0:T(8,128)(2,1)S(1)}, u32[]{:S(2)}, u32[]{:S(2)}) collective-permute-start(bf16[80,1536]{1,0:T(8,128)(2,1)S(1)} %get-tuple-element.115), channel_id=1, source_target_pairs={{0,4},{4,0},{8,12},{12,8},{16,20},{20,16},{24,28},{28,24},{1,5},{5... | collective-permute-start | bytes 737288 | tf_op jit(solution)/shard_map/ppermute | solution.py:410
  129.7 3.2 %weight_grad.9 = (f32[2,1536,1024]{2,1,0:T(8,128)}, f32[8,128]{1,0:T(8,128)S(1)}) custom-call(s32[1]{0:T(128)} %bitcast.2.refs_0_, bf16[160,1536]{1,0:T(8,128)(2,1)S(1)} %copy-done.5, bf16[160,1536]{1,0:T(8,128)(2,1)S(1)} %copy-done.7, bf16[2,320,512]{2,1,0:T(8,128)(2,1)S(1)} %gate_up_grads.2.refs_5_.refs_1_.refs_3_, ...), custom_call_target="tpu_custom_call" | custom-call | flops 10000000000 | bytes 100000000 | tf_op jit(solution)/shard_map/weight_grad/pallas_call | solution.py:48
  133.0 1.6 %collective-permute-start.35 = (bf16[40,1536]{1,0:T(8,128)(2,1)S(1)}, bf16[40,1536]{1,0:T(8,128)(2,1)S(1)}, u32[]{:S(2)}, u32[]{:S(2)}) collective-permute-start(bf16[40,1536]{1,0:T(8,128)(2,1)S(1)} %get-tuple-element.111), channel_id=1, source_target_pairs={{0,16},{4,20},{8,24},{12,28},{16,0},{20,4},{24,8},{28,12},{1,17},{... | collective-permute-start | bytes 368648 | tf_op jit(solution)/shard_map/ppermute | solution.py:410
  136.5 3.4 %weight_grad.10 = (f32[2,1536,1024]{2,1,0:T(8,128)}, f32[8,128]{1,0:T(8,128)S(1)}) custom-call(s32[1]{0:T(128)} %bitcast.2.refs_0_, bf16[160,1536]{1,0:T(8,128)(2,1)S(1)} %copy-done.1, bf16[160,1536]{1,0:T(8,128)(2,1)S(1)} %copy-done.3, bf16[2,320,512]{2,1,0:T(8,128)(2,1)S(1)} %gate_up_grads.3.refs_6_.refs_1_.refs_3_, ...), custom_call_target="tpu_custom_call", output_to_operand_aliasing={{0}: (5, {})} | custom-call | flops 10000000000 | bytes 100000000 | tf_op jit(solution)/shard_map/weight_grad/pallas_call | solution.py:48
  141.2 1.8 %collective-permute-start.39 = (bf16[40,1536]{1,0:T(8,128)(2,1)S(1)}, bf16[40,1536]{1,0:T(8,128)(2,1)S(1)}, u32[]{:S(2)}, u32[]{:S(2)}) collective-permute-start(bf16[40,1536]{1,0:T(8,128)(2,1)S(1)} %get-tuple-element.121), channel_id=1, source_target_pairs={{0,16},{4,20},{8,24},{12,28},{16,0},{20,4},{24,8},{28,12},{1,17},{... | collective-permute-start | bytes 368648 | tf_op jit(solution)/shard_map/ppermute | solution.py:410
  143.0 3.2 %weight_grad.11 = (f32[2,1536,1024]{2,1,0:T(8,128)}, f32[8,128]{1,0:T(8,128)S(1)}) custom-call(s32[1]{0:T(128)} %bitcast.2.refs_0_, bf16[160,1536]{1,0:T(8,128)(2,1)S(1)} %copy-done.1, bf16[160,1536]{1,0:T(8,128)(2,1)S(1)} %copy-done.3, bf16[2,320,512]{2,1,0:T(8,128)(2,1)S(1)} %gate_up_grads.3.refs_6_.refs_1_.refs_3_, ...), custom_call_target="tpu_custom_call", output_to_operand_aliasing={{0}: (5, {})} | custom-call | flops 10000000000 | bytes 100000000 | tf_op jit(solution)/shard_map/weight_grad/pallas_call | solution.py:48
  147.4 3.1 %collective-permute-done.38.refs_6_ = bf16[40,1536]{1,0:T(8,128)(2,1)S(1)} collective-permute-done((bf16[40,1536]{1,0:T(8,128)(2,1)S(1)}, bf16[40,1536]{1,0:T(8,128)(2,1)S(1)}, u32[]{:S(2)}, u32[]{:S(2)}) %collective-permute-start.38) | collective-permute-done | bytes 122912 | tf_op jit(solution)/shard_map/ppermute | solution.py:410
  150.5 2.1 %collective-permute-done.39.refs_7_ = bf16[40,1536]{1,0:T(8,128)(2,1)S(1)} collective-permute-done((bf16[40,1536]{1,0:T(8,128)(2,1)S(1)}, bf16[40,1536]{1,0:T(8,128)(2,1)S(1)}, u32[]{:S(2)}, u32[]{:S(2)}) %collective-permute-start.39) | collective-permute-done | bytes 122912 | tf_op jit(solution)/shard_map/ppermute | solution.py:410
  (158 shorter events, 36.0 us)
Async XLA Ops:
  2.8 13.5 %collective-permute-start.1 = (bf16[40,1536]{1,0:T(8,128)(2,1)S(1)}, bf16[40,1536]{1,0:T(8,128)(2,1)S(1)}, u32[]{:S(2)}, u32[]{:S(2)}) collective-permute-start(bf16[40,1536]{1,0:T(8,128)(2,1)S(1)} %get-tuple-element.66.refs_0_.refs_2_), channel_id=1, source_target_pairs={{0,16},{4,20},{8,24},{12,28},{16,0},{20,4},{24,8},{28,12},{1,17},{... | collective-permute-start | bytes 368648 | tf_op jit(solution)/shard_map/ppermute | solution.py:410
  6.9 11.3 %collective-permute-start = (bf16[40,1536]{1,0:T(8,128)(2,1)S(1)}, bf16[40,1536]{1,0:T(8,128)(2,1)S(1)}, u32[]{:S(2)}, u32[]{:S(2)}) collective-permute-start(bf16[40,1536]{1,0:T(8,128)(2,1)S(1)} %get-tuple-element.65.refs_0_), channel_id=1, source_target_pairs={{0,16},{4,20},{8,24},{12,28},{16,0},{20,4},{24,8},{28,12},{1,17},{... | collective-permute-start | bytes 368648 | tf_op jit(solution)/shard_map/ppermute | solution.py:410
  16.4 8.3 %collective-permute-start.2 = (bf16[80,1536]{1,0:T(8,128)(2,1)S(1)}, bf16[80,1536]{1,0:T(8,128)(2,1)S(1)}, u32[]{:S(2)}, u32[]{:S(2)}) collective-permute-start(bf16[80,1536]{1,0:T(8,128)(2,1)S(1)} %join.8.refs_2_.refs_0_), channel_id=1, source_target_pairs={{0,8},{4,12},{8,0},{12,4},{16,24},{20,28},{24,16},{28,20},{1,9},{5... | collective-permute-start | bytes 737288 | tf_op jit(solution)/shard_map/ppermute | solution.py:410
  18.2 10.9 %collective-permute-start.4 = (bf16[80,1536]{1,0:T(8,128)(2,1)S(1)}, bf16[80,1536]{1,0:T(8,128)(2,1)S(1)}, u32[]{:S(2)}, u32[]{:S(2)}) collective-permute-start(bf16[80,1536]{1,0:T(8,128)(2,1)S(1)} %join.9.refs_3_.refs_0_), channel_id=1, source_target_pairs={{0,4},{4,0},{8,12},{12,8},{16,20},{20,16},{24,28},{28,24},{1,5},{5... | collective-permute-start | bytes 737288 | tf_op jit(solution)/shard_map/ppermute | solution.py:410
  20.3 13.4 %collective-permute-start.9 = (bf16[40,1536]{1,0:T(8,128)(2,1)S(1)}, bf16[40,1536]{1,0:T(8,128)(2,1)S(1)}, u32[]{:S(2)}, u32[]{:S(2)}) collective-permute-start(bf16[40,1536]{1,0:T(8,128)(2,1)S(1)} %get-tuple-element.72.refs_0_), channel_id=1, source_target_pairs={{0,16},{4,20},{8,24},{12,28},{16,0},{20,4},{24,8},{28,12},{1,17},{... | collective-permute-start | bytes 368648 | tf_op jit(solution)/shard_map/ppermute | solution.py:410
  24.8 11.2 %collective-permute-start.7 = (bf16[160,1536]{1,0:T(8,128)(2,1)S(1)}, bf16[160,1536]{1,0:T(8,128)(2,1)S(1)}, u32[]{:S(2)}, u32[]{:S(2)}) collective-permute-start(bf16[160,1536]{1,0:T(8,128)(2,1)S(1)} %join.10.refs_1_.refs_4_), channel_id=1, source_target_pairs={{0,4},{4,0},{8,12},{12,8},{16,20},{20,16},{24,28},{28,24},{1,5},{5... | collective-permute-start | bytes 1474568 | tf_op jit(solution)/shard_map/ppermute | solution.py:410
  29.1 20.7 %collective-permute-start.6 = (bf16[160,1536]{1,0:T(8,128)(2,1)S(1)}, bf16[160,1536]{1,0:T(8,128)(2,1)S(1)}, u32[]{:S(2)}, u32[]{:S(2)}) collective-permute-start(bf16[160,1536]{1,0:T(8,128)(2,1)S(1)} %join.11.refs_2_.refs_1_), channel_id=1, source_target_pairs={{0,8},{4,12},{8,0},{12,4},{16,24},{20,28},{24,16},{28,20},{1,9},{5... | collective-permute-start | bytes 1474568 | tf_op jit(solution)/shard_map/ppermute | solution.py:410
  30.8 20.4 %collective-permute-start.5 = (bf16[2,160,512]{2,1,0:T(8,128)(2,1)S(1)}, bf16[2,160,512]{2,1,0:T(8,128)(2,1)S(1)}, u32[]{:S(2)}, u32[]{:S(2)}) collective-permute-start(bf16[2,160,512]{2,1,0:T(8,128)(2,1)S(1)} %add.11.refs_4_), channel_id=1, source_target_pairs={{0,2},{1,3},{2,0},{3,1},{4,6},{5,7},{6,4},{7,5},{8,10},{9,11},{10,... | collective-permute-start | bytes 983048 | tf_op jit(solution)/shard_map/ppermute | solution.py:417
  33.7 14.4 %collective-permute-start.11 = (bf16[80,1536]{1,0:T(8,128)(2,1)S(1)}, bf16[80,1536]{1,0:T(8,128)(2,1)S(1)}, u32[]{:S(2)}, u32[]{:S(2)}) collective-permute-start(bf16[80,1536]{1,0:T(8,128)(2,1)S(1)} %join.12.refs_2_.refs_0_), channel_id=1, source_target_pairs={{0,8},{4,12},{8,0},{12,4},{16,24},{20,28},{24,16},{28,20},{1,9},{5... | collective-permute-start | bytes 737288 | tf_op jit(solution)/shard_map/ppermute | solution.py:410
  35.3 25.5 %collective-permute-start.16 = (bf16[2,160,512]{2,1,0:T(8,128)(2,1)S(1)}, bf16[2,160,512]{2,1,0:T(8,128)(2,1)S(1)}, u32[]{:S(2)}, u32[]{:S(2)}) collective-permute-start(bf16[2,160,512]{2,1,0:T(8,128)(2,1)S(1)} %add.12.refs_4_), channel_id=1, source_target_pairs={{0,2},{1,3},{2,0},{3,1},{4,6},{5,7},{6,4},{7,5},{8,10},{9,11},{10,... | collective-permute-start | bytes 983048 | tf_op jit(solution)/shard_map/ppermute | solution.py:417
  37.2 11.0 %collective-permute-start.10 = (bf16[2,160,512]{2,1,0:T(8,128)(2,1)S(1)}, bf16[2,160,512]{2,1,0:T(8,128)(2,1)S(1)}, u32[]{:S(2)}, u32[]{:S(2)}) collective-permute-start(bf16[2,160,512]{2,1,0:T(8,128)(2,1)S(1)} %get-tuple-element.74), channel_id=1, source_target_pairs={{0,1},{1,0},{2,3},{3,2},{4,5},{5,4},{6,7},{7,6},{8,9},{9,8},{10,11... | collective-permute-start | bytes 983048 | tf_op jit(solution)/shard_map/ppermute | solution.py:413
  48.1 23.1 %collective-permute-start.18 = (bf16[160,1536]{1,0:T(8,128)(2,1)S(1)}, bf16[160,1536]{1,0:T(8,128)(2,1)S(1)}, u32[]{:S(2)}, u32[]{:S(2)}) collective-permute-start(bf16[160,1536]{1,0:T(8,128)(2,1)S(1)} %join.13.refs_2_.refs_1_), channel_id=1, source_target_pairs={{0,4},{4,0},{8,12},{12,8},{16,20},{20,16},{24,28},{28,24},{1,5},{5... | collective-permute-start | bytes 1474568 | tf_op jit(solution)/shard_map/ppermute | solution.py:410
  48.3 22.5 %collective-permute-start.12 = (bf16[2,160,512]{2,1,0:T(8,128)(2,1)S(1)}, bf16[2,160,512]{2,1,0:T(8,128)(2,1)S(1)}, u32[]{:S(2)}, u32[]{:S(2)}) collective-permute-start(bf16[2,160,512]{2,1,0:T(8,128)(2,1)S(1)} %add.13.refs_4_), channel_id=1, source_target_pairs={{0,2},{1,3},{2,0},{3,1},{4,6},{5,7},{6,4},{7,5},{8,10},{9,11},{10,... | collective-permute-start | bytes 983048 | tf_op jit(solution)/shard_map/ppermute | solution.py:417
  51.7 9.0 %collective-permute-start.13 = (bf16[40,1536]{1,0:T(8,128)(2,1)S(1)}, bf16[40,1536]{1,0:T(8,128)(2,1)S(1)}, u32[]{:S(2)}, u32[]{:S(2)}) collective-permute-start(bf16[40,1536]{1,0:T(8,128)(2,1)S(1)} %get-tuple-element.79.refs_0_), channel_id=1, source_target_pairs={{0,16},{4,20},{8,24},{12,28},{16,0},{20,4},{24,8},{28,12},{1,17},{... | collective-permute-start | bytes 368648 | tf_op jit(solution)/shard_map/ppermute | solution.py:410
  52.9 22.3 %collective-permute-start.23 = (bf16[2,160,512]{2,1,0:T(8,128)(2,1)S(1)}, bf16[2,160,512]{2,1,0:T(8,128)(2,1)S(1)}, u32[]{:S(2)}, u32[]{:S(2)}) collective-permute-start(bf16[2,160,512]{2,1,0:T(8,128)(2,1)S(1)} %add.14.refs_2_), channel_id=1, source_target_pairs={{0,2},{1,3},{2,0},{3,1},{4,6},{5,7},{6,4},{7,5},{8,10},{9,11},{10,... | collective-permute-start | bytes 983048 | tf_op jit(solution)/shard_map/ppermute | solution.py:417
  60.7 8.0 %collective-permute-start.15 = (bf16[80,1536]{1,0:T(8,128)(2,1)S(1)}, bf16[80,1536]{1,0:T(8,128)(2,1)S(1)}, u32[]{:S(2)}, u32[]{:S(2)}) collective-permute-start(bf16[80,1536]{1,0:T(8,128)(2,1)S(1)} %join.14.refs_3_.refs_0_), channel_id=1, source_target_pairs={{0,8},{4,12},{8,0},{12,4},{16,24},{20,28},{24,16},{28,20},{1,9},{5... | collective-permute-start | bytes 737288 | tf_op jit(solution)/shard_map/ppermute | solution.py:410
  68.8 14.2 %collective-permute-start.22 = (bf16[160,1536]{1,0:T(8,128)(2,1)S(1)}, bf16[160,1536]{1,0:T(8,128)(2,1)S(1)}, u32[]{:S(2)}, u32[]{:S(2)}) collective-permute-start(bf16[160,1536]{1,0:T(8,128)(2,1)S(1)} %join.15.refs_4_.refs_1_), channel_id=1, source_target_pairs={{0,4},{4,0},{8,12},{12,8},{16,20},{20,16},{24,28},{28,24},{1,5},{5... | collective-permute-start | bytes 1474568 | tf_op jit(solution)/shard_map/ppermute | solution.py:410
  74.6 13.4 %collective-permute-start.21 = (bf16[1,320,512]{2,1,0:T(8,128)(2,1)S(1)}, bf16[1,320,512]{2,1,0:T(8,128)(2,1)S(1)}, u32[]{:S(2)}, u32[]{:S(2)}) collective-permute-start(bf16[1,320,512]{2,1,0:T(8,128)(2,1)S(1)} %add.15.refs_4_), channel_id=1, source_target_pairs={{0,2},{1,3},{2,0},{3,1},{4,6},{5,7},{6,4},{7,5},{8,10},{9,11},{10,... | collective-permute-start | bytes 983048 | tf_op jit(solution)/shard_map/ppermute | solution.py:417
  75.5 8.8 %collective-permute-start.25 = (bf16[1,320,512]{2,1,0:T(8,128)(2,1)S(1)}, bf16[1,320,512]{2,1,0:T(8,128)(2,1)S(1)}, u32[]{:S(2)}, u32[]{:S(2)}) collective-permute-start(bf16[1,320,512]{2,1,0:T(8,128)(2,1)S(1)} %get-tuple-element.87.refs_4_.refs_1_.refs_3_), channel_id=1, source_target_pairs={{0,1},{1,0},{2,3},{3,2},{4,5},{5,4},{6,7},{7,6},{8,9},{9,8},{10,11... | collective-permute-start | bytes 983048 | tf_op jit(solution)/shard_map/ppermute | solution.py:413
  75.5 21.7 %collective-permute-start.19 = (bf16[160,1536]{1,0:T(8,128)(2,1)S(1)}, bf16[160,1536]{1,0:T(8,128)(2,1)S(1)}, u32[]{:S(2)}, u32[]{:S(2)}) collective-permute-start(bf16[160,1536]{1,0:T(8,128)(2,1)S(1)} %get-tuple-element.84), channel_id=1, source_target_pairs={{0,4},{4,0},{8,12},{12,8},{16,20},{20,16},{24,28},{28,24},{1,5},{5... | collective-permute-start | bytes 1474568 | tf_op jit(solution)/shard_map/ppermute | solution.py:410
  85.5 20.7 %collective-permute-start.30 = (bf16[160,1536]{1,0:T(8,128)(2,1)S(1)}, bf16[160,1536]{1,0:T(8,128)(2,1)S(1)}, u32[]{:S(2)}, u32[]{:S(2)}) collective-permute-start(bf16[160,1536]{1,0:T(8,128)(2,1)S(1)} %get-tuple-element.100), channel_id=1, source_target_pairs={{0,4},{4,0},{8,12},{12,8},{16,20},{20,16},{24,28},{28,24},{1,5},{5... | collective-permute-start | bytes 1474568 | tf_op jit(solution)/shard_map/ppermute | solution.py:410
  87.6 10.7 %collective-permute-start.28 = (bf16[1,320,512]{2,1,0:T(8,128)(2,1)S(1)}, bf16[1,320,512]{2,1,0:T(8,128)(2,1)S(1)}, u32[]{:S(2)}, u32[]{:S(2)}) collective-permute-start(bf16[1,320,512]{2,1,0:T(8,128)(2,1)S(1)} %add.16.refs_4_), channel_id=1, source_target_pairs={{0,2},{1,3},{2,0},{3,1},{4,6},{5,7},{6,4},{7,5},{8,10},{9,11},{10,... | collective-permute-start | bytes 983048 | tf_op jit(solution)/shard_map/ppermute | solution.py:417
  97.3 7.9 %collective-permute-start.27 = (bf16[80,1536]{1,0:T(8,128)(2,1)S(1)}, bf16[80,1536]{1,0:T(8,128)(2,1)S(1)}, u32[]{:S(2)}, u32[]{:S(2)}) collective-permute-start(bf16[80,1536]{1,0:T(8,128)(2,1)S(1)} %get-tuple-element.94), channel_id=1, source_target_pairs={{0,8},{4,12},{8,0},{12,4},{16,24},{20,28},{24,16},{28,20},{1,9},{5... | collective-permute-start | bytes 737288 | tf_op jit(solution)/shard_map/ppermute | solution.py:410
  98.0 29.0 %collective-permute-start.32 = (bf16[160,1536]{1,0:T(8,128)(2,1)S(1)}, bf16[160,1536]{1,0:T(8,128)(2,1)S(1)}, u32[]{:S(2)}, u32[]{:S(2)}) collective-permute-start(bf16[160,1536]{1,0:T(8,128)(2,1)S(1)} %get-tuple-element.103), channel_id=1, source_target_pairs={{0,4},{4,0},{8,12},{12,8},{16,20},{20,16},{24,28},{28,24},{1,5},{5... | collective-permute-start | bytes 1474568 | tf_op jit(solution)/shard_map/ppermute | solution.py:410
  105.3 40.8 %collective-permute-start.34 = (bf16[40,1536]{1,0:T(8,128)(2,1)S(1)}, bf16[40,1536]{1,0:T(8,128)(2,1)S(1)}, u32[]{:S(2)}, u32[]{:S(2)}) collective-permute-start(bf16[40,1536]{1,0:T(8,128)(2,1)S(1)} %get-tuple-element.110), channel_id=1, source_target_pairs={{0,16},{4,20},{8,24},{12,28},{16,0},{20,4},{24,8},{28,12},{1,17},{... | collective-permute-start | bytes 368648 | tf_op jit(solution)/shard_map/ppermute | solution.py:410
  106.3 26.6 %collective-permute-start.31 = (bf16[80,1536]{1,0:T(8,128)(2,1)S(1)}, bf16[80,1536]{1,0:T(8,128)(2,1)S(1)}, u32[]{:S(2)}, u32[]{:S(2)}) collective-permute-start(bf16[80,1536]{1,0:T(8,128)(2,1)S(1)} %get-tuple-element.102), channel_id=1, source_target_pairs={{0,8},{4,12},{8,0},{12,4},{16,24},{20,28},{24,16},{28,20},{1,9},{5... | collective-permute-start | bytes 737288 | tf_op jit(solution)/shard_map/ppermute | solution.py:410
  107.9 18.9 %collective-permute-start.33 = (bf16[160,1536]{1,0:T(8,128)(2,1)S(1)}, bf16[160,1536]{1,0:T(8,128)(2,1)S(1)}, u32[]{:S(2)}, u32[]{:S(2)}) collective-permute-start(bf16[160,1536]{1,0:T(8,128)(2,1)S(1)} %get-tuple-element.104), channel_id=1, source_target_pairs={{0,8},{4,12},{8,0},{12,4},{16,24},{20,28},{24,16},{28,20},{1,9},{5... | collective-permute-start | bytes 1474568 | tf_op jit(solution)/shard_map/ppermute | solution.py:410
  127.1 12.8 %collective-permute-start.36 = (bf16[80,1536]{1,0:T(8,128)(2,1)S(1)}, bf16[80,1536]{1,0:T(8,128)(2,1)S(1)}, u32[]{:S(2)}, u32[]{:S(2)}) collective-permute-start(bf16[80,1536]{1,0:T(8,128)(2,1)S(1)} %get-tuple-element.113), channel_id=1, source_target_pairs={{0,8},{4,12},{8,0},{12,4},{16,24},{20,28},{24,16},{28,20},{1,9},{5... | collective-permute-start | bytes 737288 | tf_op jit(solution)/shard_map/ppermute | solution.py:410
  128.0 7.3 %collective-permute-start.37 = (bf16[80,1536]{1,0:T(8,128)(2,1)S(1)}, bf16[80,1536]{1,0:T(8,128)(2,1)S(1)}, u32[]{:S(2)}, u32[]{:S(2)}) collective-permute-start(bf16[80,1536]{1,0:T(8,128)(2,1)S(1)} %get-tuple-element.115), channel_id=1, source_target_pairs={{0,4},{4,0},{8,12},{12,8},{16,20},{20,16},{24,28},{28,24},{1,5},{5... | collective-permute-start | bytes 737288 | tf_op jit(solution)/shard_map/ppermute | solution.py:410
  133.0 13.2 %collective-permute-start.35 = (bf16[40,1536]{1,0:T(8,128)(2,1)S(1)}, bf16[40,1536]{1,0:T(8,128)(2,1)S(1)}, u32[]{:S(2)}, u32[]{:S(2)}) collective-permute-start(bf16[40,1536]{1,0:T(8,128)(2,1)S(1)} %get-tuple-element.111), channel_id=1, source_target_pairs={{0,16},{4,20},{8,24},{12,28},{16,0},{20,4},{24,8},{28,12},{1,17},{... | collective-permute-start | bytes 368648 | tf_op jit(solution)/shard_map/ppermute | solution.py:410
  140.0 10.5 %collective-permute-start.38 = (bf16[40,1536]{1,0:T(8,128)(2,1)S(1)}, bf16[40,1536]{1,0:T(8,128)(2,1)S(1)}, u32[]{:S(2)}, u32[]{:S(2)}) collective-permute-start(bf16[40,1536]{1,0:T(8,128)(2,1)S(1)} %get-tuple-element.120), channel_id=1, source_target_pairs={{0,16},{4,20},{8,24},{12,28},{16,0},{20,4},{24,8},{28,12},{1,17},{... | collective-permute-start | bytes 368648 | tf_op jit(solution)/shard_map/ppermute | solution.py:410
  141.2 11.4 %collective-permute-start.39 = (bf16[40,1536]{1,0:T(8,128)(2,1)S(1)}, bf16[40,1536]{1,0:T(8,128)(2,1)S(1)}, u32[]{:S(2)}, u32[]{:S(2)}) collective-permute-start(bf16[40,1536]{1,0:T(8,128)(2,1)S(1)} %get-tuple-element.121), channel_id=1, source_target_pairs={{0,16},{4,20},{8,24},{12,28},{16,0},{20,4},{24,8},{28,12},{1,17},{... | collective-permute-start | bytes 368648 | tf_op jit(solution)/shard_map/ppermute | solution.py:410
  (36 other events, 119.2 us)

commit v3 on v2

--- a/solution.py
+++ b/solution.py
@@ -73,19 +73,17 @@
     return chosen, jnp.where(match, 1.0, 0.0)
 
 
-def rows_kernel(experts, ids, tokens, *outs):
-    for e in range(experts):
-        _, match = match_of(ids, e)
-        outs[e][...] = mm(match.astype(BF), tokens[...]).astype(BF)
-
-
-def rows_of(run, ids, tokens, experts):
-    n, d = tokens.shape
-    return run(
-        functools.partial(rows_kernel, experts),
+def rows_kernel(expert, ids, tokens, out):
+    _, match = match_of(ids, expert)
+    out[...] = mm(match.astype(BF), tokens[...]).astype(BF)
+
+
+def rows_of(run, ids, tokens, expert):
+    return run(
+        functools.partial(rows_kernel, expert),
         ids,
         tokens,
-        out_shape=[shape((CAP, d))] * experts,
+        out_shape=shape((CAP, tokens.shape[1])),
         name="rows",
     )
 
@@ -109,6 +107,14 @@
         out_shape=[shape((CAP, d)), shape((CAP, n)), shape((CAP, 128), F32)],
         name="scaled",
     )
+
+
+def tick_kernel(out):
+    out[...] = jnp.zeros(out.shape, F32)
+
+
+def tick(run):
+    run(tick_kernel, out_shape=shape((8, 128), F32), name="tick")
 
 
 def swapped(q):
@@ -234,13 +240,8 @@
 
 
 def join(run, a, b):
-    return run(
-        join_kernel,
-        a,
-        b,
-        out_shape=shape((2 * a.shape[0], a.shape[1])),
-        name="join",
-    )
+    n, d = a.shape
+    return run(join_kernel, a, b, out_shape=shape((2 * n, d)), name="join")
 
 
 def total_of(terms):
@@ -375,30 +376,42 @@
 
 
 def combine_kernel(experts, weighted, *refs):
-    picks, weights = refs[:experts], refs[experts : 2 * experts]
-    keeps, gots = refs[2 * experts : 3 * experts], refs[3 * experts : 4 * experts]
-    out = refs[-1]
-    total = 0.0
-    for e in range(experts):
-        val = keeps[e][...].astype(F32) + gots[e][...].astype(F32)
-        if weighted:
-            val = weights[e][:, :1] * val
-        total = total + lax.dot_general(
-            picks[e][...], val.astype(BF), ROWS, preferred_element_type=F32
+    pick, weight, keeps, gots = (refs[i * experts : (i + 1) * experts] for i in range(4))
+    out, token, buf, sem = refs[-4:]
+    token[...] = jnp.zeros(token.shape, F32)
+    half = out.shape[1] // 2
+    copies = []
+    for i in range(2):
+        cols = slice(i * half, (i + 1) * half)
+        total = 0.0
+        for e in range(experts):
+            val = keeps[e][:, cols].astype(F32) + gots[e][:, cols].astype(F32)
+            if weighted:
+                val = weight[e][:, :1] * val
+            total = total + lax.dot_general(
+                pick[e][...], val.astype(BF), ROWS, preferred_element_type=F32
+            )
+        buf[i] = total.astype(BF)
+        copies.append(
+            pltpu.make_async_copy(buf.at[i], out.at[:, pl.ds(i * half, half)], sem.at[i])
         )
-    out[...] = total.astype(BF)
-
-
-def combine(run, picks, weights, pairs, weighted):
-    experts, (_, n) = len(picks), picks[0].shape
+        copies[-1].start()
+    for copy in copies:
+        copy.wait()
+
+
+def combine(run, pick, weight, pairs, weighted):
+    experts, n = len(pick), pick[0].shape[1]
     d = pairs[0][0].shape[1]
-    args = [*picks, *weights, *[p[0] for p in pairs], *[p[1] for p in pairs]]
+    args = [*pick, *weight, *[p[0] for p in pairs], *[p[1] for p in pairs]]
     return run(
         functools.partial(combine_kernel, experts, weighted),
         *args,
-        out_shape=shape((n, d)),
+        out_specs=[AN, VM],
+        out_shape=[shape((n, d)), shape((8, 128), F32)],
+        scratch=[pltpu.VMEM((2, n, d // 2), BF), pltpu.SemaphoreType.DMA((2,))],
         name="combine",
-    )
+    )[0]
 
 
 def build(n_dp, n_own):
@@ -448,76 +461,91 @@
             keep, send = project(run, core, rows, [gate_weight, up_weight], e, False)
             return keep, swap_core(send)
 
+        def grad_part(rows, e):
+            keep, send = project(run, core, rows, [down_weight], e, True)
+            return keep, swap_core(send)
+
         def across(part):
             return (*part, *shift_x(add(run, *part)))
 
-        r0, r1 = rows_of(run, ids, tokens, experts)
-        a0, a1 = gather(run, r0, plain), gather(run, r1, mixed_order)
+        def hidden_pair(groups):
+            sums, mine = hidden_of(run, groups)
+            return sums, (mine, swap_core(mine))
+
+        def grads_pair(sums, terms):
+            mine = grads_of(run, sums, terms)
+            return mine, swap_core(mine)
+
+        def expert_out(hidden, e, mixed):
+            pair = back(run, core, *hidden, [down_weight], e, False, mixed)
+            gen = scatter(run, *pair, mixed_order if mixed else plain)
+            next(gen)
+            return gen
+
+        def row_out(grads, e, mixed):
+            pair = back(run, core, *grads, [gate_weight, up_weight], e, True, mixed)
+            gen = scatter(run, *pair, mixed_order if mixed else plain)
+            next(gen)
+            return gen
+
+        a0 = gather(run, rows_of(run, ids, tokens, 0), plain)
         next(a0)
+        steps(a0, near - 1)
+        a1 = gather(run, rows_of(run, ids, tokens, 1), plain)
         next(a1)
-        steps(a0, near - 1)
+        rows0 = next(a0)
+        p0a = up_gate_part(rows0[:1], 0)
         steps(a1, near - 1)
         s0, pick0, weight0 = scaled_of(run, ids, cw, out_grad, 0)
         g0 = gather(run, s0, plain)
         next(g0)
-        rows0 = next(a0)
-        p0a = up_gate_part(rows0[:1], 0)
+        u0a = across(p0a)
         rows1 = next(a1)
-        u0a = across(p0a)
-        p1a = up_gate_part(rows1[:1], 1)
         steps(g0, near - 1)
-        u1a = across(p1a)
         p0b = up_gate_part(rows0[1:], 0)
-        scaled0 = next(g0)
-        u0b = across(p0b)
-        p1b = up_gate_part(rows1[1:], 1)
-        u0a = (sum_of(run, u0a),)
         s1, pick1, weight1 = scaled_of(run, ids, cw, out_grad, 1)
         g1 = gather(run, s1, plain)
         next(g1)
+        u0b = across(p0b)
+        u0a = (sum_of(run, u0a),)
+        p1a = up_gate_part(rows1[:1], 1)
+        scaled0 = next(g0)
+        u1a = across(p1a)
+        steps(g1, near - 1)
+        p1b = up_gate_part(rows1[1:], 1)
+        sums0, hidden0 = hidden_pair((u0a, u0b))
         u1b = across(p1b)
-        steps(g1, near - 1)
+        scaled1 = next(g1)
+        o0 = expert_out(hidden0, 0, False)
         u1a = (sum_of(run, u1a),)
-        scaled1 = next(g1)
-        sums0, hidden0 = hidden_of(run, (u0a, u0b))
-        hidden0 = (hidden0, swap_core(hidden0))
-        hp0 = project(run, core, scaled0, [down_weight], 0, True)
-        hp0 = (hp0[0], swap_core(hp0[1]))
-        o0 = scatter(run, *back(run, core, *hidden0, [down_weight], 0, False), plain)
+        hp0 = grad_part(scaled0, 0)
+        tick(run)
+        h0 = across(hp0)
+        sums1, hidden1 = hidden_pair((u1a, u1b))
+        hp1 = grad_part(scaled1, 1)
+        o1 = expert_out(hidden1, 1, True)
+        h1 = across(hp1)
+        pick, weight = (pick0, pick1), (weight0, weight1)
+        d0 = grads_pair(sums0, h0)
+        down = weight_grads(run, core, *scaled0, *hidden0, 0, 0, experts, None, False)
+        q0 = row_out(d0, 0, False)
         next(o0)
-        h0 = across(hp0)
-        sums1, hidden1 = hidden_of(run, (u1a, u1b))
-        hidden1 = (hidden1, swap_core(hidden1))
-        hp1 = project(run, core, scaled1, [down_weight], 1, True, True)
-        hp1 = (hp1[0], swap_core(hp1[1]))
-        o1 = scatter(run, *back(run, core, *hidden1, [down_weight], 1, False, True), plain)
-        next(o1)
-        h1 = across(hp1)
-        d0 = grads_of(run, sums0, h0)
-        d0 = (d0, swap_core(d0))
-        down = weight_grads(run, core, *scaled0, *hidden0, 0, 0, experts, None, False)
-        q0 = scatter(run, *back(run, core, *d0, [gate_weight, up_weight], 0, True), plain)
-        next(q0)
-        next(o0)
-        d1 = grads_of(run, sums1, h1)
-        d1 = (d1, swap_core(d1))
-        down = weight_grads(run, core, *scaled1, *hidden1, 0, 1, experts, down, False, True)
-        q1 = scatter(run, *back(run, core, *d1, [gate_weight, up_weight], 1, True), mixed_order)
-        next(q1)
-        out0 = steps(o0, near - 1)
+        d1 = grads_pair(sums1, h1)
+        down = weight_grads(run, core, *scaled1, *hidden1, 0, 1, experts, down, False)
+        q1 = row_out(d1, 1, True)
         next(o1)
         gate = weight_grads(run, core, *rows0, *d0, 0, 0, experts, None, True)
-        next(q1)
+        out0 = steps(o0, near - 1)
         next(q0)
         up = weight_grads(run, core, *rows0, *d0, 1, 0, experts, None, True)
         out1 = steps(o1, near - 1)
-        row1 = steps(q1, near - 1)
+        next(q1)
         gate = weight_grads(run, core, *rows1, *d1, 0, 1, experts, gate, True)
         row0 = steps(q0, near - 1)
+        mixed = combine(run, pick, weight, (out0, out1), True)
+        row1 = steps(q1, near - 1)
         up = weight_grads(run, core, *rows1, *d1, 1, 1, experts, up, True)
-        picks, weights = (pick0, pick1), (weight0, weight1)
-        mixed = combine(run, picks, weights, (out0, out1), True)
-        token_grad = combine(run, picks, weights, (row0, row1), False)
+        token_grad = combine(run, pick, weight, (row0, row1), False)
         return mixed, token_grad, gate, up, down
 
     return local

time: 155 us -> 132 us (0.85)
  waiting for transfers between devices: 70.3 us -> 40 us
  starting transfers between devices: 35.6 us -> 46 us
  local copies, waits for them, and re-layouts: 6.94 us -> 3.32 us
    ppermute x24, waiting for transfers between devices: 67.4 us -> 33.8 us  [swap(): return lax.ppermute(x, 'dp', [(i, i ^ 1 << bit) for i in range(n_dp)])]
    ppermute x24, starting transfers between devices: 29.6 us -> 37 us  [swap(): return lax.ppermute(x, 'dp', [(i, i ^ 1 << bit) for i in range(n_dp)])]
    unnamed x56 -> x48, local copies, waits for them, and re-layouts: 6.94 us -> 3.32 us
    ppermute x6, waiting for transfers between devices: 0.02 us -> 3.58 us  [shift_x(): lax.ppermute(x, 'own', [(i, (i + 2 * k) % n_own) for i in range(n_own)])]
    ppermute x6, starting transfers between devices: 5.22 us -> 8.38 us  [shift_x(): lax.ppermute(x, 'own', [(i, (i + 2 * k) % n_own) for i in range(n_own)])]
    pallas_call x49 -> x51, Pallas kernels: 40.5 us -> 40.6 us  [__call__(): pl.pallas_call(body, in_specs=in_specs, out_specs=out_specs, out_shape=ou...]
  transfers between devices with their start and end apart: 40 -> 40, of which waited for: 16 -> 15; matrix products, arithmetic and copies ran while one was open for 0% -> 0% of each run, Pallas kernels for 25% -> 29%
where the time goes in v3:
time: 132 us; the launch traced here: 131 us
  starting transfers between devices  46 us (35%)
  Pallas kernels  40.6 us (31%)
  waiting for transfers between devices  40 us (30%)
  local copies, waits for them, and re-layouts  3.32 us (3%)
  between operations  1.52 us (1%)
    pallas_call x51, Pallas kernels, __call__(): pl.pallas_call(body, in_specs=in_specs, out_specs=out_specs, out_shape=ou...  40.6 us
    ppermute x24, starting transfers between devices, swap(): return lax.ppermute(x, 'dp', [(i, i ^ 1 << bit) for i in range(n_dp)])  37 us
    ppermute x24, waiting for transfers between devices, swap(): return lax.ppermute(x, 'dp', [(i, i ^ 1 << bit) for i in range(n_dp)])  33.8 us
    ppermute x6, starting transfers between devices, shift_x(): lax.ppermute(x, 'own', [(i, (i + 2 * k) % n_own) for i in range(n_own)])  8.38 us
    ppermute x6, waiting for transfers between devices, shift_x(): lax.ppermute(x, 'own', [(i, (i + 2 * k) % n_own) for i in range(n_own)])  3.58 us
    unnamed x48, local copies, waits for them, and re-layouts  3.32 us
    ppermute x10, waiting for transfers between devices, swap_core(): return lax.ppermute(x, 'own', [(i, i ^ 1) for i in range(n_own)])  2.65 us
  transfers between devices with their start and end apart: 40, of which 15 were waited for; matrix products, arithmetic and copies ran while one was open for 0% of the time, Pallas kernels for 29%

profile of v3, /device:TPU:0, one launch (start us, length us, event | category | flops | bytes accessed | tf_op | source)
XLA Modules:
  0.0 131.5 jit_solution(3520425409668578024)
XLA Ops:
  2.6 4.1 %collective-permute-start = (bf16[40,1536]{1,0:T(8,128)(2,1)S(1)}, bf16[40,1536]{1,0:T(8,128)(2,1)S(1)}, u32[]{:S(2)}, u32[]{:S(2)}) collective-permute-start(bf16[40,1536]{1,0:T(8,128)(2,1)S(1)} %rows.2.refs_0_.refs_2_), channel_id=1, source_target_pairs={{0,16},{4,20},{8,24},{12,28},{16,0},{20,4},{24,8},{28,12},{1,17},{... | collective-permute-start | bytes 368648 | tf_op jit(solution)/shard_map/ppermute | solution.py:423
  6.7 5.9 %collective-permute-done.refs_1_ = bf16[40,1536]{1,0:T(8,128)(2,1)S(1)} collective-permute-done((bf16[40,1536]{1,0:T(8,128)(2,1)S(1)}, bf16[40,1536]{1,0:T(8,128)(2,1)S(1)}, u32[]{:S(2)}, u32[]{:S(2)}) %collective-permute-start) | collective-permute-done | bytes 122912 | tf_op jit(solution)/shard_map/ppermute | solution.py:423
  13.9 3.4 %collective-permute-start.1 = (bf16[40,1536]{1,0:T(8,128)(2,1)S(1)}, bf16[40,1536]{1,0:T(8,128)(2,1)S(1)}, u32[]{:S(2)}, u32[]{:S(2)}) collective-permute-start(bf16[40,1536]{1,0:T(8,128)(2,1)S(1)} %rows.3.refs_2_.refs_0_), channel_id=1, source_target_pairs={{0,16},{4,20},{8,24},{12,28},{16,0},{20,4},{24,8},{28,12},{1,17},{... | collective-permute-start | bytes 368648 | tf_op jit(solution)/shard_map/ppermute | solution.py:423
  17.3 5.2 %collective-permute-done.2.refs_1_ = bf16[80,1536]{1,0:T(8,128)(2,1)S(1)} collective-permute-done((bf16[80,1536]{1,0:T(8,128)(2,1)S(1)}, bf16[80,1536]{1,0:T(8,128)(2,1)S(1)}, u32[]{:S(2)}, u32[]{:S(2)}) %collective-permute-start.2) | collective-permute-done | bytes 245792 | tf_op jit(solution)/shard_map/ppermute | solution.py:423
  26.6 4.3 %collective-permute-start.4 = (bf16[40,1536]{1,0:T(8,128)(2,1)S(1)}, bf16[40,1536]{1,0:T(8,128)(2,1)S(1)}, u32[]{:S(2)}, u32[]{:S(2)}) collective-permute-start(bf16[40,1536]{1,0:T(8,128)(2,1)S(1)} %get-tuple-element.68.refs_0_), channel_id=1, source_target_pairs={{0,16},{4,20},{8,24},{12,28},{16,0},{20,4},{24,8},{28,12},{1,17},{... | collective-permute-start | bytes 368648 | tf_op jit(solution)/shard_map/ppermute | solution.py:423
  30.9 1.6 %collective-permute-start.7 = (bf16[2,160,512]{2,1,0:T(8,128)(2,1)S(1)}, bf16[2,160,512]{2,1,0:T(8,128)(2,1)S(1)}, u32[]{:S(2)}, u32[]{:S(2)}) collective-permute-start(bf16[2,160,512]{2,1,0:T(8,128)(2,1)S(1)} %add.11.refs_2_), channel_id=1, source_target_pairs={{0,2},{1,3},{2,0},{3,1},{4,6},{5,7},{6,4},{7,5},{8,10},{9,11},{10,... | collective-permute-start | bytes 983048 | tf_op jit(solution)/shard_map/ppermute | solution.py:430
  34.0 2.2 %collective-permute-done.4.refs_1_ = bf16[40,1536]{1,0:T(8,128)(2,1)S(1)} collective-permute-done((bf16[40,1536]{1,0:T(8,128)(2,1)S(1)}, bf16[40,1536]{1,0:T(8,128)(2,1)S(1)}, u32[]{:S(2)}, u32[]{:S(2)}) %collective-permute-start.4) | collective-permute-done | bytes 122912 | tf_op jit(solution)/shard_map/ppermute | solution.py:423
  36.2 2.0 %collective-permute-start.13 = (bf16[80,1536]{1,0:T(8,128)(2,1)S(1)}, bf16[80,1536]{1,0:T(8,128)(2,1)S(1)}, u32[]{:S(2)}, u32[]{:S(2)}) collective-permute-start(bf16[80,1536]{1,0:T(8,128)(2,1)S(1)} %join.12.refs_4_.refs_0_), channel_id=1, source_target_pairs={{0,8},{4,12},{8,0},{12,4},{16,24},{20,28},{24,16},{28,20},{1,9},{5... | collective-permute-start | bytes 737288 | tf_op jit(solution)/shard_map/ppermute | solution.py:423
  39.8 2.2 %collective-permute-start.11 = (bf16[40,1536]{1,0:T(8,128)(2,1)S(1)}, bf16[40,1536]{1,0:T(8,128)(2,1)S(1)}, u32[]{:S(2)}, u32[]{:S(2)}) collective-permute-start(bf16[40,1536]{1,0:T(8,128)(2,1)S(1)} %get-tuple-element.75.refs_0_), channel_id=1, source_target_pairs={{0,16},{4,20},{8,24},{12,28},{16,0},{20,4},{24,8},{28,12},{1,17},{... | collective-permute-start | bytes 368648 | tf_op jit(solution)/shard_map/ppermute | solution.py:423
  42.1 1.6 %collective-permute-start.9 = (bf16[2,160,512]{2,1,0:T(8,128)(2,1)S(1)}, bf16[2,160,512]{2,1,0:T(8,128)(2,1)S(1)}, u32[]{:S(2)}, u32[]{:S(2)}) collective-permute-start(bf16[2,160,512]{2,1,0:T(8,128)(2,1)S(1)} %add.12.refs_3_), channel_id=1, source_target_pairs={{0,2},{1,3},{2,0},{3,1},{4,6},{5,7},{6,4},{7,5},{8,10},{9,11},{10,... | collective-permute-start | bytes 983048 | tf_op jit(solution)/shard_map/ppermute | solution.py:430
  50.4 2.3 %collective-permute-done.9.refs_3_ = bf16[2,160,512]{2,1,0:T(8,128)(2,1)S(1)} collective-permute-done((bf16[2,160,512]{2,1,0:T(8,128)(2,1)S(1)}, bf16[2,160,512]{2,1,0:T(8,128)(2,1)S(1)}, u32[]{:S(2)}, u32[]{:S(2)}) %collective-permute-start.9) | collective-permute-done | bytes 327712 | tf_op jit(solution)/shard_map/ppermute | solution.py:430
  53.2 1.6 %collective-permute-start.23 = (bf16[2,160,512]{2,1,0:T(8,128)(2,1)S(1)}, bf16[2,160,512]{2,1,0:T(8,128)(2,1)S(1)}, u32[]{:S(2)}, u32[]{:S(2)}) collective-permute-start(bf16[2,160,512]{2,1,0:T(8,128)(2,1)S(1)} %add.14.refs_2_), channel_id=1, source_target_pairs={{0,2},{1,3},{2,0},{3,1},{4,6},{5,7},{6,4},{7,5},{8,10},{9,11},{10,... | collective-permute-start | bytes 983048 | tf_op jit(solution)/shard_map/ppermute | solution.py:430
  54.8 2.0 %collective-permute-done.15.refs_1_ = bf16[80,1536]{1,0:T(8,128)(2,1)S(1)} collective-permute-done((bf16[80,1536]{1,0:T(8,128)(2,1)S(1)}, bf16[80,1536]{1,0:T(8,128)(2,1)S(1)}, u32[]{:S(2)}, u32[]{:S(2)}) %collective-permute-start.15) | collective-permute-done | bytes 245792 | tf_op jit(solution)/shard_map/ppermute | solution.py:423
  61.6 1.6 %collective-permute-done.20.refs_1_.refs_2_ = bf16[1,320,512]{2,1,0:T(8,128)(2,1)S(1)} collective-permute-done((bf16[1,320,512]{2,1,0:T(8,128)(2,1)S(1)}, bf16[1,320,512]{2,1,0:T(8,128)(2,1)S(1)}, u32[]{:S(2)}, u32[]{:S(2)}) %collective-permute-start.20) | collective-permute-done | bytes 327712 | tf_op jit(solution)/shard_map/ppermute | solution.py:426
  63.3 1.6 %collective-permute-start.21 = (bf16[1,320,512]{2,1,0:T(8,128)(2,1)S(1)}, bf16[1,320,512]{2,1,0:T(8,128)(2,1)S(1)}, u32[]{:S(2)}, u32[]{:S(2)}) collective-permute-start(bf16[1,320,512]{2,1,0:T(8,128)(2,1)S(1)} %add.15.refs_4_), channel_id=1, source_target_pairs={{0,2},{1,3},{2,0},{3,1},{4,6},{5,7},{6,4},{7,5},{8,10},{9,11},{10,... | collective-permute-start | bytes 983048 | tf_op jit(solution)/shard_map/ppermute | solution.py:430
  66.4 4.6 %collective-permute-done.22.refs_2_ = bf16[160,1536]{1,0:T(8,128)(2,1)S(1)} collective-permute-done((bf16[160,1536]{1,0:T(8,128)(2,1)S(1)}, bf16[160,1536]{1,0:T(8,128)(2,1)S(1)}, u32[]{:S(2)}, u32[]{:S(2)}) %collective-permute-start.22) | collective-permute-done | bytes 491552 | tf_op jit(solution)/shard_map/ppermute | solution.py:423
  74.0 1.6 %collective-permute-start.29 = (bf16[1,320,512]{2,1,0:T(8,128)(2,1)S(1)}, bf16[1,320,512]{2,1,0:T(8,128)(2,1)S(1)}, u32[]{:S(2)}, u32[]{:S(2)}) collective-permute-start(bf16[1,320,512]{2,1,0:T(8,128)(2,1)S(1)} %add.16.refs_4_), channel_id=1, source_target_pairs={{0,2},{1,3},{2,0},{3,1},{4,6},{5,7},{6,4},{7,5},{8,10},{9,11},{10,... | collective-permute-start | bytes 983048 | tf_op jit(solution)/shard_map/ppermute | solution.py:430
  76.3 3.2 %weight_grad.6 = (f32[2,1024,1536]{2,1,0:T(8,128)}, f32[8,128]{1,0:T(8,128)S(1)}) custom-call(s32[1]{0:T(128)} %bitcast.2.refs_0_, bf16[160,1536]{1,0:T(8,128)(2,1)S(1)} %join.13.refs_2_.refs_1_, bf16[160,1536]{1,0:T(8,128)(2,1)S(1)} %collective-permute-done.18.refs_2_, bf16[1,320,512]{2,1,0:T(8,128)(2,1)S(1)} %get-tuple-element.79.refs_2_.refs_1_.refs_3_, ...), custom_call_target="tpu_custom_call" | custom-call | flops 10000000000 | bytes 100000000 | tf_op jit(solution)/shard_map/weight_grad/pallas_call | solution.py:48
  79.4 2.2 %row_grad_part.2 = (bf16[160,1536]{1,0:T(8,128)(2,1)S(1)}, bf16[160,1536]{1,0:T(8,128)(2,1)S(1)}) custom-call(s32[1]{0:T(128)} %bitcast.2.refs_0_, bf16[2,320,512]{2,1,0:T(8,128)(2,1)S(1)} %gate_up_grads.2.refs_5_.refs_1_.refs_3_, bf16[2,320,512]{2,1,0:T(8,128)(2,1)S(1)} %collective-permute-done.26.refs_2_.refs_4_, bf16[2,1536,1024]{2,1,0:T(8,128)(2,1)S(1)} %bitcast.6, ...), custom_call_target="tpu_custom_call" | custom-call | flops 10000000000 | bytes 100000000 | tf_op jit(solution)/shard_map/row_grad_part/pallas_call | solution.py:48
  81.8 1.7 %collective-permute-start.27 = (bf16[80,1536]{1,0:T(8,128)(2,1)S(1)}, bf16[80,1536]{1,0:T(8,128)(2,1)S(1)}, u32[]{:S(2)}, u32[]{:S(2)}) collective-permute-start(bf16[80,1536]{1,0:T(8,128)(2,1)S(1)} %get-tuple-element.93), channel_id=1, source_target_pairs={{0,8},{4,12},{8,0},{12,4},{16,24},{20,28},{24,16},{28,20},{1,9},{5... | collective-permute-start | bytes 737288 | tf_op jit(solution)/shard_map/ppermute | solution.py:423
  84.6 3.2 %weight_grad.7 = (f32[2,1024,1536]{2,1,0:T(8,128)}, f32[8,128]{1,0:T(8,128)S(1)}) custom-call(s32[1]{0:T(128)} %bitcast.2.refs_0_, bf16[160,1536]{1,0:T(8,128)(2,1)S(1)} %join.15.refs_4_.refs_1_, bf16[160,1536]{1,0:T(8,128)(2,1)S(1)} %collective-permute-done.22.refs_2_, ...), custom_call_target="tpu_custom_call", output_to_operand_aliasing={{0}: (5, {})} | custom-call | flops 10000000000 | bytes 100000000 | tf_op jit(solution)/shard_map/weight_grad/pallas_call | solution.py:48
  87.8 2.2 %row_grad_part.3 = (bf16[160,1536]{1,0:T(8,128)(2,1)S(1)}, bf16[160,1536]{1,0:T(8,128)(2,1)S(1)}) custom-call(s32[1]{0:T(128)} %bitcast.2.refs_0_, bf16[2,320,512]{2,1,0:T(8,128)(2,1)S(1)} %gate_up_grads.3.refs_6_.refs_1_.refs_3_, bf16[2,320,512]{2,1,0:T(8,128)(2,1)S(1)} %collective-permute-done.30.refs_2_.refs_4_, bf16[2,1536,1024]{2,1,0:T(8,128)(2,1)S(1)} %bitcast.6, ...), custom_call_target="tpu_custom_call" | custom-call | flops 10000000000 | bytes 100000000 | tf_op jit(solution)/shard_map/row_grad_part/pallas_call | solution.py:48
  92.3 3.2 %weight_grad.8 = (f32[2,1536,1024]{2,1,0:T(8,128)}, f32[8,128]{1,0:T(8,128)S(1)}) custom-call(s32[1]{0:T(128)} %bitcast.2.refs_0_, bf16[160,1536]{1,0:T(8,128)(2,1)S(1)} %copy-done.5, bf16[160,1536]{1,0:T(8,128)(2,1)S(1)} %copy-done.7, bf16[2,320,512]{2,1,0:T(8,128)(2,1)S(1)} %gate_up_grads.2.refs_5_.refs_1_.refs_3_, ...), custom_call_target="tpu_custom_call" | custom-call | flops 10000000000 | bytes 100000000 | tf_op jit(solution)/shard_map/weight_grad/pallas_call | solution.py:48
  95.6 2.3 %collective-permute-start.33 = (bf16[40,1536]{1,0:T(8,128)(2,1)S(1)}, bf16[40,1536]{1,0:T(8,128)(2,1)S(1)}, u32[]{:S(2)}, u32[]{:S(2)}) collective-permute-start(bf16[40,1536]{1,0:T(8,128)(2,1)S(1)} %get-tuple-element.107), channel_id=1, source_target_pairs={{0,16},{4,20},{8,24},{12,28},{16,0},{20,4},{24,8},{28,12},{1,17},{... | collective-permute-start | bytes 368648 | tf_op jit(solution)/shard_map/ppermute | solution.py:423
  98.0 1.8 %collective-permute-start.35 = (bf16[80,1536]{1,0:T(8,128)(2,1)S(1)}, bf16[80,1536]{1,0:T(8,128)(2,1)S(1)}, u32[]{:S(2)}, u32[]{:S(2)}) collective-permute-start(bf16[80,1536]{1,0:T(8,128)(2,1)S(1)} %get-tuple-element.109), channel_id=1, source_target_pairs={{0,8},{4,12},{8,0},{12,4},{16,24},{20,28},{24,16},{28,20},{1,9},{5... | collective-permute-start | bytes 737288 | tf_op jit(solution)/shard_map/ppermute | solution.py:423
  99.8 3.2 %weight_grad.9 = (f32[2,1536,1024]{2,1,0:T(8,128)}, f32[8,128]{1,0:T(8,128)S(1)}) custom-call(s32[1]{0:T(128)} %bitcast.2.refs_0_, bf16[160,1536]{1,0:T(8,128)(2,1)S(1)} %copy-done.5, bf16[160,1536]{1,0:T(8,128)(2,1)S(1)} %copy-done.7, bf16[2,320,512]{2,1,0:T(8,128)(2,1)S(1)} %gate_up_grads.2.refs_5_.refs_1_.refs_3_, ...), custom_call_target="tpu_custom_call" | custom-call | flops 10000000000 | bytes 100000000 | tf_op jit(solution)/shard_map/weight_grad/pallas_call | solution.py:48
  103.6 6.5 %collective-permute-done.36.refs_1_ = bf16[160,1536]{1,0:T(8,128)(2,1)S(1)} collective-permute-done((bf16[160,1536]{1,0:T(8,128)(2,1)S(1)}, bf16[160,1536]{1,0:T(8,128)(2,1)S(1)}, u32[]{:S(2)}, u32[]{:S(2)}) %collective-permute-start.36) | collective-permute-done | bytes 491552 | tf_op jit(solution)/shard_map/ppermute | solution.py:423
  111.3 3.4 %weight_grad.10 = (f32[2,1536,1024]{2,1,0:T(8,128)}, f32[8,128]{1,0:T(8,128)S(1)}) custom-call(s32[1]{0:T(128)} %bitcast.2.refs_0_, bf16[160,1536]{1,0:T(8,128)(2,1)S(1)} %copy-done.1, bf16[160,1536]{1,0:T(8,128)(2,1)S(1)} %copy-done.3, bf16[2,320,512]{2,1,0:T(8,128)(2,1)S(1)} %gate_up_grads.3.refs_6_.refs_1_.refs_3_, ...), custom_call_target="tpu_custom_call", output_to_operand_aliasing={{0}: (5, {})} | custom-call | flops 10000000000 | bytes 100000000 | tf_op jit(solution)/shard_map/weight_grad/pallas_call | solution.py:48
  119.0 4.2 %collective-permute-done.37.refs_1_ = bf16[80,1536]{1,0:T(8,128)(2,1)S(1)} collective-permute-done((bf16[80,1536]{1,0:T(8,128)(2,1)S(1)}, bf16[80,1536]{1,0:T(8,128)(2,1)S(1)}, u32[]{:S(2)}, u32[]{:S(2)}) %collective-permute-start.37) | collective-permute-done | bytes 245792 | tf_op jit(solution)/shard_map/ppermute | solution.py:423
  123.3 2.5 %collective-permute-start.39 = (bf16[40,1536]{1,0:T(8,128)(2,1)S(1)}, bf16[40,1536]{1,0:T(8,128)(2,1)S(1)}, u32[]{:S(2)}, u32[]{:S(2)}) collective-permute-start(bf16[40,1536]{1,0:T(8,128)(2,1)S(1)} %get-tuple-element.120), channel_id=1, source_target_pairs={{0,16},{4,20},{8,24},{12,28},{16,0},{20,4},{24,8},{28,12},{1,17},{... | collective-permute-start | bytes 368648 | tf_op jit(solution)/shard_map/ppermute | solution.py:423
  125.8 3.2 %weight_grad.11 = (f32[2,1536,1024]{2,1,0:T(8,128)}, f32[8,128]{1,0:T(8,128)S(1)}) custom-call(s32[1]{0:T(128)} %bitcast.2.refs_0_, bf16[160,1536]{1,0:T(8,128)(2,1)S(1)} %copy-done.1, bf16[160,1536]{1,0:T(8,128)(2,1)S(1)} %copy-done.3, bf16[2,320,512]{2,1,0:T(8,128)(2,1)S(1)} %gate_up_grads.3.refs_6_.refs_1_.refs_3_, ...), custom_call_target="tpu_custom_call", output_to_operand_aliasing={{0}: (5, {})} | custom-call | flops 10000000000 | bytes 100000000 | tf_op jit(solution)/shard_map/weight_grad/pallas_call | solution.py:48
  129.6 1.7 %combine.3 = (bf16[128,1536]{1,0:T(8,128)(2,1)}, f32[8,128]{1,0:T(8,128)}) custom-call(bf16[40,128]{1,0:T(8,128)(2,1)S(1)} %copy-done.15, bf16[40,128]{1,0:T(8,128)(2,1)S(1)} %copy-done.17, f32[40,128]{1,0:T(8,128)S(1)} %get-tuple-element.72.refs_2_, f32[40,128]{1,0:T(8,128)S(1)} %get-tuple-element.73.refs_3_, ...), custom_call_target="tpu_custom_call" | custom-call | flops 10000000000 | bytes 100000000 | tf_op jit(solution)/shard_map/combine/pallas_call | solution.py:48
  (150 shorter events, 37.8 us)
Async XLA Ops:
  2.6 10.1 %collective-permute-start = (bf16[40,1536]{1,0:T(8,128)(2,1)S(1)}, bf16[40,1536]{1,0:T(8,128)(2,1)S(1)}, u32[]{:S(2)}, u32[]{:S(2)}) collective-permute-start(bf16[40,1536]{1,0:T(8,128)(2,1)S(1)} %rows.2.refs_0_.refs_2_), channel_id=1, source_target_pairs={{0,16},{4,20},{8,24},{12,28},{16,0},{20,4},{24,8},{28,12},{1,17},{... | collective-permute-start | bytes 368648 | tf_op jit(solution)/shard_map/ppermute | solution.py:423
  12.7 9.8 %collective-permute-start.2 = (bf16[80,1536]{1,0:T(8,128)(2,1)S(1)}, bf16[80,1536]{1,0:T(8,128)(2,1)S(1)}, u32[]{:S(2)}, u32[]{:S(2)}) collective-permute-start(bf16[80,1536]{1,0:T(8,128)(2,1)S(1)} %join.8.refs_2_.refs_0_), channel_id=1, source_target_pairs={{0,8},{4,12},{8,0},{12,4},{16,24},{20,28},{24,16},{28,20},{1,9},{5... | collective-permute-start | bytes 737288 | tf_op jit(solution)/shard_map/ppermute | solution.py:423
  13.9 11.4 %collective-permute-start.1 = (bf16[40,1536]{1,0:T(8,128)(2,1)S(1)}, bf16[40,1536]{1,0:T(8,128)(2,1)S(1)}, u32[]{:S(2)}, u32[]{:S(2)}) collective-permute-start(bf16[40,1536]{1,0:T(8,128)(2,1)S(1)} %rows.3.refs_2_.refs_0_), channel_id=1, source_target_pairs={{0,16},{4,20},{8,24},{12,28},{16,0},{20,4},{24,8},{28,12},{1,17},{... | collective-permute-start | bytes 368648 | tf_op jit(solution)/shard_map/ppermute | solution.py:423
  22.6 15.6 %collective-permute-start.3 = (bf16[160,1536]{1,0:T(8,128)(2,1)S(1)}, bf16[160,1536]{1,0:T(8,128)(2,1)S(1)}, u32[]{:S(2)}, u32[]{:S(2)}) collective-permute-start(bf16[160,1536]{1,0:T(8,128)(2,1)S(1)} %join.9.refs_1_.refs_4_), channel_id=1, source_target_pairs={{0,4},{4,0},{8,12},{12,8},{16,20},{20,16},{24,28},{28,24},{1,5},{5... | collective-permute-start | bytes 1474568 | tf_op jit(solution)/shard_map/ppermute | solution.py:423
  25.3 7.2 %collective-permute-start.5 = (bf16[80,1536]{1,0:T(8,128)(2,1)S(1)}, bf16[80,1536]{1,0:T(8,128)(2,1)S(1)}, u32[]{:S(2)}, u32[]{:S(2)}) collective-permute-start(bf16[80,1536]{1,0:T(8,128)(2,1)S(1)} %join.10.refs_3_.refs_0_), channel_id=1, source_target_pairs={{0,8},{4,12},{8,0},{12,4},{16,24},{20,28},{24,16},{28,20},{1,9},{5... | collective-permute-start | bytes 737288 | tf_op jit(solution)/shard_map/ppermute | solution.py:423
  25.7 5.1 %collective-permute-start.6 = (bf16[2,160,512]{2,1,0:T(8,128)(2,1)S(1)}, bf16[2,160,512]{2,1,0:T(8,128)(2,1)S(1)}, u32[]{:S(2)}, u32[]{:S(2)}) collective-permute-start(bf16[2,160,512]{2,1,0:T(8,128)(2,1)S(1)} %get-tuple-element.69), channel_id=1, source_target_pairs={{0,1},{1,0},{2,3},{3,2},{4,5},{5,4},{6,7},{7,6},{8,9},{9,8},{10,11... | collective-permute-start | bytes 983048 | tf_op jit(solution)/shard_map/ppermute | solution.py:426
  26.6 9.6 %collective-permute-start.4 = (bf16[40,1536]{1,0:T(8,128)(2,1)S(1)}, bf16[40,1536]{1,0:T(8,128)(2,1)S(1)}, u32[]{:S(2)}, u32[]{:S(2)}) collective-permute-start(bf16[40,1536]{1,0:T(8,128)(2,1)S(1)} %get-tuple-element.68.refs_0_), channel_id=1, source_target_pairs={{0,16},{4,20},{8,24},{12,28},{16,0},{20,4},{24,8},{28,12},{1,17},{... | collective-permute-start | bytes 368648 | tf_op jit(solution)/shard_map/ppermute | solution.py:423
  30.9 12.8 %collective-permute-start.7 = (bf16[2,160,512]{2,1,0:T(8,128)(2,1)S(1)}, bf16[2,160,512]{2,1,0:T(8,128)(2,1)S(1)}, u32[]{:S(2)}, u32[]{:S(2)}) collective-permute-start(bf16[2,160,512]{2,1,0:T(8,128)(2,1)S(1)} %add.11.refs_2_), channel_id=1, source_target_pairs={{0,2},{1,3},{2,0},{3,1},{4,6},{5,7},{6,4},{7,5},{8,10},{9,11},{10,... | collective-permute-start | bytes 983048 | tf_op jit(solution)/shard_map/ppermute | solution.py:430
  32.5 16.5 %collective-permute-start.10 = (bf16[160,1536]{1,0:T(8,128)(2,1)S(1)}, bf16[160,1536]{1,0:T(8,128)(2,1)S(1)}, u32[]{:S(2)}, u32[]{:S(2)}) collective-permute-start(bf16[160,1536]{1,0:T(8,128)(2,1)S(1)} %join.11.refs_2_.refs_1_), channel_id=1, source_target_pairs={{0,4},{4,0},{8,12},{12,8},{16,20},{20,16},{24,28},{28,24},{1,5},{5... | collective-permute-start | bytes 1474568 | tf_op jit(solution)/shard_map/ppermute | solution.py:423
  36.2 9.0 %collective-permute-start.13 = (bf16[80,1536]{1,0:T(8,128)(2,1)S(1)}, bf16[80,1536]{1,0:T(8,128)(2,1)S(1)}, u32[]{:S(2)}, u32[]{:S(2)}) collective-permute-start(bf16[80,1536]{1,0:T(8,128)(2,1)S(1)} %join.12.refs_4_.refs_0_), channel_id=1, source_target_pairs={{0,8},{4,12},{8,0},{12,4},{16,24},{20,28},{24,16},{28,20},{1,9},{5... | collective-permute-start | bytes 737288 | tf_op jit(solution)/shard_map/ppermute | solution.py:423
  39.8 9.1 %collective-permute-start.11 = (bf16[40,1536]{1,0:T(8,128)(2,1)S(1)}, bf16[40,1536]{1,0:T(8,128)(2,1)S(1)}, u32[]{:S(2)}, u32[]{:S(2)}) collective-permute-start(bf16[40,1536]{1,0:T(8,128)(2,1)S(1)} %get-tuple-element.75.refs_0_), channel_id=1, source_target_pairs={{0,16},{4,20},{8,24},{12,28},{16,0},{20,4},{24,8},{28,12},{1,17},{... | collective-permute-start | bytes 368648 | tf_op jit(solution)/shard_map/ppermute | solution.py:423
  42.1 10.6 %collective-permute-start.9 = (bf16[2,160,512]{2,1,0:T(8,128)(2,1)S(1)}, bf16[2,160,512]{2,1,0:T(8,128)(2,1)S(1)}, u32[]{:S(2)}, u32[]{:S(2)}) collective-permute-start(bf16[2,160,512]{2,1,0:T(8,128)(2,1)S(1)} %add.12.refs_3_), channel_id=1, source_target_pairs={{0,2},{1,3},{2,0},{3,1},{4,6},{5,7},{6,4},{7,5},{8,10},{9,11},{10,... | collective-permute-start | bytes 983048 | tf_op jit(solution)/shard_map/ppermute | solution.py:430
  45.2 15.1 %collective-permute-start.18 = (bf16[160,1536]{1,0:T(8,128)(2,1)S(1)}, bf16[160,1536]{1,0:T(8,128)(2,1)S(1)}, u32[]{:S(2)}, u32[]{:S(2)}) collective-permute-start(bf16[160,1536]{1,0:T(8,128)(2,1)S(1)} %join.13.refs_2_.refs_1_), channel_id=1, source_target_pairs={{0,4},{4,0},{8,12},{12,8},{16,20},{20,16},{24,28},{28,24},{1,5},{5... | collective-permute-start | bytes 1474568 | tf_op jit(solution)/shard_map/ppermute | solution.py:423
  46.8 13.3 %collective-permute-start.19 = (bf16[2,160,512]{2,1,0:T(8,128)(2,1)S(1)}, bf16[2,160,512]{2,1,0:T(8,128)(2,1)S(1)}, u32[]{:S(2)}, u32[]{:S(2)}) collective-permute-start(bf16[2,160,512]{2,1,0:T(8,128)(2,1)S(1)} %add.13.refs_2_), channel_id=1, source_target_pairs={{0,2},{1,3},{2,0},{3,1},{4,6},{5,7},{6,4},{7,5},{8,10},{9,11},{10,... | collective-permute-start | bytes 983048 | tf_op jit(solution)/shard_map/ppermute | solution.py:430
  49.0 7.8 %collective-permute-start.15 = (bf16[80,1536]{1,0:T(8,128)(2,1)S(1)}, bf16[80,1536]{1,0:T(8,128)(2,1)S(1)}, u32[]{:S(2)}, u32[]{:S(2)}) collective-permute-start(bf16[80,1536]{1,0:T(8,128)(2,1)S(1)} %join.14.refs_4_.refs_0_), channel_id=1, source_target_pairs={{0,8},{4,12},{8,0},{12,4},{16,24},{20,28},{24,16},{28,20},{1,9},{5... | collective-permute-start | bytes 737288 | tf_op jit(solution)/shard_map/ppermute | solution.py:423
  53.2 12.9 %collective-permute-start.23 = (bf16[2,160,512]{2,1,0:T(8,128)(2,1)S(1)}, bf16[2,160,512]{2,1,0:T(8,128)(2,1)S(1)}, u32[]{:S(2)}, u32[]{:S(2)}) collective-permute-start(bf16[2,160,512]{2,1,0:T(8,128)(2,1)S(1)} %add.14.refs_2_), channel_id=1, source_target_pairs={{0,2},{1,3},{2,0},{3,1},{4,6},{5,7},{6,4},{7,5},{8,10},{9,11},{10,... | collective-permute-start | bytes 983048 | tf_op jit(solution)/shard_map/ppermute | solution.py:430
  56.8 14.2 %collective-permute-start.22 = (bf16[160,1536]{1,0:T(8,128)(2,1)S(1)}, bf16[160,1536]{1,0:T(8,128)(2,1)S(1)}, u32[]{:S(2)}, u32[]{:S(2)}) collective-permute-start(bf16[160,1536]{1,0:T(8,128)(2,1)S(1)} %join.15.refs_4_.refs_1_), channel_id=1, source_target_pairs={{0,4},{4,0},{8,12},{12,8},{16,20},{20,16},{24,28},{28,24},{1,5},{5... | collective-permute-start | bytes 1474568 | tf_op jit(solution)/shard_map/ppermute | solution.py:423
  58.6 23.1 %collective-permute-start.17 = (bf16[160,1536]{1,0:T(8,128)(2,1)S(1)}, bf16[160,1536]{1,0:T(8,128)(2,1)S(1)}, u32[]{:S(2)}, u32[]{:S(2)}) collective-permute-start(bf16[160,1536]{1,0:T(8,128)(2,1)S(1)} %get-tuple-element.82), channel_id=1, source_target_pairs={{0,4},{4,0},{8,12},{12,8},{16,20},{20,16},{24,28},{28,24},{1,5},{5... | collective-permute-start | bytes 1474568 | tf_op jit(solution)/shard_map/ppermute | solution.py:423
  63.3 12.3 %collective-permute-start.21 = (bf16[1,320,512]{2,1,0:T(8,128)(2,1)S(1)}, bf16[1,320,512]{2,1,0:T(8,128)(2,1)S(1)}, u32[]{:S(2)}, u32[]{:S(2)}) collective-permute-start(bf16[1,320,512]{2,1,0:T(8,128)(2,1)S(1)} %add.15.refs_4_), channel_id=1, source_target_pairs={{0,2},{1,3},{2,0},{3,1},{4,6},{5,7},{6,4},{7,5},{8,10},{9,11},{10,... | collective-permute-start | bytes 983048 | tf_op jit(solution)/shard_map/ppermute | solution.py:430
  66.3 6.0 %collective-permute-start.25 = (bf16[1,320,512]{2,1,0:T(8,128)(2,1)S(1)}, bf16[1,320,512]{2,1,0:T(8,128)(2,1)S(1)}, u32[]{:S(2)}, u32[]{:S(2)}) collective-permute-start(bf16[1,320,512]{2,1,0:T(8,128)(2,1)S(1)} %get-tuple-element.86.refs_4_.refs_1_.refs_3_), channel_id=1, source_target_pairs={{0,1},{1,0},{2,3},{3,2},{4,5},{5,4},{6,7},{7,6},{8,9},{9,8},{10,11... | collective-permute-start | bytes 983048 | tf_op jit(solution)/shard_map/ppermute | solution.py:426
  73.5 16.5 %collective-permute-start.28 = (bf16[160,1536]{1,0:T(8,128)(2,1)S(1)}, bf16[160,1536]{1,0:T(8,128)(2,1)S(1)}, u32[]{:S(2)}, u32[]{:S(2)}) collective-permute-start(bf16[160,1536]{1,0:T(8,128)(2,1)S(1)} %get-tuple-element.94), channel_id=1, source_target_pairs={{0,8},{4,12},{8,0},{12,4},{16,24},{20,28},{24,16},{28,20},{1,9},{5... | collective-permute-start | bytes 1474568 | tf_op jit(solution)/shard_map/ppermute | solution.py:423
  74.0 10.1 %collective-permute-start.29 = (bf16[1,320,512]{2,1,0:T(8,128)(2,1)S(1)}, bf16[1,320,512]{2,1,0:T(8,128)(2,1)S(1)}, u32[]{:S(2)}, u32[]{:S(2)}) collective-permute-start(bf16[1,320,512]{2,1,0:T(8,128)(2,1)S(1)} %add.16.refs_4_), channel_id=1, source_target_pairs={{0,2},{1,3},{2,0},{3,1},{4,6},{5,7},{6,4},{7,5},{8,10},{9,11},{10,... | collective-permute-start | bytes 983048 | tf_op jit(solution)/shard_map/ppermute | solution.py:430
  81.8 13.7 %collective-permute-start.27 = (bf16[80,1536]{1,0:T(8,128)(2,1)S(1)}, bf16[80,1536]{1,0:T(8,128)(2,1)S(1)}, u32[]{:S(2)}, u32[]{:S(2)}) collective-permute-start(bf16[80,1536]{1,0:T(8,128)(2,1)S(1)} %get-tuple-element.93), channel_id=1, source_target_pairs={{0,8},{4,12},{8,0},{12,4},{16,24},{20,28},{24,16},{28,20},{1,9},{5... | collective-permute-start | bytes 737288 | tf_op jit(solution)/shard_map/ppermute | solution.py:423
  83.6 14.3 %collective-permute-start.32 = (bf16[160,1536]{1,0:T(8,128)(2,1)S(1)}, bf16[160,1536]{1,0:T(8,128)(2,1)S(1)}, u32[]{:S(2)}, u32[]{:S(2)}) collective-permute-start(bf16[160,1536]{1,0:T(8,128)(2,1)S(1)} %get-tuple-element.103), channel_id=1, source_target_pairs={{0,4},{4,0},{8,12},{12,8},{16,20},{20,16},{24,28},{28,24},{1,5},{5... | collective-permute-start | bytes 1474568 | tf_op jit(solution)/shard_map/ppermute | solution.py:423
  90.2 12.8 %collective-permute-start.31 = (bf16[80,1536]{1,0:T(8,128)(2,1)S(1)}, bf16[80,1536]{1,0:T(8,128)(2,1)S(1)}, u32[]{:S(2)}, u32[]{:S(2)}) collective-permute-start(bf16[80,1536]{1,0:T(8,128)(2,1)S(1)} %get-tuple-element.102), channel_id=1, source_target_pairs={{0,4},{4,0},{8,12},{12,8},{16,20},{20,16},{24,28},{28,24},{1,5},{5... | collective-permute-start | bytes 737288 | tf_op jit(solution)/shard_map/ppermute | solution.py:423
  91.8 18.3 %collective-permute-start.36 = (bf16[160,1536]{1,0:T(8,128)(2,1)S(1)}, bf16[160,1536]{1,0:T(8,128)(2,1)S(1)}, u32[]{:S(2)}, u32[]{:S(2)}) collective-permute-start(bf16[160,1536]{1,0:T(8,128)(2,1)S(1)} %get-tuple-element.111), channel_id=1, source_target_pairs={{0,8},{4,12},{8,0},{12,4},{16,24},{20,28},{24,16},{28,20},{1,9},{5... | collective-permute-start | bytes 1474568 | tf_op jit(solution)/shard_map/ppermute | solution.py:423
  95.6 22.3 %collective-permute-start.33 = (bf16[40,1536]{1,0:T(8,128)(2,1)S(1)}, bf16[40,1536]{1,0:T(8,128)(2,1)S(1)}, u32[]{:S(2)}, u32[]{:S(2)}) collective-permute-start(bf16[40,1536]{1,0:T(8,128)(2,1)S(1)} %get-tuple-element.107), channel_id=1, source_target_pairs={{0,16},{4,20},{8,24},{12,28},{16,0},{20,4},{24,8},{28,12},{1,17},{... | collective-permute-start | bytes 368648 | tf_op jit(solution)/shard_map/ppermute | solution.py:423
  98.0 17.6 %collective-permute-start.35 = (bf16[80,1536]{1,0:T(8,128)(2,1)S(1)}, bf16[80,1536]{1,0:T(8,128)(2,1)S(1)}, u32[]{:S(2)}, u32[]{:S(2)}) collective-permute-start(bf16[80,1536]{1,0:T(8,128)(2,1)S(1)} %get-tuple-element.109), channel_id=1, source_target_pairs={{0,8},{4,12},{8,0},{12,4},{16,24},{20,28},{24,16},{28,20},{1,9},{5... | collective-permute-start | bytes 737288 | tf_op jit(solution)/shard_map/ppermute | solution.py:423
  103.1 14.8 %collective-permute-start.34 = (bf16[40,1536]{1,0:T(8,128)(2,1)S(1)}, bf16[40,1536]{1,0:T(8,128)(2,1)S(1)}, u32[]{:S(2)}, u32[]{:S(2)}) collective-permute-start(bf16[40,1536]{1,0:T(8,128)(2,1)S(1)} %get-tuple-element.108), channel_id=1, source_target_pairs={{0,16},{4,20},{8,24},{12,28},{16,0},{20,4},{24,8},{28,12},{1,17},{... | collective-permute-start | bytes 368648 | tf_op jit(solution)/shard_map/ppermute | solution.py:423
  115.7 13.3 %collective-permute-start.38 = (bf16[40,1536]{1,0:T(8,128)(2,1)S(1)}, bf16[40,1536]{1,0:T(8,128)(2,1)S(1)}, u32[]{:S(2)}, u32[]{:S(2)}) collective-permute-start(bf16[40,1536]{1,0:T(8,128)(2,1)S(1)} %get-tuple-element.119), channel_id=1, source_target_pairs={{0,16},{4,20},{8,24},{12,28},{16,0},{20,4},{24,8},{28,12},{1,17},{... | collective-permute-start | bytes 368648 | tf_op jit(solution)/shard_map/ppermute | solution.py:423
  116.4 6.8 %collective-permute-start.37 = (bf16[80,1536]{1,0:T(8,128)(2,1)S(1)}, bf16[80,1536]{1,0:T(8,128)(2,1)S(1)}, u32[]{:S(2)}, u32[]{:S(2)}) collective-permute-start(bf16[80,1536]{1,0:T(8,128)(2,1)S(1)} %get-tuple-element.116), channel_id=1, source_target_pairs={{0,4},{4,0},{8,12},{12,8},{16,20},{20,16},{24,28},{28,24},{1,5},{5... | collective-permute-start | bytes 737288 | tf_op jit(solution)/shard_map/ppermute | solution.py:423
  123.3 6.4 %collective-permute-start.39 = (bf16[40,1536]{1,0:T(8,128)(2,1)S(1)}, bf16[40,1536]{1,0:T(8,128)(2,1)S(1)}, u32[]{:S(2)}, u32[]{:S(2)}) collective-permute-start(bf16[40,1536]{1,0:T(8,128)(2,1)S(1)} %get-tuple-element.120), channel_id=1, source_target_pairs={{0,16},{4,20},{8,24},{12,28},{16,0},{20,4},{24,8},{28,12},{1,17},{... | collective-permute-start | bytes 368648 | tf_op jit(solution)/shard_map/ppermute | solution.py:423
  (32 other events, 122.5 us)

commit v4 on v3

--- a/solution.py
+++ b/solution.py
@@ -29,6 +29,7 @@
 class Sequence:
     def __init__(self):
         self.last = None
+        self.flops = 10**10
 
     def __call__(self, kernel, *args, out_shape, name, in_specs=None, out_specs=None, scratch=(), aliases=None):
         n_in = len(args)
@@ -53,7 +54,7 @@
             scratch_shapes=list(scratch),
             input_output_aliases=aliases or {},
             compiler_params=pltpu.CompilerParams(vmem_limit_bytes=LIMIT * MIB),
-            cost_estimate=pl.CostEstimate(flops=10**10, bytes_accessed=10**8, transcendentals=0),
+            cost_estimate=pl.CostEstimate(flops=self.flops, bytes_accessed=1, transcendentals=0),
             name=name,
         )(*args)
         self.last = min(jax.tree.leaves(out), key=lambda o: o.size)
@@ -73,17 +74,22 @@
     return chosen, jnp.where(match, 1.0, 0.0)
 
 
-def rows_kernel(expert, ids, tokens, out):
+def rows_kernel(expert, ids, tokens, out, held, sem):
+    copy = pltpu.make_async_copy(tokens, held, sem)
+    copy.start()
     _, match = match_of(ids, expert)
-    out[...] = mm(match.astype(BF), tokens[...]).astype(BF)
+    copy.wait()
+    out[...] = mm(match.astype(BF), held[...]).astype(BF)
 
 
 def rows_of(run, ids, tokens, expert):
     return run(
         functools.partial(rows_kernel, expert),
         ids,
-        tokens,
+        pltpu.with_memory_space_constraint(tokens, pltpu.HBM),
+        in_specs=[VM, AN],
         out_shape=shape((CAP, tokens.shape[1])),
+        scratch=[pltpu.VMEM(tokens.shape, tokens.dtype), pltpu.SemaphoreType.DMA],
         name="rows",
     )
 
@@ -160,9 +166,10 @@
     )
 
 
-def back_kernel(parts, expert, transposed, swap, core, mine, other, *refs):
-    weights, keep, send = refs[:parts], refs[parts], refs[parts + 1]
-    h, d = keep.shape
+def back_kernel(parts, expert, transposed, swaps, core, mine, other, *refs):
+    weights, outs = refs[:parts], refs[parts:]
+    h, width = outs[0].shape
+    d = width * len(swaps)
     half = mine.shape[2]
     db = 256 if d % 256 == 0 else 128
     first = core[0] * half
@@ -180,23 +187,25 @@
                     val = mm(act[p], weights[p][expert, base, cols])
                 total = val if total is None else total + val
         total = total.astype(BF)
-        if swap:
+        at = j * db // width
+        if swaps[at]:
             total = swapped(total)
-        keep[:, cols] = total[:h]
-        send[:, cols] = total[h:]
-
-
-def back(run, core, mine, other, weights, expert, transposed, swap=False):
+        cols = slice(j * db - at * width, (j + 1) * db - at * width)
+        outs[2 * at][:, cols] = total[:h]
+        outs[2 * at + 1][:, cols] = total[h:]
+
+
+def back(run, core, mine, other, weights, expert, transposed, swaps):
     parts, r, _ = mine.shape
     d = weights[0].shape[1] if transposed else weights[0].shape[2]
     return run(
-        functools.partial(back_kernel, parts, expert, transposed, swap),
+        functools.partial(back_kernel, parts, expert, transposed, swaps),
         core,
         mine,
         other,
         *weights,
         in_specs=[SM] + [VM] * (2 + parts),
-        out_shape=[shape((r // 2, d))] * 2,
+        out_shape=[shape((r // 2, d // len(swaps)))] * (2 * len(swaps)),
         name="row_grad_part" if transposed else "expert_part",
     )
 
@@ -477,13 +486,13 @@
             return mine, swap_core(mine)
 
         def expert_out(hidden, e, mixed):
-            pair = back(run, core, *hidden, [down_weight], e, False, mixed)
+            pair = back(run, core, *hidden, [down_weight], e, False, (mixed,))
             gen = scatter(run, *pair, mixed_order if mixed else plain)
             next(gen)
             return gen
 
         def row_out(grads, e, mixed):
-            pair = back(run, core, *grads, [gate_weight, up_weight], e, True, mixed)
+            pair = back(run, core, *grads, [gate_weight, up_weight], e, True, (mixed,))
             gen = scatter(run, *pair, mixed_order if mixed else plain)
             next(gen)
             return gen
@@ -525,7 +534,6 @@
         hp1 = grad_part(scaled1, 1)
         o1 = expert_out(hidden1, 1, True)
         h1 = across(hp1)
-        pick, weight = (pick0, pick1), (weight0, weight1)
         d0 = grads_pair(sums0, h0)
         down = weight_grads(run, core, *scaled0, *hidden0, 0, 0, experts, None, False)
         q0 = row_out(d0, 0, False)
@@ -542,10 +550,10 @@
         next(q1)
         gate = weight_grads(run, core, *rows1, *d1, 0, 1, experts, gate, True)
         row0 = steps(q0, near - 1)
-        mixed = combine(run, pick, weight, (out0, out1), True)
         row1 = steps(q1, near - 1)
         up = weight_grads(run, core, *rows1, *d1, 1, 1, experts, up, True)
-        token_grad = combine(run, pick, weight, (row0, row1), False)
+        mixed = combine(run, (pick0, pick1), (weight0, weight1), (out0, out1), True)
+        token_grad = combine(run, (pick0, pick1), (weight0, weight1), (row0, row1), False)
         return mixed, token_grad, gate, up, down
 
     return local

time: 132 us -> 131 us (level)
  local copies, waits for them, and re-layouts: 3.32 us -> 1.27 us
  Pallas kernels: 40.6 us -> 42.5 us
  waiting for transfers between devices: 40 us -> 38.4 us
    unnamed x48 -> x44, local copies, waits for them, and re-layouts: 3.32 us -> 1.27 us
    pallas_call x51, Pallas kernels: 40.6 us -> 42.5 us  [__call__(): pl.pallas_call(body, in_specs=in_specs, out_specs=out_specs, out_shape=ou...]
  transfers between devices with their start and end apart: 40 -> 40, of which waited for: 15 -> 15; matrix products, arithmetic and copies ran while one was open for 0% -> 0% of each run, Pallas kernels for 29% -> 30%
where the time goes in v4:
time: 131 us
  starting transfers between devices  46.9 us (36%)
  Pallas kernels  42.5 us (32%)
  waiting for transfers between devices  38.4 us (29%)
  between operations  1.5 us (1%)
    pallas_call x51, Pallas kernels, __call__(): pl.pallas_call(body, in_specs=in_specs, out_specs=out_specs, out_shape=ou...  42.5 us
    ppermute x24, starting transfers between devices, swap(): return lax.ppermute(x, 'dp', [(i, i ^ 1 << bit) for i in range(n_dp)])  36.9 us
    ppermute x24, waiting for transfers between devices, swap(): return lax.ppermute(x, 'dp', [(i, i ^ 1 << bit) for i in range(n_dp)])  33 us
    ppermute x6, starting transfers between devices, shift_x(): lax.ppermute(x, 'own', [(i, (i + 2 * k) % n_own) for i in range(n_own)])  9.31 us
    ppermute x6, waiting for transfers between devices, shift_x(): lax.ppermute(x, 'own', [(i, (i + 2 * k) % n_own) for i in range(n_own)])  3.71 us
  transfers between devices with their start and end apart: 40, of which 15 were waited for; matrix products, arithmetic and copies ran while one was open for 0% of the time, Pallas kernels for 30%

profile of v4, /device:TPU:0, one launch (start us, length us, event | category | flops | bytes accessed | tf_op | source)
XLA Modules:
  0.0 130.6 jit_solution(6330774663087892835)
XLA Ops:
  2.5 4.1 %collective-permute-start = (bf16[40,1536]{1,0:T(8,128)(2,1)S(1)}, bf16[40,1536]{1,0:T(8,128)(2,1)S(1)}, u32[]{:S(2)}, u32[]{:S(2)}) collective-permute-start(bf16[40,1536]{1,0:T(8,128)(2,1)S(1)} %rows.2.refs_0_.refs_2_), channel_id=1, source_target_pairs={{0,16},{4,20},{8,24},{12,28},{16,0},{20,4},{24,8},{28,12},{1,17},{... | collective-permute-start | bytes 368648 | tf_op jit(solution)/shard_map/ppermute | solution.py:432
  6.6 6.0 %collective-permute-done.refs_1_ = bf16[40,1536]{1,0:T(8,128)(2,1)S(1)} collective-permute-done((bf16[40,1536]{1,0:T(8,128)(2,1)S(1)}, bf16[40,1536]{1,0:T(8,128)(2,1)S(1)}, u32[]{:S(2)}, u32[]{:S(2)}) %collective-permute-start) | collective-permute-done | bytes 122912 | tf_op jit(solution)/shard_map/ppermute | solution.py:432
  14.8 3.4 %collective-permute-start.1 = (bf16[40,1536]{1,0:T(8,128)(2,1)S(1)}, bf16[40,1536]{1,0:T(8,128)(2,1)S(1)}, u32[]{:S(2)}, u32[]{:S(2)}) collective-permute-start(bf16[40,1536]{1,0:T(8,128)(2,1)S(1)} %rows.3.refs_2_.refs_0_), channel_id=1, source_target_pairs={{0,16},{4,20},{8,24},{12,28},{16,0},{20,4},{24,8},{28,12},{1,17},{... | collective-permute-start | bytes 368648 | tf_op jit(solution)/shard_map/ppermute | solution.py:432
  18.2 4.2 %collective-permute-done.2.refs_1_ = bf16[80,1536]{1,0:T(8,128)(2,1)S(1)} collective-permute-done((bf16[80,1536]{1,0:T(8,128)(2,1)S(1)}, bf16[80,1536]{1,0:T(8,128)(2,1)S(1)}, u32[]{:S(2)}, u32[]{:S(2)}) %collective-permute-start.2) | collective-permute-done | bytes 245792 | tf_op jit(solution)/shard_map/ppermute | solution.py:432
  26.5 4.3 %collective-permute-start.4 = (bf16[40,1536]{1,0:T(8,128)(2,1)S(1)}, bf16[40,1536]{1,0:T(8,128)(2,1)S(1)}, u32[]{:S(2)}, u32[]{:S(2)}) collective-permute-start(bf16[40,1536]{1,0:T(8,128)(2,1)S(1)} %get-tuple-element.68.refs_0_), channel_id=1, source_target_pairs={{0,16},{4,20},{8,24},{12,28},{16,0},{20,4},{24,8},{28,12},{1,17},{... | collective-permute-start | bytes 368648 | tf_op jit(solution)/shard_map/ppermute | solution.py:432
  33.0 4.1 %collective-permute-done.4.refs_1_ = bf16[40,1536]{1,0:T(8,128)(2,1)S(1)} collective-permute-done((bf16[40,1536]{1,0:T(8,128)(2,1)S(1)}, bf16[40,1536]{1,0:T(8,128)(2,1)S(1)}, u32[]{:S(2)}, u32[]{:S(2)}) %collective-permute-start.4) | collective-permute-done | bytes 122912 | tf_op jit(solution)/shard_map/ppermute | solution.py:432
  39.1 2.9 %collective-permute-start.11 = (bf16[40,1536]{1,0:T(8,128)(2,1)S(1)}, bf16[40,1536]{1,0:T(8,128)(2,1)S(1)}, u32[]{:S(2)}, u32[]{:S(2)}) collective-permute-start(bf16[40,1536]{1,0:T(8,128)(2,1)S(1)} %get-tuple-element.75.refs_0_), channel_id=1, source_target_pairs={{0,16},{4,20},{8,24},{12,28},{16,0},{20,4},{24,8},{28,12},{1,17},{... | collective-permute-start | bytes 368648 | tf_op jit(solution)/shard_map/ppermute | solution.py:432
  47.6 1.6 %collective-permute-start.19 = (bf16[2,160,512]{2,1,0:T(8,128)(2,1)S(1)}, bf16[2,160,512]{2,1,0:T(8,128)(2,1)S(1)}, u32[]{:S(2)}, u32[]{:S(2)}) collective-permute-start(bf16[2,160,512]{2,1,0:T(8,128)(2,1)S(1)} %add.13.refs_2_), channel_id=1, source_target_pairs={{0,2},{1,3},{2,0},{3,1},{4,6},{5,7},{6,4},{7,5},{8,10},{9,11},{10,... | collective-permute-start | bytes 983048 | tf_op jit(solution)/shard_map/ppermute | solution.py:439
  50.6 2.0 %collective-permute-done.9.refs_3_ = bf16[2,160,512]{2,1,0:T(8,128)(2,1)S(1)} collective-permute-done((bf16[2,160,512]{2,1,0:T(8,128)(2,1)S(1)}, bf16[2,160,512]{2,1,0:T(8,128)(2,1)S(1)}, u32[]{:S(2)}, u32[]{:S(2)}) %collective-permute-start.9) | collective-permute-done | bytes 327712 | tf_op jit(solution)/shard_map/ppermute | solution.py:439
  54.7 1.7 %collective-permute-done.15.refs_1_ = bf16[80,1536]{1,0:T(8,128)(2,1)S(1)} collective-permute-done((bf16[80,1536]{1,0:T(8,128)(2,1)S(1)}, bf16[80,1536]{1,0:T(8,128)(2,1)S(1)}, u32[]{:S(2)}, u32[]{:S(2)}) %collective-permute-start.15) | collective-permute-done | bytes 245792 | tf_op jit(solution)/shard_map/ppermute | solution.py:432
  58.2 1.6 %collective-permute-start.17 = (bf16[160,1536]{1,0:T(8,128)(2,1)S(1)}, bf16[160,1536]{1,0:T(8,128)(2,1)S(1)}, u32[]{:S(2)}, u32[]{:S(2)}) collective-permute-start(bf16[160,1536]{1,0:T(8,128)(2,1)S(1)} %get-tuple-element.82), channel_id=1, source_target_pairs={{0,4},{4,0},{8,12},{12,8},{16,20},{20,16},{24,28},{28,24},{1,5},{5... | collective-permute-start | bytes 1474568 | tf_op jit(solution)/shard_map/ppermute | solution.py:432
  61.2 1.6 %collective-permute-done.20.refs_1_.refs_2_ = bf16[1,320,512]{2,1,0:T(8,128)(2,1)S(1)} collective-permute-done((bf16[1,320,512]{2,1,0:T(8,128)(2,1)S(1)}, bf16[1,320,512]{2,1,0:T(8,128)(2,1)S(1)}, u32[]{:S(2)}, u32[]{:S(2)}) %collective-permute-start.20) | collective-permute-done | bytes 327712 | tf_op jit(solution)/shard_map/ppermute | solution.py:435
  64.4 1.7 %collective-permute-done.23.refs_3_ = bf16[2,160,512]{2,1,0:T(8,128)(2,1)S(1)} collective-permute-done((bf16[2,160,512]{2,1,0:T(8,128)(2,1)S(1)}, bf16[2,160,512]{2,1,0:T(8,128)(2,1)S(1)}, u32[]{:S(2)}, u32[]{:S(2)}) %collective-permute-start.23) | collective-permute-done | bytes 327712 | tf_op jit(solution)/shard_map/ppermute | solution.py:439
  66.5 4.1 %collective-permute-done.22.refs_2_ = bf16[160,1536]{1,0:T(8,128)(2,1)S(1)} collective-permute-done((bf16[160,1536]{1,0:T(8,128)(2,1)S(1)}, bf16[160,1536]{1,0:T(8,128)(2,1)S(1)}, u32[]{:S(2)}, u32[]{:S(2)}) %collective-permute-start.22) | collective-permute-done | bytes 491552 | tf_op jit(solution)/shard_map/ppermute | solution.py:432
  73.6 1.6 %collective-permute-start.29 = (bf16[1,320,512]{2,1,0:T(8,128)(2,1)S(1)}, bf16[1,320,512]{2,1,0:T(8,128)(2,1)S(1)}, u32[]{:S(2)}, u32[]{:S(2)}) collective-permute-start(bf16[1,320,512]{2,1,0:T(8,128)(2,1)S(1)} %add.16.refs_4_), channel_id=1, source_target_pairs={{0,2},{1,3},{2,0},{3,1},{4,6},{5,7},{6,4},{7,5},{8,10},{9,11},{10,... | collective-permute-start | bytes 983048 | tf_op jit(solution)/shard_map/ppermute | solution.py:439
  75.9 3.2 %weight_grad.6 = (f32[2,1024,1536]{2,1,0:T(8,128)}, f32[8,128]{1,0:T(8,128)S(1)}) custom-call(s32[1]{0:T(128)} %bitcast.2.refs_0_, bf16[160,1536]{1,0:T(8,128)(2,1)S(1)} %join.13.refs_2_.refs_1_, bf16[160,1536]{1,0:T(8,128)(2,1)S(1)} %collective-permute-done.18.refs_2_, bf16[1,320,512]{2,1,0:T(8,128)(2,1)S(1)} %get-tuple-element.79.refs_2_.refs_1_.refs_3_, ...), custom_call_target="tpu_custom_call" | custom-call | flops 10000000000 | bytes 1 | tf_op jit(solution)/shard_map/weight_grad/pallas_call | solution.py:49
  79.0 2.2 %row_grad_part.2 = (bf16[160,1536]{1,0:T(8,128)(2,1)S(1)}, bf16[160,1536]{1,0:T(8,128)(2,1)S(1)}) custom-call(s32[1]{0:T(128)} %bitcast.2.refs_0_, bf16[2,320,512]{2,1,0:T(8,128)(2,1)S(1)} %gate_up_grads.2.refs_5_.refs_1_.refs_3_, bf16[2,320,512]{2,1,0:T(8,128)(2,1)S(1)} %collective-permute-done.26.refs_2_.refs_4_, bf16[2,1536,1024]{2,1,0:T(8,128)(2,1)S(1)} %bitcast.6, ...), custom_call_target="tpu_custom_call" | custom-call | flops 10000000000 | bytes 1 | tf_op jit(solution)/shard_map/row_grad_part/pallas_call | solution.py:49
  81.4 1.8 %collective-permute-start.27 = (bf16[80,1536]{1,0:T(8,128)(2,1)S(1)}, bf16[80,1536]{1,0:T(8,128)(2,1)S(1)}, u32[]{:S(2)}, u32[]{:S(2)}) collective-permute-start(bf16[80,1536]{1,0:T(8,128)(2,1)S(1)} %get-tuple-element.93), channel_id=1, source_target_pairs={{0,8},{4,12},{8,0},{12,4},{16,24},{20,28},{24,16},{28,20},{1,9},{5... | collective-permute-start | bytes 737288 | tf_op jit(solution)/shard_map/ppermute | solution.py:432
  84.8 3.2 %weight_grad.7 = (f32[2,1024,1536]{2,1,0:T(8,128)}, f32[8,128]{1,0:T(8,128)S(1)}) custom-call(s32[1]{0:T(128)} %bitcast.2.refs_0_, bf16[160,1536]{1,0:T(8,128)(2,1)S(1)} %join.15.refs_4_.refs_1_, bf16[160,1536]{1,0:T(8,128)(2,1)S(1)} %collective-permute-done.22.refs_2_, ...), custom_call_target="tpu_custom_call", output_to_operand_aliasing={{0}: (5, {})} | custom-call | flops 10000000000 | bytes 1 | tf_op jit(solution)/shard_map/weight_grad/pallas_call | solution.py:49
  88.0 2.2 %row_grad_part.3 = (bf16[160,1536]{1,0:T(8,128)(2,1)S(1)}, bf16[160,1536]{1,0:T(8,128)(2,1)S(1)}) custom-call(s32[1]{0:T(128)} %bitcast.2.refs_0_, bf16[2,320,512]{2,1,0:T(8,128)(2,1)S(1)} %gate_up_grads.3.refs_6_.refs_1_.refs_3_, bf16[2,320,512]{2,1,0:T(8,128)(2,1)S(1)} %collective-permute-done.30.refs_2_.refs_4_, bf16[2,1536,1024]{2,1,0:T(8,128)(2,1)S(1)} %bitcast.6, ...), custom_call_target="tpu_custom_call" | custom-call | flops 10000000000 | bytes 1 | tf_op jit(solution)/shard_map/row_grad_part/pallas_call | solution.py:49
  92.8 3.2 %weight_grad.8 = (f32[2,1536,1024]{2,1,0:T(8,128)}, f32[8,128]{1,0:T(8,128)S(1)}) custom-call(s32[1]{0:T(128)} %bitcast.2.refs_0_, bf16[160,1536]{1,0:T(8,128)(2,1)S(1)} %copy-done.5, bf16[160,1536]{1,0:T(8,128)(2,1)S(1)} %copy-done.7, bf16[2,320,512]{2,1,0:T(8,128)(2,1)S(1)} %gate_up_grads.2.refs_5_.refs_1_.refs_3_, ...), custom_call_target="tpu_custom_call" | custom-call | flops 10000000000 | bytes 1 | tf_op jit(solution)/shard_map/weight_grad/pallas_call | solution.py:49
  96.1 2.2 %collective-permute-start.33 = (bf16[40,1536]{1,0:T(8,128)(2,1)S(1)}, bf16[40,1536]{1,0:T(8,128)(2,1)S(1)}, u32[]{:S(2)}, u32[]{:S(2)}) collective-permute-start(bf16[40,1536]{1,0:T(8,128)(2,1)S(1)} %get-tuple-element.107), channel_id=1, source_target_pairs={{0,16},{4,20},{8,24},{12,28},{16,0},{20,4},{24,8},{28,12},{1,17},{... | collective-permute-start | bytes 368648 | tf_op jit(solution)/shard_map/ppermute | solution.py:432
  98.4 1.6 %collective-permute-start.37 = (bf16[80,1536]{1,0:T(8,128)(2,1)S(1)}, bf16[80,1536]{1,0:T(8,128)(2,1)S(1)}, u32[]{:S(2)}, u32[]{:S(2)}) collective-permute-start(bf16[80,1536]{1,0:T(8,128)(2,1)S(1)} %get-tuple-element.113), channel_id=1, source_target_pairs={{0,8},{4,12},{8,0},{12,4},{16,24},{20,28},{24,16},{28,20},{1,9},{5... | collective-permute-start | bytes 737288 | tf_op jit(solution)/shard_map/ppermute | solution.py:432
  100.0 3.2 %weight_grad.9 = (f32[2,1536,1024]{2,1,0:T(8,128)}, f32[8,128]{1,0:T(8,128)S(1)}) custom-call(s32[1]{0:T(128)} %bitcast.2.refs_0_, bf16[160,1536]{1,0:T(8,128)(2,1)S(1)} %copy-done.5, bf16[160,1536]{1,0:T(8,128)(2,1)S(1)} %copy-done.7, bf16[2,320,512]{2,1,0:T(8,128)(2,1)S(1)} %gate_up_grads.2.refs_5_.refs_1_.refs_3_, ...), custom_call_target="tpu_custom_call" | custom-call | flops 10000000000 | bytes 1 | tf_op jit(solution)/shard_map/weight_grad/pallas_call | solution.py:49
  104.4 4.8 %collective-permute-done.35.refs_1_ = bf16[160,1536]{1,0:T(8,128)(2,1)S(1)} collective-permute-done((bf16[160,1536]{1,0:T(8,128)(2,1)S(1)}, bf16[160,1536]{1,0:T(8,128)(2,1)S(1)}, u32[]{:S(2)}, u32[]{:S(2)}) %collective-permute-start.35) | collective-permute-done | bytes 491552 | tf_op jit(solution)/shard_map/ppermute | solution.py:432
  109.3 1.8 %collective-permute-start.36 = (bf16[80,1536]{1,0:T(8,128)(2,1)S(1)}, bf16[80,1536]{1,0:T(8,128)(2,1)S(1)}, u32[]{:S(2)}, u32[]{:S(2)}) collective-permute-start(bf16[80,1536]{1,0:T(8,128)(2,1)S(1)} %get-tuple-element.112), channel_id=1, source_target_pairs={{0,4},{4,0},{8,12},{12,8},{16,20},{20,16},{24,28},{28,24},{1,5},{5... | collective-permute-start | bytes 737288 | tf_op jit(solution)/shard_map/ppermute | solution.py:432
  111.1 3.4 %weight_grad.10 = (f32[2,1536,1024]{2,1,0:T(8,128)}, f32[8,128]{1,0:T(8,128)S(1)}) custom-call(s32[1]{0:T(128)} %bitcast.2.refs_0_, bf16[160,1536]{1,0:T(8,128)(2,1)S(1)} %copy-done.1, bf16[160,1536]{1,0:T(8,128)(2,1)S(1)} %copy-done.3, bf16[2,320,512]{2,1,0:T(8,128)(2,1)S(1)} %gate_up_grads.3.refs_6_.refs_1_.refs_3_, ...), custom_call_target="tpu_custom_call", output_to_operand_aliasing={{0}: (5, {})} | custom-call | flops 10000000000 | bytes 1 | tf_op jit(solution)/shard_map/weight_grad/pallas_call | solution.py:49
  115.3 1.8 %collective-permute-start.38 = (bf16[40,1536]{1,0:T(8,128)(2,1)S(1)}, bf16[40,1536]{1,0:T(8,128)(2,1)S(1)}, u32[]{:S(2)}, u32[]{:S(2)}) collective-permute-start(bf16[40,1536]{1,0:T(8,128)(2,1)S(1)} %get-tuple-element.120), channel_id=1, source_target_pairs={{0,16},{4,20},{8,24},{12,28},{16,0},{20,4},{24,8},{28,12},{1,17},{... | collective-permute-start | bytes 368648 | tf_op jit(solution)/shard_map/ppermute | solution.py:432
  118.4 3.2 %weight_grad.11 = (f32[2,1536,1024]{2,1,0:T(8,128)}, f32[8,128]{1,0:T(8,128)S(1)}) custom-call(s32[1]{0:T(128)} %bitcast.2.refs_0_, bf16[160,1536]{1,0:T(8,128)(2,1)S(1)} %copy-done.1, bf16[160,1536]{1,0:T(8,128)(2,1)S(1)} %copy-done.3, bf16[2,320,512]{2,1,0:T(8,128)(2,1)S(1)} %gate_up_grads.3.refs_6_.refs_1_.refs_3_, ...), custom_call_target="tpu_custom_call", output_to_operand_aliasing={{0}: (5, {})} | custom-call | flops 10000000000 | bytes 1 | tf_op jit(solution)/shard_map/weight_grad/pallas_call | solution.py:49
  122.7 4.0 %collective-permute-done.38.refs_6_ = bf16[40,1536]{1,0:T(8,128)(2,1)S(1)} collective-permute-done((bf16[40,1536]{1,0:T(8,128)(2,1)S(1)}, bf16[40,1536]{1,0:T(8,128)(2,1)S(1)}, u32[]{:S(2)}, u32[]{:S(2)}) %collective-permute-start.38) | collective-permute-done | bytes 122912 | tf_op jit(solution)/shard_map/ppermute | solution.py:432
  126.7 2.0 %collective-permute-done.39.refs_7_ = bf16[40,1536]{1,0:T(8,128)(2,1)S(1)} collective-permute-done((bf16[40,1536]{1,0:T(8,128)(2,1)S(1)}, bf16[40,1536]{1,0:T(8,128)(2,1)S(1)}, u32[]{:S(2)}, u32[]{:S(2)}) %collective-permute-start.39) | collective-permute-done | bytes 122912 | tf_op jit(solution)/shard_map/ppermute | solution.py:432
  128.8 1.7 %combine.3 = (bf16[128,1536]{1,0:T(8,128)(2,1)}, f32[8,128]{1,0:T(8,128)}) custom-call(bf16[40,128]{1,0:T(8,128)(2,1)S(1)} %copy-done.13, bf16[40,128]{1,0:T(8,128)(2,1)S(1)} %copy-done.15, f32[40,128]{1,0:T(8,128)S(1)} %get-tuple-element.72.refs_2_, f32[40,128]{1,0:T(8,128)S(1)} %get-tuple-element.73.refs_3_, ...), custom_call_target="tpu_custom_call" | custom-call | flops 10000000000 | bytes 1 | tf_op jit(solution)/shard_map/combine/pallas_call | solution.py:49
  (146 shorter events, 39.1 us)
Async XLA Ops:
  2.5 10.1 %collective-permute-start = (bf16[40,1536]{1,0:T(8,128)(2,1)S(1)}, bf16[40,1536]{1,0:T(8,128)(2,1)S(1)}, u32[]{:S(2)}, u32[]{:S(2)}) collective-permute-start(bf16[40,1536]{1,0:T(8,128)(2,1)S(1)} %rows.2.refs_0_.refs_2_), channel_id=1, source_target_pairs={{0,16},{4,20},{8,24},{12,28},{16,0},{20,4},{24,8},{28,12},{1,17},{... | collective-permute-start | bytes 368648 | tf_op jit(solution)/shard_map/ppermute | solution.py:432
  12.6 9.8 %collective-permute-start.2 = (bf16[80,1536]{1,0:T(8,128)(2,1)S(1)}, bf16[80,1536]{1,0:T(8,128)(2,1)S(1)}, u32[]{:S(2)}, u32[]{:S(2)}) collective-permute-start(bf16[80,1536]{1,0:T(8,128)(2,1)S(1)} %join.8.refs_2_.refs_0_), channel_id=1, source_target_pairs={{0,8},{4,12},{8,0},{12,4},{16,24},{20,28},{24,16},{28,20},{1,9},{5... | collective-permute-start | bytes 737288 | tf_op jit(solution)/shard_map/ppermute | solution.py:432
  14.8 10.3 %collective-permute-start.1 = (bf16[40,1536]{1,0:T(8,128)(2,1)S(1)}, bf16[40,1536]{1,0:T(8,128)(2,1)S(1)}, u32[]{:S(2)}, u32[]{:S(2)}) collective-permute-start(bf16[40,1536]{1,0:T(8,128)(2,1)S(1)} %rows.3.refs_2_.refs_0_), channel_id=1, source_target_pairs={{0,16},{4,20},{8,24},{12,28},{16,0},{20,4},{24,8},{28,12},{1,17},{... | collective-permute-start | bytes 368648 | tf_op jit(solution)/shard_map/ppermute | solution.py:432
  22.5 14.9 %collective-permute-start.3 = (bf16[160,1536]{1,0:T(8,128)(2,1)S(1)}, bf16[160,1536]{1,0:T(8,128)(2,1)S(1)}, u32[]{:S(2)}, u32[]{:S(2)}) collective-permute-start(bf16[160,1536]{1,0:T(8,128)(2,1)S(1)} %join.9.refs_1_.refs_4_), channel_id=1, source_target_pairs={{0,4},{4,0},{8,12},{12,8},{16,20},{20,16},{24,28},{28,24},{1,5},{5... | collective-permute-start | bytes 1474568 | tf_op jit(solution)/shard_map/ppermute | solution.py:432
  25.2 7.2 %collective-permute-start.5 = (bf16[80,1536]{1,0:T(8,128)(2,1)S(1)}, bf16[80,1536]{1,0:T(8,128)(2,1)S(1)}, u32[]{:S(2)}, u32[]{:S(2)}) collective-permute-start(bf16[80,1536]{1,0:T(8,128)(2,1)S(1)} %join.10.refs_3_.refs_0_), channel_id=1, source_target_pairs={{0,8},{4,12},{8,0},{12,4},{16,24},{20,28},{24,16},{28,20},{1,9},{5... | collective-permute-start | bytes 737288 | tf_op jit(solution)/shard_map/ppermute | solution.py:432
  25.6 5.1 %collective-permute-start.6 = (bf16[2,160,512]{2,1,0:T(8,128)(2,1)S(1)}, bf16[2,160,512]{2,1,0:T(8,128)(2,1)S(1)}, u32[]{:S(2)}, u32[]{:S(2)}) collective-permute-start(bf16[2,160,512]{2,1,0:T(8,128)(2,1)S(1)} %get-tuple-element.69), channel_id=1, source_target_pairs={{0,1},{1,0},{2,3},{3,2},{4,5},{5,4},{6,7},{7,6},{8,9},{9,8},{10,11... | collective-permute-start | bytes 983048 | tf_op jit(solution)/shard_map/ppermute | solution.py:435
  26.5 10.7 %collective-permute-start.4 = (bf16[40,1536]{1,0:T(8,128)(2,1)S(1)}, bf16[40,1536]{1,0:T(8,128)(2,1)S(1)}, u32[]{:S(2)}, u32[]{:S(2)}) collective-permute-start(bf16[40,1536]{1,0:T(8,128)(2,1)S(1)} %get-tuple-element.68.refs_0_), channel_id=1, source_target_pairs={{0,16},{4,20},{8,24},{12,28},{16,0},{20,4},{24,8},{28,12},{1,17},{... | collective-permute-start | bytes 368648 | tf_op jit(solution)/shard_map/ppermute | solution.py:432
  30.8 12.8 %collective-permute-start.7 = (bf16[2,160,512]{2,1,0:T(8,128)(2,1)S(1)}, bf16[2,160,512]{2,1,0:T(8,128)(2,1)S(1)}, u32[]{:S(2)}, u32[]{:S(2)}) collective-permute-start(bf16[2,160,512]{2,1,0:T(8,128)(2,1)S(1)} %add.11.refs_2_), channel_id=1, source_target_pairs={{0,2},{1,3},{2,0},{3,1},{4,6},{5,7},{6,4},{7,5},{8,10},{9,11},{10,... | collective-permute-start | bytes 983048 | tf_op jit(solution)/shard_map/ppermute | solution.py:439
  32.4 16.9 %collective-permute-start.10 = (bf16[160,1536]{1,0:T(8,128)(2,1)S(1)}, bf16[160,1536]{1,0:T(8,128)(2,1)S(1)}, u32[]{:S(2)}, u32[]{:S(2)}) collective-permute-start(bf16[160,1536]{1,0:T(8,128)(2,1)S(1)} %join.11.refs_2_.refs_1_), channel_id=1, source_target_pairs={{0,4},{4,0},{8,12},{12,8},{16,20},{20,16},{24,28},{28,24},{1,5},{5... | collective-permute-start | bytes 1474568 | tf_op jit(solution)/shard_map/ppermute | solution.py:432
  37.1 9.2 %collective-permute-start.13 = (bf16[80,1536]{1,0:T(8,128)(2,1)S(1)}, bf16[80,1536]{1,0:T(8,128)(2,1)S(1)}, u32[]{:S(2)}, u32[]{:S(2)}) collective-permute-start(bf16[80,1536]{1,0:T(8,128)(2,1)S(1)} %join.12.refs_4_.refs_0_), channel_id=1, source_target_pairs={{0,8},{4,12},{8,0},{12,4},{16,24},{20,28},{24,16},{28,20},{1,9},{5... | collective-permute-start | bytes 737288 | tf_op jit(solution)/shard_map/ppermute | solution.py:432
  39.1 10.1 %collective-permute-start.11 = (bf16[40,1536]{1,0:T(8,128)(2,1)S(1)}, bf16[40,1536]{1,0:T(8,128)(2,1)S(1)}, u32[]{:S(2)}, u32[]{:S(2)}) collective-permute-start(bf16[40,1536]{1,0:T(8,128)(2,1)S(1)} %get-tuple-element.75.refs_0_), channel_id=1, source_target_pairs={{0,16},{4,20},{8,24},{12,28},{16,0},{20,4},{24,8},{28,12},{1,17},{... | collective-permute-start | bytes 368648 | tf_op jit(solution)/shard_map/ppermute | solution.py:432
  42.0 10.6 %collective-permute-start.9 = (bf16[2,160,512]{2,1,0:T(8,128)(2,1)S(1)}, bf16[2,160,512]{2,1,0:T(8,128)(2,1)S(1)}, u32[]{:S(2)}, u32[]{:S(2)}) collective-permute-start(bf16[2,160,512]{2,1,0:T(8,128)(2,1)S(1)} %add.12.refs_3_), channel_id=1, source_target_pairs={{0,2},{1,3},{2,0},{3,1},{4,6},{5,7},{6,4},{7,5},{8,10},{9,11},{10,... | collective-permute-start | bytes 983048 | tf_op jit(solution)/shard_map/ppermute | solution.py:439
  46.4 13.5 %collective-permute-start.18 = (bf16[160,1536]{1,0:T(8,128)(2,1)S(1)}, bf16[160,1536]{1,0:T(8,128)(2,1)S(1)}, u32[]{:S(2)}, u32[]{:S(2)}) collective-permute-start(bf16[160,1536]{1,0:T(8,128)(2,1)S(1)} %join.13.refs_2_.refs_1_), channel_id=1, source_target_pairs={{0,4},{4,0},{8,12},{12,8},{16,20},{20,16},{24,28},{28,24},{1,5},{5... | collective-permute-start | bytes 1474568 | tf_op jit(solution)/shard_map/ppermute | solution.py:432
  47.6 12.1 %collective-permute-start.19 = (bf16[2,160,512]{2,1,0:T(8,128)(2,1)S(1)}, bf16[2,160,512]{2,1,0:T(8,128)(2,1)S(1)}, u32[]{:S(2)}, u32[]{:S(2)}) collective-permute-start(bf16[2,160,512]{2,1,0:T(8,128)(2,1)S(1)} %add.13.refs_2_), channel_id=1, source_target_pairs={{0,2},{1,3},{2,0},{3,1},{4,6},{5,7},{6,4},{7,5},{8,10},{9,11},{10,... | collective-permute-start | bytes 983048 | tf_op jit(solution)/shard_map/ppermute | solution.py:439
  49.2 7.1 %collective-permute-start.15 = (bf16[80,1536]{1,0:T(8,128)(2,1)S(1)}, bf16[80,1536]{1,0:T(8,128)(2,1)S(1)}, u32[]{:S(2)}, u32[]{:S(2)}) collective-permute-start(bf16[80,1536]{1,0:T(8,128)(2,1)S(1)} %join.14.refs_4_.refs_0_), channel_id=1, source_target_pairs={{0,8},{4,12},{8,0},{12,4},{16,24},{20,28},{24,16},{28,20},{1,9},{5... | collective-permute-start | bytes 737288 | tf_op jit(solution)/shard_map/ppermute | solution.py:432
  53.1 13.0 %collective-permute-start.23 = (bf16[2,160,512]{2,1,0:T(8,128)(2,1)S(1)}, bf16[2,160,512]{2,1,0:T(8,128)(2,1)S(1)}, u32[]{:S(2)}, u32[]{:S(2)}) collective-permute-start(bf16[2,160,512]{2,1,0:T(8,128)(2,1)S(1)} %add.14.refs_2_), channel_id=1, source_target_pairs={{0,2},{1,3},{2,0},{3,1},{4,6},{5,7},{6,4},{7,5},{8,10},{9,11},{10,... | collective-permute-start | bytes 983048 | tf_op jit(solution)/shard_map/ppermute | solution.py:439
  56.4 14.2 %collective-permute-start.22 = (bf16[160,1536]{1,0:T(8,128)(2,1)S(1)}, bf16[160,1536]{1,0:T(8,128)(2,1)S(1)}, u32[]{:S(2)}, u32[]{:S(2)}) collective-permute-start(bf16[160,1536]{1,0:T(8,128)(2,1)S(1)} %join.15.refs_4_.refs_1_), channel_id=1, source_target_pairs={{0,4},{4,0},{8,12},{12,8},{16,20},{20,16},{24,28},{28,24},{1,5},{5... | collective-permute-start | bytes 1474568 | tf_op jit(solution)/shard_map/ppermute | solution.py:432
  58.2 23.1 %collective-permute-start.17 = (bf16[160,1536]{1,0:T(8,128)(2,1)S(1)}, bf16[160,1536]{1,0:T(8,128)(2,1)S(1)}, u32[]{:S(2)}, u32[]{:S(2)}) collective-permute-start(bf16[160,1536]{1,0:T(8,128)(2,1)S(1)} %get-tuple-element.82), channel_id=1, source_target_pairs={{0,4},{4,0},{8,12},{12,8},{16,20},{20,16},{24,28},{28,24},{1,5},{5... | collective-permute-start | bytes 1474568 | tf_op jit(solution)/shard_map/ppermute | solution.py:432
  62.9 12.2 %collective-permute-start.21 = (bf16[1,320,512]{2,1,0:T(8,128)(2,1)S(1)}, bf16[1,320,512]{2,1,0:T(8,128)(2,1)S(1)}, u32[]{:S(2)}, u32[]{:S(2)}) collective-permute-start(bf16[1,320,512]{2,1,0:T(8,128)(2,1)S(1)} %add.15.refs_4_), channel_id=1, source_target_pairs={{0,2},{1,3},{2,0},{3,1},{4,6},{5,7},{6,4},{7,5},{8,10},{9,11},{10,... | collective-permute-start | bytes 983048 | tf_op jit(solution)/shard_map/ppermute | solution.py:439
  66.4 5.5 %collective-permute-start.25 = (bf16[1,320,512]{2,1,0:T(8,128)(2,1)S(1)}, bf16[1,320,512]{2,1,0:T(8,128)(2,1)S(1)}, u32[]{:S(2)}, u32[]{:S(2)}) collective-permute-start(bf16[1,320,512]{2,1,0:T(8,128)(2,1)S(1)} %get-tuple-element.86.refs_4_.refs_1_.refs_3_), channel_id=1, source_target_pairs={{0,1},{1,0},{2,3},{3,2},{4,5},{5,4},{6,7},{7,6},{8,9},{9,8},{10,11... | collective-permute-start | bytes 983048 | tf_op jit(solution)/shard_map/ppermute | solution.py:435
  73.1 17.2 %collective-permute-start.28 = (bf16[160,1536]{1,0:T(8,128)(2,1)S(1)}, bf16[160,1536]{1,0:T(8,128)(2,1)S(1)}, u32[]{:S(2)}, u32[]{:S(2)}) collective-permute-start(bf16[160,1536]{1,0:T(8,128)(2,1)S(1)} %get-tuple-element.94), channel_id=1, source_target_pairs={{0,8},{4,12},{8,0},{12,4},{16,24},{20,28},{24,16},{28,20},{1,9},{5... | collective-permute-start | bytes 1474568 | tf_op jit(solution)/shard_map/ppermute | solution.py:432
  73.6 10.7 %collective-permute-start.29 = (bf16[1,320,512]{2,1,0:T(8,128)(2,1)S(1)}, bf16[1,320,512]{2,1,0:T(8,128)(2,1)S(1)}, u32[]{:S(2)}, u32[]{:S(2)}) collective-permute-start(bf16[1,320,512]{2,1,0:T(8,128)(2,1)S(1)} %add.16.refs_4_), channel_id=1, source_target_pairs={{0,2},{1,3},{2,0},{3,1},{4,6},{5,7},{6,4},{7,5},{8,10},{9,11},{10,... | collective-permute-start | bytes 983048 | tf_op jit(solution)/shard_map/ppermute | solution.py:439
  81.4 14.6 %collective-permute-start.27 = (bf16[80,1536]{1,0:T(8,128)(2,1)S(1)}, bf16[80,1536]{1,0:T(8,128)(2,1)S(1)}, u32[]{:S(2)}, u32[]{:S(2)}) collective-permute-start(bf16[80,1536]{1,0:T(8,128)(2,1)S(1)} %get-tuple-element.93), channel_id=1, source_target_pairs={{0,8},{4,12},{8,0},{12,4},{16,24},{20,28},{24,16},{28,20},{1,9},{5... | collective-permute-start | bytes 737288 | tf_op jit(solution)/shard_map/ppermute | solution.py:432
  83.2 15.1 %collective-permute-start.32 = (bf16[160,1536]{1,0:T(8,128)(2,1)S(1)}, bf16[160,1536]{1,0:T(8,128)(2,1)S(1)}, u32[]{:S(2)}, u32[]{:S(2)}) collective-permute-start(bf16[160,1536]{1,0:T(8,128)(2,1)S(1)} %get-tuple-element.103), channel_id=1, source_target_pairs={{0,4},{4,0},{8,12},{12,8},{16,20},{20,16},{24,28},{28,24},{1,5},{5... | collective-permute-start | bytes 1474568 | tf_op jit(solution)/shard_map/ppermute | solution.py:432
  90.4 12.8 %collective-permute-start.31 = (bf16[80,1536]{1,0:T(8,128)(2,1)S(1)}, bf16[80,1536]{1,0:T(8,128)(2,1)S(1)}, u32[]{:S(2)}, u32[]{:S(2)}) collective-permute-start(bf16[80,1536]{1,0:T(8,128)(2,1)S(1)} %get-tuple-element.102), channel_id=1, source_target_pairs={{0,4},{4,0},{8,12},{12,8},{16,20},{20,16},{24,28},{28,24},{1,5},{5... | collective-permute-start | bytes 737288 | tf_op jit(solution)/shard_map/ppermute | solution.py:432
  91.3 17.9 %collective-permute-start.35 = (bf16[160,1536]{1,0:T(8,128)(2,1)S(1)}, bf16[160,1536]{1,0:T(8,128)(2,1)S(1)}, u32[]{:S(2)}, u32[]{:S(2)}) collective-permute-start(bf16[160,1536]{1,0:T(8,128)(2,1)S(1)} %get-tuple-element.110), channel_id=1, source_target_pairs={{0,8},{4,12},{8,0},{12,4},{16,24},{20,28},{24,16},{28,20},{1,9},{5... | collective-permute-start | bytes 1474568 | tf_op jit(solution)/shard_map/ppermute | solution.py:432
  96.1 25.5 %collective-permute-start.33 = (bf16[40,1536]{1,0:T(8,128)(2,1)S(1)}, bf16[40,1536]{1,0:T(8,128)(2,1)S(1)}, u32[]{:S(2)}, u32[]{:S(2)}) collective-permute-start(bf16[40,1536]{1,0:T(8,128)(2,1)S(1)} %get-tuple-element.107), channel_id=1, source_target_pairs={{0,16},{4,20},{8,24},{12,28},{16,0},{20,4},{24,8},{28,12},{1,17},{... | collective-permute-start | bytes 368648 | tf_op jit(solution)/shard_map/ppermute | solution.py:432
  98.4 16.8 %collective-permute-start.37 = (bf16[80,1536]{1,0:T(8,128)(2,1)S(1)}, bf16[80,1536]{1,0:T(8,128)(2,1)S(1)}, u32[]{:S(2)}, u32[]{:S(2)}) collective-permute-start(bf16[80,1536]{1,0:T(8,128)(2,1)S(1)} %get-tuple-element.113), channel_id=1, source_target_pairs={{0,8},{4,12},{8,0},{12,4},{16,24},{20,28},{24,16},{28,20},{1,9},{5... | collective-permute-start | bytes 737288 | tf_op jit(solution)/shard_map/ppermute | solution.py:432
  103.3 18.3 %collective-permute-start.34 = (bf16[40,1536]{1,0:T(8,128)(2,1)S(1)}, bf16[40,1536]{1,0:T(8,128)(2,1)S(1)}, u32[]{:S(2)}, u32[]{:S(2)}) collective-permute-start(bf16[40,1536]{1,0:T(8,128)(2,1)S(1)} %get-tuple-element.108), channel_id=1, source_target_pairs={{0,16},{4,20},{8,24},{12,28},{16,0},{20,4},{24,8},{28,12},{1,17},{... | collective-permute-start | bytes 368648 | tf_op jit(solution)/shard_map/ppermute | solution.py:432
  109.3 7.7 %collective-permute-start.36 = (bf16[80,1536]{1,0:T(8,128)(2,1)S(1)}, bf16[80,1536]{1,0:T(8,128)(2,1)S(1)}, u32[]{:S(2)}, u32[]{:S(2)}) collective-permute-start(bf16[80,1536]{1,0:T(8,128)(2,1)S(1)} %get-tuple-element.112), channel_id=1, source_target_pairs={{0,4},{4,0},{8,12},{12,8},{16,20},{20,16},{24,28},{28,24},{1,5},{5... | collective-permute-start | bytes 737288 | tf_op jit(solution)/shard_map/ppermute | solution.py:432
  115.3 11.4 %collective-permute-start.38 = (bf16[40,1536]{1,0:T(8,128)(2,1)S(1)}, bf16[40,1536]{1,0:T(8,128)(2,1)S(1)}, u32[]{:S(2)}, u32[]{:S(2)}) collective-permute-start(bf16[40,1536]{1,0:T(8,128)(2,1)S(1)} %get-tuple-element.120), channel_id=1, source_target_pairs={{0,16},{4,20},{8,24},{12,28},{16,0},{20,4},{24,8},{28,12},{1,17},{... | collective-permute-start | bytes 368648 | tf_op jit(solution)/shard_map/ppermute | solution.py:432
  117.1 11.6 %collective-permute-start.39 = (bf16[40,1536]{1,0:T(8,128)(2,1)S(1)}, bf16[40,1536]{1,0:T(8,128)(2,1)S(1)}, u32[]{:S(2)}, u32[]{:S(2)}) collective-permute-start(bf16[40,1536]{1,0:T(8,128)(2,1)S(1)} %get-tuple-element.121), channel_id=1, source_target_pairs={{0,16},{4,20},{8,24},{12,28},{16,0},{20,4},{24,8},{28,12},{1,17},{... | collective-permute-start | bytes 368648 | tf_op jit(solution)/shard_map/ppermute | solution.py:432
  (30 other events, 117.6 us)

commit v5 on v4

--- a/solution.py
+++ b/solution.py
@@ -543,11 +543,11 @@
         q1 = row_out(d1, 1, True)
         next(o1)
         gate = weight_grads(run, core, *rows0, *d0, 0, 0, experts, None, True)
-        out0 = steps(o0, near - 1)
         next(q0)
         up = weight_grads(run, core, *rows0, *d0, 1, 0, experts, None, True)
+        next(q1)
+        out0 = steps(o0, near - 1)
         out1 = steps(o1, near - 1)
-        next(q1)
         gate = weight_grads(run, core, *rows1, *d1, 0, 1, experts, gate, True)
         row0 = steps(q0, near - 1)
         row1 = steps(q1, near - 1)

time: 131 us -> 137 us (1.046)
  waiting for transfers between devices: 38.4 us -> 45.2 us
  starting transfers between devices: 46.9 us -> 44.7 us
    ppermute x24, waiting for transfers between devices: 33 us -> 39.8 us  [swap(): return lax.ppermute(x, 'dp', [(i, i ^ 1 << bit) for i in range(n_dp)])]
    ppermute x24, starting transfers between devices: 36.9 us -> 34.8 us  [swap(): return lax.ppermute(x, 'dp', [(i, i ^ 1 << bit) for i in range(n_dp)])]
  transfers between devices with their start and end apart: 40 -> 40, of which waited for: 15 -> 16; matrix products, arithmetic and copies ran while one was open for 0% -> 0% of each run, Pallas kernels for 30% -> 29%
where the time goes in v5:
time: 137 us; the launch traced here: 136 us
  waiting for transfers between devices  45.2 us (33%)
  starting transfers between devices  44.7 us (33%)
  Pallas kernels  42.6 us (31%)
  local copies, waits for them, and re-layouts  2.36 us (2%)
  between operations  1.5 us (1%)
    pallas_call x51, Pallas kernels, __call__(): pl.pallas_call(body, in_specs=in_specs, out_specs=out_specs, out_shape=ou...  42.6 us
    ppermute x24, waiting for transfers between devices, swap(): return lax.ppermute(x, 'dp', [(i, i ^ 1 << bit) for i in range(n_dp)])  39.8 us
    ppermute x24, starting transfers between devices, swap(): return lax.ppermute(x, 'dp', [(i, i ^ 1 << bit) for i in range(n_dp)])  34.8 us
    ppermute x6, starting transfers between devices, shift_x(): lax.ppermute(x, 'own', [(i, (i + 2 * k) % n_own) for i in range(n_own)])  9.31 us
    ppermute x6, waiting for transfers between devices, shift_x(): lax.ppermute(x, 'own', [(i, (i + 2 * k) % n_own) for i in range(n_own)])  3.71 us
  transfers between devices with their start and end apart: 40, of which 16 were waited for; matrix products, arithmetic and copies ran while one was open for 0% of the time, Pallas kernels for 29%

profile of v5, /device:TPU:0, one launch (start us, length us, event | category | flops | bytes accessed | tf_op | source)
XLA Modules:
  0.0 136.4 jit_solution(1762102985898983933)
XLA Ops:
  2.5 4.1 %collective-permute-start = (bf16[40,1536]{1,0:T(8,128)(2,1)S(1)}, bf16[40,1536]{1,0:T(8,128)(2,1)S(1)}, u32[]{:S(2)}, u32[]{:S(2)}) collective-permute-start(bf16[40,1536]{1,0:T(8,128)(2,1)S(1)} %rows.2.refs_0_.refs_2_), channel_id=1, source_target_pairs={{0,16},{4,20},{8,24},{12,28},{16,0},{20,4},{24,8},{28,12},{1,17},{... | collective-permute-start | bytes 368648 | tf_op jit(solution)/shard_map/ppermute | solution.py:432
  6.6 6.0 %collective-permute-done.refs_1_ = bf16[40,1536]{1,0:T(8,128)(2,1)S(1)} collective-permute-done((bf16[40,1536]{1,0:T(8,128)(2,1)S(1)}, bf16[40,1536]{1,0:T(8,128)(2,1)S(1)}, u32[]{:S(2)}, u32[]{:S(2)}) %collective-permute-start) | collective-permute-done | bytes 122912 | tf_op jit(solution)/shard_map/ppermute | solution.py:432
  14.8 3.4 %collective-permute-start.1 = (bf16[40,1536]{1,0:T(8,128)(2,1)S(1)}, bf16[40,1536]{1,0:T(8,128)(2,1)S(1)}, u32[]{:S(2)}, u32[]{:S(2)}) collective-permute-start(bf16[40,1536]{1,0:T(8,128)(2,1)S(1)} %rows.3.refs_2_.refs_0_), channel_id=1, source_target_pairs={{0,16},{4,20},{8,24},{12,28},{16,0},{20,4},{24,8},{28,12},{1,17},{... | collective-permute-start | bytes 368648 | tf_op jit(solution)/shard_map/ppermute | solution.py:432
  18.2 4.2 %collective-permute-done.2.refs_1_ = bf16[80,1536]{1,0:T(8,128)(2,1)S(1)} collective-permute-done((bf16[80,1536]{1,0:T(8,128)(2,1)S(1)}, bf16[80,1536]{1,0:T(8,128)(2,1)S(1)}, u32[]{:S(2)}, u32[]{:S(2)}) %collective-permute-start.2) | collective-permute-done | bytes 245792 | tf_op jit(solution)/shard_map/ppermute | solution.py:432
  26.5 4.3 %collective-permute-start.4 = (bf16[40,1536]{1,0:T(8,128)(2,1)S(1)}, bf16[40,1536]{1,0:T(8,128)(2,1)S(1)}, u32[]{:S(2)}, u32[]{:S(2)}) collective-permute-start(bf16[40,1536]{1,0:T(8,128)(2,1)S(1)} %get-tuple-element.68.refs_0_), channel_id=1, source_target_pairs={{0,16},{4,20},{8,24},{12,28},{16,0},{20,4},{24,8},{28,12},{1,17},{... | collective-permute-start | bytes 368648 | tf_op jit(solution)/shard_map/ppermute | solution.py:432
  30.8 1.6 %collective-permute-start.7 = (bf16[2,160,512]{2,1,0:T(8,128)(2,1)S(1)}, bf16[2,160,512]{2,1,0:T(8,128)(2,1)S(1)}, u32[]{:S(2)}, u32[]{:S(2)}) collective-permute-start(bf16[2,160,512]{2,1,0:T(8,128)(2,1)S(1)} %add.11.refs_2_), channel_id=1, source_target_pairs={{0,2},{1,3},{2,0},{3,1},{4,6},{5,7},{6,4},{7,5},{8,10},{9,11},{10,... | collective-permute-start | bytes 983048 | tf_op jit(solution)/shard_map/ppermute | solution.py:439
  33.0 4.1 %collective-permute-done.4.refs_1_ = bf16[40,1536]{1,0:T(8,128)(2,1)S(1)} collective-permute-done((bf16[40,1536]{1,0:T(8,128)(2,1)S(1)}, bf16[40,1536]{1,0:T(8,128)(2,1)S(1)}, u32[]{:S(2)}, u32[]{:S(2)}) %collective-permute-start.4) | collective-permute-done | bytes 122912 | tf_op jit(solution)/shard_map/ppermute | solution.py:432
  39.1 2.9 %collective-permute-start.11 = (bf16[40,1536]{1,0:T(8,128)(2,1)S(1)}, bf16[40,1536]{1,0:T(8,128)(2,1)S(1)}, u32[]{:S(2)}, u32[]{:S(2)}) collective-permute-start(bf16[40,1536]{1,0:T(8,128)(2,1)S(1)} %get-tuple-element.75.refs_0_), channel_id=1, source_target_pairs={{0,16},{4,20},{8,24},{12,28},{16,0},{20,4},{24,8},{28,12},{1,17},{... | collective-permute-start | bytes 368648 | tf_op jit(solution)/shard_map/ppermute | solution.py:432
  47.6 1.6 %collective-permute-start.19 = (bf16[2,160,512]{2,1,0:T(8,128)(2,1)S(1)}, bf16[2,160,512]{2,1,0:T(8,128)(2,1)S(1)}, u32[]{:S(2)}, u32[]{:S(2)}) collective-permute-start(bf16[2,160,512]{2,1,0:T(8,128)(2,1)S(1)} %add.13.refs_2_), channel_id=1, source_target_pairs={{0,2},{1,3},{2,0},{3,1},{4,6},{5,7},{6,4},{7,5},{8,10},{9,11},{10,... | collective-permute-start | bytes 983048 | tf_op jit(solution)/shard_map/ppermute | solution.py:439
  50.6 2.0 %collective-permute-done.9.refs_3_ = bf16[2,160,512]{2,1,0:T(8,128)(2,1)S(1)} collective-permute-done((bf16[2,160,512]{2,1,0:T(8,128)(2,1)S(1)}, bf16[2,160,512]{2,1,0:T(8,128)(2,1)S(1)}, u32[]{:S(2)}, u32[]{:S(2)}) %collective-permute-start.9) | collective-permute-done | bytes 327712 | tf_op jit(solution)/shard_map/ppermute | solution.py:439
  53.1 1.6 %collective-permute-start.23 = (bf16[2,160,512]{2,1,0:T(8,128)(2,1)S(1)}, bf16[2,160,512]{2,1,0:T(8,128)(2,1)S(1)}, u32[]{:S(2)}, u32[]{:S(2)}) collective-permute-start(bf16[2,160,512]{2,1,0:T(8,128)(2,1)S(1)} %add.14.refs_2_), channel_id=1, source_target_pairs={{0,2},{1,3},{2,0},{3,1},{4,6},{5,7},{6,4},{7,5},{8,10},{9,11},{10,... | collective-permute-start | bytes 983048 | tf_op jit(solution)/shard_map/ppermute | solution.py:439
  54.7 1.7 %collective-permute-done.15.refs_1_ = bf16[80,1536]{1,0:T(8,128)(2,1)S(1)} collective-permute-done((bf16[80,1536]{1,0:T(8,128)(2,1)S(1)}, bf16[80,1536]{1,0:T(8,128)(2,1)S(1)}, u32[]{:S(2)}, u32[]{:S(2)}) %collective-permute-start.15) | collective-permute-done | bytes 245792 | tf_op jit(solution)/shard_map/ppermute | solution.py:432
  58.2 1.6 %collective-permute-start.17 = (bf16[160,1536]{1,0:T(8,128)(2,1)S(1)}, bf16[160,1536]{1,0:T(8,128)(2,1)S(1)}, u32[]{:S(2)}, u32[]{:S(2)}) collective-permute-start(bf16[160,1536]{1,0:T(8,128)(2,1)S(1)} %get-tuple-element.82), channel_id=1, source_target_pairs={{0,4},{4,0},{8,12},{12,8},{16,20},{20,16},{24,28},{28,24},{1,5},{5... | collective-permute-start | bytes 1474568 | tf_op jit(solution)/shard_map/ppermute | solution.py:432
  61.2 1.6 %collective-permute-done.20.refs_1_.refs_2_ = bf16[1,320,512]{2,1,0:T(8,128)(2,1)S(1)} collective-permute-done((bf16[1,320,512]{2,1,0:T(8,128)(2,1)S(1)}, bf16[1,320,512]{2,1,0:T(8,128)(2,1)S(1)}, u32[]{:S(2)}, u32[]{:S(2)}) %collective-permute-start.20) | collective-permute-done | bytes 327712 | tf_op jit(solution)/shard_map/ppermute | solution.py:435
  64.4 1.7 %collective-permute-done.23.refs_3_ = bf16[2,160,512]{2,1,0:T(8,128)(2,1)S(1)} collective-permute-done((bf16[2,160,512]{2,1,0:T(8,128)(2,1)S(1)}, bf16[2,160,512]{2,1,0:T(8,128)(2,1)S(1)}, u32[]{:S(2)}, u32[]{:S(2)}) %collective-permute-start.23) | collective-permute-done | bytes 327712 | tf_op jit(solution)/shard_map/ppermute | solution.py:439
  66.5 4.1 %collective-permute-done.22.refs_2_ = bf16[160,1536]{1,0:T(8,128)(2,1)S(1)} collective-permute-done((bf16[160,1536]{1,0:T(8,128)(2,1)S(1)}, bf16[160,1536]{1,0:T(8,128)(2,1)S(1)}, u32[]{:S(2)}, u32[]{:S(2)}) %collective-permute-start.22) | collective-permute-done | bytes 491552 | tf_op jit(solution)/shard_map/ppermute | solution.py:432
  73.6 1.6 %collective-permute-start.28 = (bf16[1,320,512]{2,1,0:T(8,128)(2,1)S(1)}, bf16[1,320,512]{2,1,0:T(8,128)(2,1)S(1)}, u32[]{:S(2)}, u32[]{:S(2)}) collective-permute-start(bf16[1,320,512]{2,1,0:T(8,128)(2,1)S(1)} %add.16.refs_4_), channel_id=1, source_target_pairs={{0,2},{1,3},{2,0},{3,1},{4,6},{5,7},{6,4},{7,5},{8,10},{9,11},{10,... | collective-permute-start | bytes 983048 | tf_op jit(solution)/shard_map/ppermute | solution.py:439
  75.9 3.2 %weight_grad.6 = (f32[2,1024,1536]{2,1,0:T(8,128)}, f32[8,128]{1,0:T(8,128)S(1)}) custom-call(s32[1]{0:T(128)} %bitcast.2.refs_0_, bf16[160,1536]{1,0:T(8,128)(2,1)S(1)} %join.13.refs_2_.refs_1_, bf16[160,1536]{1,0:T(8,128)(2,1)S(1)} %collective-permute-done.18.refs_2_, bf16[1,320,512]{2,1,0:T(8,128)(2,1)S(1)} %get-tuple-element.79.refs_2_.refs_1_.refs_3_, ...), custom_call_target="tpu_custom_call" | custom-call | flops 10000000000 | bytes 1 | tf_op jit(solution)/shard_map/weight_grad/pallas_call | solution.py:49
  79.0 2.2 %row_grad_part.2 = (bf16[160,1536]{1,0:T(8,128)(2,1)S(1)}, bf16[160,1536]{1,0:T(8,128)(2,1)S(1)}) custom-call(s32[1]{0:T(128)} %bitcast.2.refs_0_, bf16[2,320,512]{2,1,0:T(8,128)(2,1)S(1)} %gate_up_grads.2.refs_5_.refs_1_.refs_3_, bf16[2,320,512]{2,1,0:T(8,128)(2,1)S(1)} %collective-permute-done.26.refs_2_.refs_4_, bf16[2,1536,1024]{2,1,0:T(8,128)(2,1)S(1)} %bitcast.6, ...), custom_call_target="tpu_custom_call" | custom-call | flops 10000000000 | bytes 1 | tf_op jit(solution)/shard_map/row_grad_part/pallas_call | solution.py:49
  81.4 1.8 %collective-permute-start.27 = (bf16[80,1536]{1,0:T(8,128)(2,1)S(1)}, bf16[80,1536]{1,0:T(8,128)(2,1)S(1)}, u32[]{:S(2)}, u32[]{:S(2)}) collective-permute-start(bf16[80,1536]{1,0:T(8,128)(2,1)S(1)} %get-tuple-element.93), channel_id=1, source_target_pairs={{0,8},{4,12},{8,0},{12,4},{16,24},{20,28},{24,16},{28,20},{1,9},{5... | collective-permute-start | bytes 737288 | tf_op jit(solution)/shard_map/ppermute | solution.py:432
  84.8 3.2 %weight_grad.7 = (f32[2,1024,1536]{2,1,0:T(8,128)}, f32[8,128]{1,0:T(8,128)S(1)}) custom-call(s32[1]{0:T(128)} %bitcast.2.refs_0_, bf16[160,1536]{1,0:T(8,128)(2,1)S(1)} %join.15.refs_4_.refs_1_, bf16[160,1536]{1,0:T(8,128)(2,1)S(1)} %collective-permute-done.22.refs_2_, ...), custom_call_target="tpu_custom_call", output_to_operand_aliasing={{0}: (5, {})} | custom-call | flops 10000000000 | bytes 1 | tf_op jit(solution)/shard_map/weight_grad/pallas_call | solution.py:49
  88.0 2.2 %row_grad_part.3 = (bf16[160,1536]{1,0:T(8,128)(2,1)S(1)}, bf16[160,1536]{1,0:T(8,128)(2,1)S(1)}) custom-call(s32[1]{0:T(128)} %bitcast.2.refs_0_, bf16[2,320,512]{2,1,0:T(8,128)(2,1)S(1)} %gate_up_grads.3.refs_6_.refs_1_.refs_3_, bf16[2,320,512]{2,1,0:T(8,128)(2,1)S(1)} %collective-permute-done.29.refs_2_.refs_4_, bf16[2,1536,1024]{2,1,0:T(8,128)(2,1)S(1)} %bitcast.6, ...), custom_call_target="tpu_custom_call" | custom-call | flops 10000000000 | bytes 1 | tf_op jit(solution)/shard_map/row_grad_part/pallas_call | solution.py:49
  92.8 3.2 %weight_grad.8 = (f32[2,1536,1024]{2,1,0:T(8,128)}, f32[8,128]{1,0:T(8,128)S(1)}) custom-call(s32[1]{0:T(128)} %bitcast.2.refs_0_, bf16[160,1536]{1,0:T(8,128)(2,1)S(1)} %copy-done.5, bf16[160,1536]{1,0:T(8,128)(2,1)S(1)} %copy-done.7, bf16[2,320,512]{2,1,0:T(8,128)(2,1)S(1)} %gate_up_grads.2.refs_5_.refs_1_.refs_3_, ...), custom_call_target="tpu_custom_call" | custom-call | flops 10000000000 | bytes 1 | tf_op jit(solution)/shard_map/weight_grad/pallas_call | solution.py:49
  97.7 3.2 %weight_grad.9 = (f32[2,1536,1024]{2,1,0:T(8,128)}, f32[8,128]{1,0:T(8,128)S(1)}) custom-call(s32[1]{0:T(128)} %bitcast.2.refs_0_, bf16[160,1536]{1,0:T(8,128)(2,1)S(1)} %copy-done.5, bf16[160,1536]{1,0:T(8,128)(2,1)S(1)} %copy-done.7, bf16[2,320,512]{2,1,0:T(8,128)(2,1)S(1)} %gate_up_grads.2.refs_5_.refs_1_.refs_3_, ...), custom_call_target="tpu_custom_call" | custom-call | flops 10000000000 | bytes 1 | tf_op jit(solution)/shard_map/weight_grad/pallas_call | solution.py:49
  100.9 4.5 %collective-permute-done.30.refs_1_ = bf16[160,1536]{1,0:T(8,128)(2,1)S(1)} collective-permute-done((bf16[160,1536]{1,0:T(8,128)(2,1)S(1)}, bf16[160,1536]{1,0:T(8,128)(2,1)S(1)}, u32[]{:S(2)}, u32[]{:S(2)}) %collective-permute-start.30) | collective-permute-done | bytes 491552 | tf_op jit(solution)/shard_map/ppermute | solution.py:432
  108.0 3.4 %weight_grad.10 = (f32[2,1536,1024]{2,1,0:T(8,128)}, f32[8,128]{1,0:T(8,128)S(1)}) custom-call(s32[1]{0:T(128)} %bitcast.2.refs_0_, bf16[160,1536]{1,0:T(8,128)(2,1)S(1)} %copy-done.1, bf16[160,1536]{1,0:T(8,128)(2,1)S(1)} %copy-done.3, bf16[2,320,512]{2,1,0:T(8,128)(2,1)S(1)} %gate_up_grads.3.refs_6_.refs_1_.refs_3_, ...), custom_call_target="tpu_custom_call", output_to_operand_aliasing={{0}: (5, {})} | custom-call | flops 10000000000 | bytes 1 | tf_op jit(solution)/shard_map/weight_grad/pallas_call | solution.py:49
  111.5 2.5 %collective-permute-start.38 = (bf16[40,1536]{1,0:T(8,128)(2,1)S(1)}, bf16[40,1536]{1,0:T(8,128)(2,1)S(1)}, u32[]{:S(2)}, u32[]{:S(2)}) collective-permute-start(bf16[40,1536]{1,0:T(8,128)(2,1)S(1)} %get-tuple-element.120), channel_id=1, source_target_pairs={{0,16},{4,20},{8,24},{12,28},{16,0},{20,4},{24,8},{28,12},{1,17},{... | collective-permute-start | bytes 368648 | tf_op jit(solution)/shard_map/ppermute | solution.py:432
  114.5 2.4 %collective-permute-start.34 = (bf16[40,1536]{1,0:T(8,128)(2,1)S(1)}, bf16[40,1536]{1,0:T(8,128)(2,1)S(1)}, u32[]{:S(2)}, u32[]{:S(2)}) collective-permute-start(bf16[40,1536]{1,0:T(8,128)(2,1)S(1)} %get-tuple-element.109), channel_id=1, source_target_pairs={{0,16},{4,20},{8,24},{12,28},{16,0},{20,4},{24,8},{28,12},{1,17},{... | collective-permute-start | bytes 368648 | tf_op jit(solution)/shard_map/ppermute | solution.py:432
  117.6 3.2 %weight_grad.11 = (f32[2,1536,1024]{2,1,0:T(8,128)}, f32[8,128]{1,0:T(8,128)S(1)}) custom-call(s32[1]{0:T(128)} %bitcast.2.refs_0_, bf16[160,1536]{1,0:T(8,128)(2,1)S(1)} %copy-done.1, bf16[160,1536]{1,0:T(8,128)(2,1)S(1)} %copy-done.3, bf16[2,320,512]{2,1,0:T(8,128)(2,1)S(1)} %gate_up_grads.3.refs_6_.refs_1_.refs_3_, ...), custom_call_target="tpu_custom_call", output_to_operand_aliasing={{0}: (5, {})} | custom-call | flops 10000000000 | bytes 1 | tf_op jit(solution)/shard_map/weight_grad/pallas_call | solution.py:49
  120.7 9.8 %collective-permute-done.35.refs_7_ = bf16[40,1536]{1,0:T(8,128)(2,1)S(1)} collective-permute-done((bf16[40,1536]{1,0:T(8,128)(2,1)S(1)}, bf16[40,1536]{1,0:T(8,128)(2,1)S(1)}, u32[]{:S(2)}, u32[]{:S(2)}) %collective-permute-start.35) | collective-permute-done | bytes 122912 | tf_op jit(solution)/shard_map/ppermute | solution.py:432
  130.6 2.6 %collective-permute-done.34.refs_6_ = bf16[40,1536]{1,0:T(8,128)(2,1)S(1)} collective-permute-done((bf16[40,1536]{1,0:T(8,128)(2,1)S(1)}, bf16[40,1536]{1,0:T(8,128)(2,1)S(1)}, u32[]{:S(2)}, u32[]{:S(2)}) %collective-permute-start.34) | collective-permute-done | bytes 122912 | tf_op jit(solution)/shard_map/ppermute | solution.py:432
  134.5 1.7 %combine.3 = (bf16[128,1536]{1,0:T(8,128)(2,1)}, f32[8,128]{1,0:T(8,128)}) custom-call(bf16[40,128]{1,0:T(8,128)(2,1)S(1)} %copy-done.13, bf16[40,128]{1,0:T(8,128)(2,1)S(1)} %copy-done.15, f32[40,128]{1,0:T(8,128)S(1)} %get-tuple-element.72.refs_2_, f32[40,128]{1,0:T(8,128)S(1)} %get-tuple-element.73.refs_3_, ...), custom_call_target="tpu_custom_call" | custom-call | flops 10000000000 | bytes 1 | tf_op jit(solution)/shard_map/combine/pallas_call | solution.py:49
  (146 shorter events, 38.0 us)
Async XLA Ops:
  2.5 10.1 %collective-permute-start = (bf16[40,1536]{1,0:T(8,128)(2,1)S(1)}, bf16[40,1536]{1,0:T(8,128)(2,1)S(1)}, u32[]{:S(2)}, u32[]{:S(2)}) collective-permute-start(bf16[40,1536]{1,0:T(8,128)(2,1)S(1)} %rows.2.refs_0_.refs_2_), channel_id=1, source_target_pairs={{0,16},{4,20},{8,24},{12,28},{16,0},{20,4},{24,8},{28,12},{1,17},{... | collective-permute-start | bytes 368648 | tf_op jit(solution)/shard_map/ppermute | solution.py:432
  12.6 9.8 %collective-permute-start.2 = (bf16[80,1536]{1,0:T(8,128)(2,1)S(1)}, bf16[80,1536]{1,0:T(8,128)(2,1)S(1)}, u32[]{:S(2)}, u32[]{:S(2)}) collective-permute-start(bf16[80,1536]{1,0:T(8,128)(2,1)S(1)} %join.8.refs_2_.refs_0_), channel_id=1, source_target_pairs={{0,8},{4,12},{8,0},{12,4},{16,24},{20,28},{24,16},{28,20},{1,9},{5... | collective-permute-start | bytes 737288 | tf_op jit(solution)/shard_map/ppermute | solution.py:432
  14.8 10.3 %collective-permute-start.1 = (bf16[40,1536]{1,0:T(8,128)(2,1)S(1)}, bf16[40,1536]{1,0:T(8,128)(2,1)S(1)}, u32[]{:S(2)}, u32[]{:S(2)}) collective-permute-start(bf16[40,1536]{1,0:T(8,128)(2,1)S(1)} %rows.3.refs_2_.refs_0_), channel_id=1, source_target_pairs={{0,16},{4,20},{8,24},{12,28},{16,0},{20,4},{24,8},{28,12},{1,17},{... | collective-permute-start | bytes 368648 | tf_op jit(solution)/shard_map/ppermute | solution.py:432
  22.5 14.9 %collective-permute-start.3 = (bf16[160,1536]{1,0:T(8,128)(2,1)S(1)}, bf16[160,1536]{1,0:T(8,128)(2,1)S(1)}, u32[]{:S(2)}, u32[]{:S(2)}) collective-permute-start(bf16[160,1536]{1,0:T(8,128)(2,1)S(1)} %join.9.refs_1_.refs_4_), channel_id=1, source_target_pairs={{0,4},{4,0},{8,12},{12,8},{16,20},{20,16},{24,28},{28,24},{1,5},{5... | collective-permute-start | bytes 1474568 | tf_op jit(solution)/shard_map/ppermute | solution.py:432
  25.2 7.2 %collective-permute-start.5 = (bf16[80,1536]{1,0:T(8,128)(2,1)S(1)}, bf16[80,1536]{1,0:T(8,128)(2,1)S(1)}, u32[]{:S(2)}, u32[]{:S(2)}) collective-permute-start(bf16[80,1536]{1,0:T(8,128)(2,1)S(1)} %join.10.refs_3_.refs_0_), channel_id=1, source_target_pairs={{0,8},{4,12},{8,0},{12,4},{16,24},{20,28},{24,16},{28,20},{1,9},{5... | collective-permute-start | bytes 737288 | tf_op jit(solution)/shard_map/ppermute | solution.py:432
  25.6 5.1 %collective-permute-start.6 = (bf16[2,160,512]{2,1,0:T(8,128)(2,1)S(1)}, bf16[2,160,512]{2,1,0:T(8,128)(2,1)S(1)}, u32[]{:S(2)}, u32[]{:S(2)}) collective-permute-start(bf16[2,160,512]{2,1,0:T(8,128)(2,1)S(1)} %get-tuple-element.69), channel_id=1, source_target_pairs={{0,1},{1,0},{2,3},{3,2},{4,5},{5,4},{6,7},{7,6},{8,9},{9,8},{10,11... | collective-permute-start | bytes 983048 | tf_op jit(solution)/shard_map/ppermute | solution.py:435
  26.5 10.7 %collective-permute-start.4 = (bf16[40,1536]{1,0:T(8,128)(2,1)S(1)}, bf16[40,1536]{1,0:T(8,128)(2,1)S(1)}, u32[]{:S(2)}, u32[]{:S(2)}) collective-permute-start(bf16[40,1536]{1,0:T(8,128)(2,1)S(1)} %get-tuple-element.68.refs_0_), channel_id=1, source_target_pairs={{0,16},{4,20},{8,24},{12,28},{16,0},{20,4},{24,8},{28,12},{1,17},{... | collective-permute-start | bytes 368648 | tf_op jit(solution)/shard_map/ppermute | solution.py:432
  30.8 12.8 %collective-permute-start.7 = (bf16[2,160,512]{2,1,0:T(8,128)(2,1)S(1)}, bf16[2,160,512]{2,1,0:T(8,128)(2,1)S(1)}, u32[]{:S(2)}, u32[]{:S(2)}) collective-permute-start(bf16[2,160,512]{2,1,0:T(8,128)(2,1)S(1)} %add.11.refs_2_), channel_id=1, source_target_pairs={{0,2},{1,3},{2,0},{3,1},{4,6},{5,7},{6,4},{7,5},{8,10},{9,11},{10,... | collective-permute-start | bytes 983048 | tf_op jit(solution)/shard_map/ppermute | solution.py:439
  32.4 16.9 %collective-permute-start.10 = (bf16[160,1536]{1,0:T(8,128)(2,1)S(1)}, bf16[160,1536]{1,0:T(8,128)(2,1)S(1)}, u32[]{:S(2)}, u32[]{:S(2)}) collective-permute-start(bf16[160,1536]{1,0:T(8,128)(2,1)S(1)} %join.11.refs_2_.refs_1_), channel_id=1, source_target_pairs={{0,4},{4,0},{8,12},{12,8},{16,20},{20,16},{24,28},{28,24},{1,5},{5... | collective-permute-start | bytes 1474568 | tf_op jit(solution)/shard_map/ppermute | solution.py:432
  37.1 9.2 %collective-permute-start.13 = (bf16[80,1536]{1,0:T(8,128)(2,1)S(1)}, bf16[80,1536]{1,0:T(8,128)(2,1)S(1)}, u32[]{:S(2)}, u32[]{:S(2)}) collective-permute-start(bf16[80,1536]{1,0:T(8,128)(2,1)S(1)} %join.12.refs_4_.refs_0_), channel_id=1, source_target_pairs={{0,8},{4,12},{8,0},{12,4},{16,24},{20,28},{24,16},{28,20},{1,9},{5... | collective-permute-start | bytes 737288 | tf_op jit(solution)/shard_map/ppermute | solution.py:432
  39.1 10.1 %collective-permute-start.11 = (bf16[40,1536]{1,0:T(8,128)(2,1)S(1)}, bf16[40,1536]{1,0:T(8,128)(2,1)S(1)}, u32[]{:S(2)}, u32[]{:S(2)}) collective-permute-start(bf16[40,1536]{1,0:T(8,128)(2,1)S(1)} %get-tuple-element.75.refs_0_), channel_id=1, source_target_pairs={{0,16},{4,20},{8,24},{12,28},{16,0},{20,4},{24,8},{28,12},{1,17},{... | collective-permute-start | bytes 368648 | tf_op jit(solution)/shard_map/ppermute | solution.py:432
  42.0 10.6 %collective-permute-start.9 = (bf16[2,160,512]{2,1,0:T(8,128)(2,1)S(1)}, bf16[2,160,512]{2,1,0:T(8,128)(2,1)S(1)}, u32[]{:S(2)}, u32[]{:S(2)}) collective-permute-start(bf16[2,160,512]{2,1,0:T(8,128)(2,1)S(1)} %add.12.refs_3_), channel_id=1, source_target_pairs={{0,2},{1,3},{2,0},{3,1},{4,6},{5,7},{6,4},{7,5},{8,10},{9,11},{10,... | collective-permute-start | bytes 983048 | tf_op jit(solution)/shard_map/ppermute | solution.py:439
  46.4 13.5 %collective-permute-start.18 = (bf16[160,1536]{1,0:T(8,128)(2,1)S(1)}, bf16[160,1536]{1,0:T(8,128)(2,1)S(1)}, u32[]{:S(2)}, u32[]{:S(2)}) collective-permute-start(bf16[160,1536]{1,0:T(8,128)(2,1)S(1)} %join.13.refs_2_.refs_1_), channel_id=1, source_target_pairs={{0,4},{4,0},{8,12},{12,8},{16,20},{20,16},{24,28},{28,24},{1,5},{5... | collective-permute-start | bytes 1474568 | tf_op jit(solution)/shard_map/ppermute | solution.py:432
  47.6 12.1 %collective-permute-start.19 = (bf16[2,160,512]{2,1,0:T(8,128)(2,1)S(1)}, bf16[2,160,512]{2,1,0:T(8,128)(2,1)S(1)}, u32[]{:S(2)}, u32[]{:S(2)}) collective-permute-start(bf16[2,160,512]{2,1,0:T(8,128)(2,1)S(1)} %add.13.refs_2_), channel_id=1, source_target_pairs={{0,2},{1,3},{2,0},{3,1},{4,6},{5,7},{6,4},{7,5},{8,10},{9,11},{10,... | collective-permute-start | bytes 983048 | tf_op jit(solution)/shard_map/ppermute | solution.py:439
  49.2 7.1 %collective-permute-start.15 = (bf16[80,1536]{1,0:T(8,128)(2,1)S(1)}, bf16[80,1536]{1,0:T(8,128)(2,1)S(1)}, u32[]{:S(2)}, u32[]{:S(2)}) collective-permute-start(bf16[80,1536]{1,0:T(8,128)(2,1)S(1)} %join.14.refs_4_.refs_0_), channel_id=1, source_target_pairs={{0,8},{4,12},{8,0},{12,4},{16,24},{20,28},{24,16},{28,20},{1,9},{5... | collective-permute-start | bytes 737288 | tf_op jit(solution)/shard_map/ppermute | solution.py:432
  53.1 13.0 %collective-permute-start.23 = (bf16[2,160,512]{2,1,0:T(8,128)(2,1)S(1)}, bf16[2,160,512]{2,1,0:T(8,128)(2,1)S(1)}, u32[]{:S(2)}, u32[]{:S(2)}) collective-permute-start(bf16[2,160,512]{2,1,0:T(8,128)(2,1)S(1)} %add.14.refs_2_), channel_id=1, source_target_pairs={{0,2},{1,3},{2,0},{3,1},{4,6},{5,7},{6,4},{7,5},{8,10},{9,11},{10,... | collective-permute-start | bytes 983048 | tf_op jit(solution)/shard_map/ppermute | solution.py:439
  56.4 14.2 %collective-permute-start.22 = (bf16[160,1536]{1,0:T(8,128)(2,1)S(1)}, bf16[160,1536]{1,0:T(8,128)(2,1)S(1)}, u32[]{:S(2)}, u32[]{:S(2)}) collective-permute-start(bf16[160,1536]{1,0:T(8,128)(2,1)S(1)} %join.15.refs_4_.refs_1_), channel_id=1, source_target_pairs={{0,4},{4,0},{8,12},{12,8},{16,20},{20,16},{24,28},{28,24},{1,5},{5... | collective-permute-start | bytes 1474568 | tf_op jit(solution)/shard_map/ppermute | solution.py:432
  58.2 23.1 %collective-permute-start.17 = (bf16[160,1536]{1,0:T(8,128)(2,1)S(1)}, bf16[160,1536]{1,0:T(8,128)(2,1)S(1)}, u32[]{:S(2)}, u32[]{:S(2)}) collective-permute-start(bf16[160,1536]{1,0:T(8,128)(2,1)S(1)} %get-tuple-element.82), channel_id=1, source_target_pairs={{0,4},{4,0},{8,12},{12,8},{16,20},{20,16},{24,28},{28,24},{1,5},{5... | collective-permute-start | bytes 1474568 | tf_op jit(solution)/shard_map/ppermute | solution.py:432
  62.9 12.2 %collective-permute-start.21 = (bf16[1,320,512]{2,1,0:T(8,128)(2,1)S(1)}, bf16[1,320,512]{2,1,0:T(8,128)(2,1)S(1)}, u32[]{:S(2)}, u32[]{:S(2)}) collective-permute-start(bf16[1,320,512]{2,1,0:T(8,128)(2,1)S(1)} %add.15.refs_4_), channel_id=1, source_target_pairs={{0,2},{1,3},{2,0},{3,1},{4,6},{5,7},{6,4},{7,5},{8,10},{9,11},{10,... | collective-permute-start | bytes 983048 | tf_op jit(solution)/shard_map/ppermute | solution.py:439
  66.4 5.5 %collective-permute-start.25 = (bf16[1,320,512]{2,1,0:T(8,128)(2,1)S(1)}, bf16[1,320,512]{2,1,0:T(8,128)(2,1)S(1)}, u32[]{:S(2)}, u32[]{:S(2)}) collective-permute-start(bf16[1,320,512]{2,1,0:T(8,128)(2,1)S(1)} %get-tuple-element.86.refs_4_.refs_1_.refs_3_), channel_id=1, source_target_pairs={{0,1},{1,0},{2,3},{3,2},{4,5},{5,4},{6,7},{7,6},{8,9},{9,8},{10,11... | collective-permute-start | bytes 983048 | tf_op jit(solution)/shard_map/ppermute | solution.py:435
  73.1 17.2 %collective-permute-start.32 = (bf16[160,1536]{1,0:T(8,128)(2,1)S(1)}, bf16[160,1536]{1,0:T(8,128)(2,1)S(1)}, u32[]{:S(2)}, u32[]{:S(2)}) collective-permute-start(bf16[160,1536]{1,0:T(8,128)(2,1)S(1)} %get-tuple-element.100), channel_id=1, source_target_pairs={{0,8},{4,12},{8,0},{12,4},{16,24},{20,28},{24,16},{28,20},{1,9},{5... | collective-permute-start | bytes 1474568 | tf_op jit(solution)/shard_map/ppermute | solution.py:432
  73.6 10.7 %collective-permute-start.28 = (bf16[1,320,512]{2,1,0:T(8,128)(2,1)S(1)}, bf16[1,320,512]{2,1,0:T(8,128)(2,1)S(1)}, u32[]{:S(2)}, u32[]{:S(2)}) collective-permute-start(bf16[1,320,512]{2,1,0:T(8,128)(2,1)S(1)} %add.16.refs_4_), channel_id=1, source_target_pairs={{0,2},{1,3},{2,0},{3,1},{4,6},{5,7},{6,4},{7,5},{8,10},{9,11},{10,... | collective-permute-start | bytes 983048 | tf_op jit(solution)/shard_map/ppermute | solution.py:439
  81.4 25.4 %collective-permute-start.27 = (bf16[80,1536]{1,0:T(8,128)(2,1)S(1)}, bf16[80,1536]{1,0:T(8,128)(2,1)S(1)}, u32[]{:S(2)}, u32[]{:S(2)}) collective-permute-start(bf16[80,1536]{1,0:T(8,128)(2,1)S(1)} %get-tuple-element.93), channel_id=1, source_target_pairs={{0,8},{4,12},{8,0},{12,4},{16,24},{20,28},{24,16},{28,20},{1,9},{5... | collective-permute-start | bytes 737288 | tf_op jit(solution)/shard_map/ppermute | solution.py:432
  83.2 14.1 %collective-permute-start.31 = (bf16[160,1536]{1,0:T(8,128)(2,1)S(1)}, bf16[160,1536]{1,0:T(8,128)(2,1)S(1)}, u32[]{:S(2)}, u32[]{:S(2)}) collective-permute-start(bf16[160,1536]{1,0:T(8,128)(2,1)S(1)} %get-tuple-element.99), channel_id=1, source_target_pairs={{0,4},{4,0},{8,12},{12,8},{16,20},{20,16},{24,28},{28,24},{1,5},{5... | collective-permute-start | bytes 1474568 | tf_op jit(solution)/shard_map/ppermute | solution.py:432
  90.4 16.4 %collective-permute-start.33 = (bf16[80,1536]{1,0:T(8,128)(2,1)S(1)}, bf16[80,1536]{1,0:T(8,128)(2,1)S(1)}, u32[]{:S(2)}, u32[]{:S(2)}) collective-permute-start(bf16[80,1536]{1,0:T(8,128)(2,1)S(1)} %get-tuple-element.107), channel_id=1, source_target_pairs={{0,4},{4,0},{8,12},{12,8},{16,20},{20,16},{24,28},{28,24},{1,5},{5... | collective-permute-start | bytes 737288 | tf_op jit(solution)/shard_map/ppermute | solution.py:432
  91.3 14.1 %collective-permute-start.30 = (bf16[160,1536]{1,0:T(8,128)(2,1)S(1)}, bf16[160,1536]{1,0:T(8,128)(2,1)S(1)}, u32[]{:S(2)}, u32[]{:S(2)}) collective-permute-start(bf16[160,1536]{1,0:T(8,128)(2,1)S(1)} %get-tuple-element.98), channel_id=1, source_target_pairs={{0,8},{4,12},{8,0},{12,4},{16,24},{20,28},{24,16},{28,20},{1,9},{5... | collective-permute-start | bytes 1474568 | tf_op jit(solution)/shard_map/ppermute | solution.py:432
  97.3 14.1 %collective-permute-start.37 = (bf16[80,1536]{1,0:T(8,128)(2,1)S(1)}, bf16[80,1536]{1,0:T(8,128)(2,1)S(1)}, u32[]{:S(2)}, u32[]{:S(2)}) collective-permute-start(bf16[80,1536]{1,0:T(8,128)(2,1)S(1)} %get-tuple-element.113), channel_id=1, source_target_pairs={{0,8},{4,12},{8,0},{12,4},{16,24},{20,28},{24,16},{28,20},{1,9},{5... | collective-permute-start | bytes 737288 | tf_op jit(solution)/shard_map/ppermute | solution.py:432
  105.5 11.4 %collective-permute-start.36 = (bf16[80,1536]{1,0:T(8,128)(2,1)S(1)}, bf16[80,1536]{1,0:T(8,128)(2,1)S(1)}, u32[]{:S(2)}, u32[]{:S(2)}) collective-permute-start(bf16[80,1536]{1,0:T(8,128)(2,1)S(1)} %get-tuple-element.112), channel_id=1, source_target_pairs={{0,4},{4,0},{8,12},{12,8},{16,20},{20,16},{24,28},{28,24},{1,5},{5... | collective-permute-start | bytes 737288 | tf_op jit(solution)/shard_map/ppermute | solution.py:432
  111.5 22.8 %collective-permute-start.38 = (bf16[40,1536]{1,0:T(8,128)(2,1)S(1)}, bf16[40,1536]{1,0:T(8,128)(2,1)S(1)}, u32[]{:S(2)}, u32[]{:S(2)}) collective-permute-start(bf16[40,1536]{1,0:T(8,128)(2,1)S(1)} %get-tuple-element.120), channel_id=1, source_target_pairs={{0,16},{4,20},{8,24},{12,28},{16,0},{20,4},{24,8},{28,12},{1,17},{... | collective-permute-start | bytes 368648 | tf_op jit(solution)/shard_map/ppermute | solution.py:432
  114.0 16.6 %collective-permute-start.35 = (bf16[40,1536]{1,0:T(8,128)(2,1)S(1)}, bf16[40,1536]{1,0:T(8,128)(2,1)S(1)}, u32[]{:S(2)}, u32[]{:S(2)}) collective-permute-start(bf16[40,1536]{1,0:T(8,128)(2,1)S(1)} %get-tuple-element.110), channel_id=1, source_target_pairs={{0,16},{4,20},{8,24},{12,28},{16,0},{20,4},{24,8},{28,12},{1,17},{... | collective-permute-start | bytes 368648 | tf_op jit(solution)/shard_map/ppermute | solution.py:432
  114.5 18.7 %collective-permute-start.34 = (bf16[40,1536]{1,0:T(8,128)(2,1)S(1)}, bf16[40,1536]{1,0:T(8,128)(2,1)S(1)}, u32[]{:S(2)}, u32[]{:S(2)}) collective-permute-start(bf16[40,1536]{1,0:T(8,128)(2,1)S(1)} %get-tuple-element.109), channel_id=1, source_target_pairs={{0,16},{4,20},{8,24},{12,28},{16,0},{20,4},{24,8},{28,12},{1,17},{... | collective-permute-start | bytes 368648 | tf_op jit(solution)/shard_map/ppermute | solution.py:432
  117.0 17.5 %collective-permute-start.39 = (bf16[40,1536]{1,0:T(8,128)(2,1)S(1)}, bf16[40,1536]{1,0:T(8,128)(2,1)S(1)}, u32[]{:S(2)}, u32[]{:S(2)}) collective-permute-start(bf16[40,1536]{1,0:T(8,128)(2,1)S(1)} %get-tuple-element.121), channel_id=1, source_target_pairs={{0,16},{4,20},{8,24},{12,28},{16,0},{20,4},{24,8},{28,12},{1,17},{... | collective-permute-start | bytes 368648 | tf_op jit(solution)/shard_map/ppermute | solution.py:432
  (30 other events, 140.9 us)
